TPU v7x, 512 devices: a whole 4x8x8 slice. The times are simulated.
512 devices in a mesh: leaf: 16 (over y, core), front: 32 (over z, x).
Axes of the slice: x: 4, y: 8, z: 8, core: 2. Of those that a mesh axis runs over, the one named last changes fastest.
Arguments:
- right_side: float32 [64, 65536], P(None, ('leaf', 'front')), may hold values from -3 to 3
- inverse_blocks: float32 [65536, 4096], P(('leaf', 'front')), as said below
- panels: float32 [4096, 4096], P('leaf', 'front'), may hold values from -0.3125 to 0.3125
- receive_rows: int32 [16, 256], P('leaf'), may hold values from 0 to 4095, as said below
- below_update: float32 [64, 256], replicated, may hold values from -6 to 6
- above_solution: float32 [64, 256], replicated, may hold values from -6 to 6
Outputs:
- solution: float32 [64, 65536], P(None, ('leaf', 'front'))
- sent_updates: float32 [64, 4096], P(None, ('leaf', 'front'))
Inputs may be any that keep to these rules, and one draw needn't show every extreme that they name: `receive_rows`: each row holds 256 distinct columns in increasing order, the first 0 and the last 4095. `inverse_blocks`: each 4096 x 4096 block is lower triangular with a positive diagonal.
All inputs are finite; a program needn't handle non-finite values.
Results may differ from a plain program's by a relative error of at most 0.00019.
Values sent between devices are 32-bit elements; how exact they have to be, the bound alone decides.
No kernel may reach another device: no remote copies, remote signals or barrier semaphores. Data moves between devices by JAX's collectives and lax.ppermute only.
A program may use at most 64 MiB of HBM per device.

v0:
```python
import jax
import jax.numpy as jnp
from jax import lax
from jax.sharding import PartitionSpec as P

highest = lax.Precision.HIGHEST


def from_behind(value, axis, steps):
    count = lax.axis_size(axis)
    first, last = (max(0, -steps), min(count, count - steps))
    return lax.ppermute(value, axis, [(source, source + steps) for source in range(first, last)])


def product(left, right):
    return jnp.dot(left, right, precision=highest, preferred_element_type=jnp.float32)


def on_device(right_side, inverse_blocks, panels, receive_rows, below_update, above_solution):
    block_rows = inverse_blocks.shape[0]
    panel_count = panels.shape[0]
    front_pos = lax.axis_index("front")
    leaf_pos = lax.axis_index("leaf")
    leaf_count = lax.axis_size("leaf")
    front_count = lax.axis_size("front")
    first_col = front_pos * block_rows
    targets = receive_rows[0]
    local_forward = product(
        lax.all_gather(right_side, "front", axis=1, tiled=True), inverse_blocks.T
    )
    target_inverse = jnp.take(inverse_blocks, targets, axis=1).T
    offset_term = product(local_forward, panels.T)
    coupling_term = product(target_inverse, panels.T)
    update_offset, update_coupling = lax.psum((offset_term, coupling_term), "front")

    def forward_turn(turn_index, state_pair):
        incoming, own_update = state_pair
        new_update = update_offset - product(incoming, update_coupling)
        sent_rows = from_behind(new_update, "leaf", 1)
        incoming = jnp.where(leaf_pos == turn_index + 1, sent_rows, incoming)
        own_update = jnp.where(leaf_pos == turn_index, new_update, own_update)
        return (incoming, own_update)

    incoming, own_update = lax.fori_loop(
        0, leaf_count, forward_turn, (below_update, jnp.zeros_like(below_update))
    )
    forward_rows = local_forward - product(incoming, target_inverse)
    update_share = panel_count // front_count
    sent_updates = lax.dynamic_slice_in_dim(own_update, front_pos * update_share, update_share, 1)
    inverse_columns = lax.all_to_all(
        inverse_blocks, "front", split_axis=1, concat_axis=0, tiled=True
    )

    def add_columns(block_piece):
        return product(block_piece, inverse_columns)

    carried = add_columns(lax.all_gather(forward_rows, "front", axis=1, tiled=True))
    panel_image = add_columns(lax.all_gather(panels, "front", axis=1, tiled=True))
    local_pos = targets - first_col
    owned_mask = (local_pos >= 0) & (local_pos < block_rows)
    safe_pos = jnp.clip(local_pos, 0, block_rows - 1)
    carried_part = jnp.where(owned_mask[None, :], jnp.take(carried, safe_pos, axis=1), 0.0)
    image_part = jnp.where(owned_mask[None, :], jnp.take(panel_image, safe_pos, axis=1), 0.0)
    return_offset, return_coupling = lax.psum((carried_part, image_part), "front")
    last_leaf = leaf_count - 1

    def backward_turn(turn_index, from_above):
        new_rows = return_offset - product(from_above, return_coupling)
        sent_rows = from_behind(new_rows, "leaf", -1)
        return jnp.where(leaf_pos == last_leaf - 1 - turn_index, sent_rows, from_above)

    from_above = lax.fori_loop(0, leaf_count, backward_turn, above_solution)
    solution = carried - product(from_above, panel_image)
    return (solution, sent_updates)


def solution(mesh):
    in_specs = (
        P(None, ("leaf", "front")),
        P(("leaf", "front"), None),
        P("leaf", "front"),
        P("leaf", None),
        P(),
        P(),
    )
    out_specs = (P(None, ("leaf", "front")), P(None, ("leaf", "front")))
    return jax.shard_map(
        on_device, mesh=mesh, in_specs=in_specs, out_specs=out_specs, check_vma=False
    )
```

profile of v0, /device:TPU:25, one launch (start us, length us, event | category | flops | bytes accessed | tf_op | source)
XLA Modules:
  0.0 843.9 jit_solution(10137367857905192095)
XLA Ops:
  14.5 74.0 %all-gather.4.cloned.1.call-done = f32[64,4096]{1,0:T(8,128)} async-done(((f32[64,128]{1,0:T(8,128)}), f32[64,4096]{1,0:T(8,128)}) %all-gather.4.cloned.1.call-update) | async-done | bytes 1048592 | tf_op jit(solution)/shard_map/all_gather | solution.py:29
  93.0 154.8 %all-reduce.7.cloned.1.call-done = (f32[256,256]{1,0:T(8,128)}, f32[64,256]{1,0:T(8,128)}) async-done(((f32[256,256]{1,0:T(8,128)}, f32[64,256]{1,0:T(8,128)}), (f32[256,256]{1,0:T(8,128)}, f32[64,256]{1,0:T(8,128)})) %all-reduce.7.cloned.1.call-update) | async-done | bytes 327696 | tf_op jit(solution)/shard_map/psum | solution.py:34
  247.9 133.3 %while.30 = (s32[]{:T(128)}, f32[64,256]{1,0:T(8,128)S(1)}, f32[64,256]{1,0:T(8,128)S(1)}, s32[]{:T(128)}, f32[256,256]{1,0:T(8,128)}, /*index=5*/f32[64,256]{1,0:T(8,128)}, s32[]{:T(128)}, s32[]{:T(128)}) while((s32[]{:T(128)}, f32[64,256]{1,0:T(8,128)S(1)}, f32[64,256]{1,0:T(8,128)S(1)}, s32[]{:T(128)}, f32[256,256]{1,0:T(8,128)}, ...), condition=%wide.region_3.4_spmd.clone, body=%wide.region_2.3_spmd.clone.sunk | while | flops 50397188 | bytes 1048731 | solution.py:44
  249.1 10.0 %collective-permute-start.1 = (f32[64,256]{1,0:T(8,128)S(1)}, f32[64,256]{1,0:T(8,128)S(1)}, u32[]{:S(2)}, u32[]{:S(2)}) collective-permute-start(f32[64,256]{1,0:T(8,128)S(1)} %get-tuple-element.347), channel_id=1, source_target_pairs={{0,32},{32,64},{64,96},{96,128},{128,160},{160,192},{192,224},{224... | collective-permute-start | bytes 196616 | tf_op jit(solution)/shard_map/while/body/eval_jaxpr/ppermute | solution.py:12
  261.6 5.5 collective-permute-start.1
  269.7 5.5 collective-permute-start.1
  277.7 5.5 collective-permute-start.1
  285.8 5.5 collective-permute-start.1
  293.8 5.5 collective-permute-start.1
  309.9 5.5 collective-permute-start.1
  318.0 5.5 collective-permute-start.1
  334.1 5.5 collective-permute-start.1
  342.1 5.5 collective-permute-start.1
  350.2 5.5 collective-permute-start.1
  358.2 5.5 collective-permute-start.1
  366.3 5.5 collective-permute-start.1
  374.3 5.5 collective-permute-start.1
  388.0 48.8 %all-to-all-done = f32[128,32,128]{0,2,1:T(8,128)S(1)} async-done(((f32[128,32,128]{0,2,1:T(8,128)}), f32[128,32,128]{0,2,1:T(8,128)S(1)}, u32[]{:S(2)}, u32[]{:S(2)}) %all-to-all-start) | async-done | bytes 2097184 | tf_op jit(solution)/shard_map/all_to_all | solution.py:50
  440.1 20.2 %all-gather.6.cloned.1.call-done = f32[64,4096]{1,0:T(8,128)} async-done(((f32[64,128]{1,0:T(8,128)}), f32[64,4096]{1,0:T(8,128)}) %all-gather.6.cloned.1.call-update) | async-done | bytes 1048592 | tf_op jit(solution)/shard_map/all_gather | solution.py:57
  464.6 88.2 %all-gather.8.cloned.1.call-done = f32[256,4096]{1,0:T(8,128)} async-done(((f32[256,128]{1,0:T(8,128)}), f32[256,4096]{1,0:T(8,128)}) %all-gather.8.cloned.1.call-update) | async-done | bytes 4194320 | tf_op jit(solution)/shard_map/all_gather | solution.py:58
  552.8 5.9 fusion.13
  561.3 155.2 %all-reduce.5.cloned.1.call-done = (f32[256,256]{0,1:T(8,128)}, f32[64,256]{0,1:T(8,128)}) async-done(((f32[256,256]{0,1:T(8,128)}, f32[64,256]{0,1:T(8,128)}), (f32[256,256]{0,1:T(8,128)}, f32[64,256]{0,1:T(8,128)})) %all-reduce.5.cloned.1.call-update) | async-done | bytes 327696 | tf_op jit(solution)/shard_map/psum | solution.py:64
  718.6 117.9 %while.29 = (s32[]{:T(128)}, f32[64,256]{1,0:T(8,128)S(1)}, s32[]{:T(128)}, f32[256,256]{1,0:T(8,128)S(1)}, f32[64,256]{1,0:T(8,128)S(1)}, /*index=5*/s32[]{:T(128)}, s32[]{:T(128)}) while((s32[]{:T(128)}, f32[64,256]{1,0:T(8,128)S(1)}, s32[]{:T(128)}, f32[256,256]{1,0:T(8,128)S(1)}, f32[64,256]{1,0:T(8,128)S(1)}, /*index=5*/s32[]{:T(128)}, ...), condition=%wide.region_7.8_spmd, body=%wide.region_6.7_spmd.sunk | while | flops 50364416 | bytes 917651 | solution.py:72
  718.9 7.1 collective-permute-start
  (161 shorter events, 193.0 us)
Async XLA Ops:
  7.2 81.4 %all-gather.4.cloned.1.call-start = ((), (), s32[]{:S(2)}) async-start(), calls=%async_computation.1 | async-start | bytes 1081344 | tf_op jit(solution)/shard_map/all_gather | solution.py:29
  7.9 240.0 %all-reduce.7.cloned.1.call-start = ((), (), s32[]{:S(2)}) async-start(), calls=%async_computation.5 | async-start | bytes 655360 | tf_op jit(solution)/shard_map/psum | solution.py:34
  93.0 367.4 %all-gather.6.cloned.1.call-start = ((), (), s32[]{:S(2)}) async-start(), calls=%async_computation.2 | async-start | bytes 1081344 | tf_op jit(solution)/shard_map/all_gather | solution.py:57
  249.1 11.3 %collective-permute-start.1 = (f32[64,256]{1,0:T(8,128)S(1)}, f32[64,256]{1,0:T(8,128)S(1)}, u32[]{:S(2)}, u32[]{:S(2)}) collective-permute-start(f32[64,256]{1,0:T(8,128)S(1)} %get-tuple-element.347), channel_id=1, source_target_pairs={{0,32},{32,64},{64,96},{96,128},{128,160},{160,192},{192,224},{224... | collective-permute-start | bytes 196616 | tf_op jit(solution)/shard_map/while/body/eval_jaxpr/ppermute | solution.py:12
  261.6 6.8 collective-permute-start.1
  269.7 6.8 collective-permute-start.1
  277.7 6.8 collective-permute-start.1
  285.8 6.8 collective-permute-start.1
  293.8 6.8 collective-permute-start.1
  301.9 6.8 collective-permute-start.1
  309.9 6.8 collective-permute-start.1
  318.0 6.8 collective-permute-start.1
  326.0 6.8 collective-permute-start.1
  334.1 6.8 collective-permute-start.1
  342.1 6.8 collective-permute-start.1
  350.2 6.8 collective-permute-start.1
  358.2 6.8 collective-permute-start.1
  366.3 6.8 collective-permute-start.1
  374.3 6.8 collective-permute-start.1
  382.1 170.7 %all-gather.8.cloned.1.call-start = ((), (), s32[]{:S(2)}) async-start(), calls=%async_computation.3 | async-start | bytes 4325376 | tf_op jit(solution)/shard_map/all_gather | solution.py:58
  382.7 54.1 %all-to-all-start = ((f32[128,32,128]{0,2,1:T(8,128)}), f32[128,32,128]{0,2,1:T(8,128)S(1)}, u32[]{:S(2)}, u32[]{:S(2)}) async-start(f32[128,32,128]{0,2,1:T(8,128)} %bitcast.3), calls=%async_computation | async-start | bytes 4194304 | tf_op jit(solution)/shard_map/all_to_all | solution.py:50
  387.9 328.7 %all-reduce.5.cloned.1.call-start = ((), (), s32[]{:S(2)}) async-start(), calls=%async_computation.4 | async-start | bytes 786432 | tf_op jit(solution)/shard_map/psum | solution.py:64
  718.9 11.3 %collective-permute-start = (f32[64,256]{1,0:T(8,128)S(1)}, f32[64,256]{1,0:T(8,128)S(1)}, u32[]{:S(2)}, u32[]{:S(2)}) collective-permute-start(f32[64,256]{1,0:T(8,128)S(1)} %convolution_subtract_fusion.5), channel_id=1, source_target_pairs={{32,0},{64,32},{96,64},{128,96},{160,128},{192,160},{224,192},{256... | collective-permute-start | bytes 196616 | tf_op jit(solution)/shard_map/while/body/eval_jaxpr/ppermute | solution.py:12
  751.8 6.8 collective-permute-start
  (20 other events, 579.9 us)
Sparse Core Ops, SparseCore 0:
  11.0 77.4 all-gather.3
  93.1 154.7 all-reduce.6
  382.2 78.0 all-gather.5
  463.7 89.0 all-gather.7
  560.8 155.7 all-reduce.4
where the time goes:
time: 845 us; the launch traced here: 844 us
  waiting for transfers between devices  641 us (76%)
  starting transfers between devices  133 us (16%)
  matrix products  39.1 us (5%)
  between operations  14 us (2%)
  local copies, waits for them, and re-layouts  13.3 us (2%)
    psum x1, waiting for transfers between devices, on_device(): lax.psum((carried_part, image_part), 'front')  155 us
    psum x1, waiting for transfers between devices, on_device(): lax.psum((offset_term, coupling_term), 'front')  155 us
    ppermute x32, starting transfers between devices, from_behind(): lax.ppermute(value, axis, [(source, source + steps) for source in range(f...  128 us
    ppermute x32, waiting for transfers between devices, from_behind(): lax.ppermute(value, axis, [(source, source + steps) for source in range(f...  97.9 us
    all_gather x1, waiting for transfers between devices, on_device(): lax.all_gather(panels, 'front', axis=1, tiled=True)  88.2 us
    all_gather x1, waiting for transfers between devices, on_device(): lax.all_gather(right_side, 'front', axis=1, tiled=True)  74 us
    all_to_all x1, waiting for transfers between devices, on_device(): lax.all_to_all(inverse_blocks, 'front', split_axis=1, concat_axis=0, tile...  48.8 us
    dot_general x39, matrix products, product(): jnp.dot(left, right, precision=highest, preferred_element_type=jnp.float32)  39.1 us
  transfers between devices with their start and end apart: 38, of which 38 were waited for; matrix products, arithmetic and copies ran while one was open for 2% of the time, Pallas kernels for 0%

commit v1 on v0

v1 whole, which is shorter than its diff:
```python
import jax
import jax.numpy as jnp
from jax import lax
from jax.sharding import PartitionSpec as P

exact = lax.Precision.HIGHEST


def product(left, right):
    return jnp.dot(left, right, precision=exact, preferred_element_type=jnp.float32)


def product_nt(left, right):
    return lax.dot_general(
        left, right, (((1,), (1,)), ((), ())), precision=exact, preferred_element_type=jnp.float32
    )


def exchange(blocks):
    return lax.all_to_all(blocks, "front", 0, 0, tiled=True)


def gather_front(block):
    count = lax.axis_size("front")
    return exchange(jnp.broadcast_to(block[None], (count, *block.shape)))


def scatter_front(total):
    count = lax.axis_size("front")
    pieces = total.reshape(count, total.shape[0] // count, *total.shape[1:])
    return jnp.sum(exchange(pieces), axis=0)


def on_device(right_side, inverse_blocks, panels, receive_rows, below_update, above_solution):
    rhs = right_side.shape[0]
    block = inverse_blocks.shape[0]
    rows = panels.shape[0]
    leaf_count = lax.axis_size("leaf")
    front_count = lax.axis_size("front")
    front_pos = lax.axis_index("front")
    leaf_pos = lax.axis_index("leaf")
    share = rhs // front_count
    targets = receive_rows[0]
    is_upper = leaf_pos % 2 == 1

    section_side = gather_front(right_side)
    picked = jnp.take(inverse_blocks, targets, axis=1)
    stacked = jnp.concatenate([panels, picked.T], axis=0)
    coupling = scatter_front(product(stacked, picked))
    coupling = gather_front(coupling).reshape(2 * rows, rows)

    section_side = section_side.transpose(1, 0, 2).reshape(rhs, front_count * block)
    local_forward = product_nt(section_side, inverse_blocks)
    vectors = scatter_front(product_nt(local_forward, stacked))

    swap = [(s, s ^ 1) for s in range(leaf_count)]
    up = [(s, (s + 2) % leaf_count) for s in range(leaf_count)]
    down = [(target, source) for source, target in up]
    mate_coupling = lax.ppermute(coupling, "leaf", swap)
    mate_vectors = lax.ppermute(vectors, "leaf", swap)
    low = jnp.where(is_upper, mate_coupling, coupling)
    high = jnp.where(is_upper, coupling, mate_coupling)
    low_vec = jnp.where(is_upper, mate_vectors, vectors)
    high_vec = jnp.where(is_upper, vectors, mate_vectors)
    d_low, g_low = (-low[:rows], low[rows:])
    d_high, g_high = (-high[:rows], high[rows:])
    u_low, w_low = (low_vec[:, :rows], low_vec[:, rows:])
    u_high, w_high = (high_vec[:, :rows], high_vec[:, rows:])
    d_pair = product(d_high, d_low)
    g_pair = g_low + product(d_low.T, product(g_high, d_low))
    u_pair = u_high + product_nt(u_low, d_high)
    w_pair = w_low + product(w_high - product(u_low, g_high), d_low)

    below_rows = lax.dynamic_slice_in_dim(below_update, front_pos * share, share, 0)
    above_rows = lax.dynamic_slice_in_dim(above_solution, front_pos * share, share, 0)
    incoming = below_rows
    for _ in range(leaf_count // 2 - 1):
        sent = lax.ppermute(u_pair + product_nt(incoming, d_pair), "leaf", up)
        incoming = jnp.where(leaf_pos < 2, below_rows, sent)
    w_full = w_pair - product(incoming, g_pair)
    from_above = above_rows
    for _ in range(leaf_count // 2 - 1):
        sent = lax.ppermute(w_full + product(from_above, d_pair), "leaf", down)
        from_above = jnp.where(leaf_pos >= leaf_count - 2, above_rows, sent)

    middle = u_low + product_nt(incoming, d_low)
    own_incoming = jnp.where(is_upper, middle, incoming)
    upper_update = u_high + product_nt(middle, d_high)
    own_update = jnp.where(is_upper, upper_update, middle)
    middle_above = w_high - product(middle, g_high) + product(from_above, d_high)
    own_above = jnp.where(is_upper, from_above, middle_above)

    result = gather_front(jnp.concatenate([own_above, own_incoming, own_update], axis=1))
    result = result.reshape(rhs, 3 * rows)
    update_share = rows // front_count
    sent_updates = lax.dynamic_slice_in_dim(
        result, 2 * rows + front_pos * update_share, update_share, 1
    )
    reduced = local_forward - product(result[:, : 2 * rows], stacked)
    spread = product(reduced, inverse_blocks)
    spread = spread.reshape(rhs, front_count, block).transpose(1, 0, 2)
    solution = jnp.sum(exchange(spread), axis=0)
    return (solution, sent_updates)


def solution(mesh):
    in_specs = (
        P(None, ("leaf", "front")),
        P(("leaf", "front"), None),
        P("leaf", "front"),
        P("leaf", None),
        P(),
        P(),
    )
    out_specs = (P(None, ("leaf", "front")), P(None, ("leaf", "front")))
    return jax.shard_map(
        on_device, mesh=mesh, in_specs=in_specs, out_specs=out_specs, check_vma=False
    )
```

time: 845 us -> 271 us (0.32)
  the two profiles are of different devices: /device:TPU:25 before, /device:TPU:26 now
where the time goes in v1:
time: 271 us; the launch traced here: 269 us
  waiting for transfers between devices  84.1 us (31%)
  blocking collectives  82.1 us (30%)
  starting transfers between devices  66.3 us (24%)
  matrix products  25.1 us (9%)
  local copies, waits for them, and re-layouts  6.65 us (2%)
  other arithmetic  3.57 us (1%)
    all_to_all x4, blocking collectives, exchange(): return lax.all_to_all(blocks, 'front', 0, 0, tiled=True)  82.1 us
    all_to_all x2, waiting for transfers between devices, exchange(): return lax.all_to_all(blocks, 'front', 0, 0, tiled=True)  42.7 us
    ppermute x7, starting transfers between devices, on_device(): sent = lax.ppermute(u_pair + product_nt(incoming, d_pair), 'leaf', up)  37.4 us
    ppermute x7, waiting for transfers between devices, on_device(): sent = lax.ppermute(w_full + product(from_above, d_pair), 'leaf', down)  32.5 us
    ppermute x7, starting transfers between devices, on_device(): sent = lax.ppermute(w_full + product(from_above, d_pair), 'leaf', down)  13.6 us
    dot_general x18, matrix products, product(): jnp.dot(left, right, precision=exact, preferred_element_type=jnp.float32)  13.4 us
    dot_general x12, matrix products, product_nt(): lax.dot_general(left, right, (((1,), (1,)), ((), ())), precision=exact, p...  11.7 us
    all_to_all x2, starting transfers between devices, exchange(): return lax.all_to_all(blocks, 'front', 0, 0, tiled=True)  11.5 us
  transfers between devices with their start and end apart: 18, of which 17 were waited for; matrix products, arithmetic and copies ran while one was open for 2% of the time, Pallas kernels for 0%

profile of v1, /device:TPU:26, one launch (start us, length us, event | category | flops | bytes accessed | tf_op | source)
XLA Modules:
  0.0 268.8 jit_solution(16048177328161426435)
XLA Ops:
  5.4 30.1 %all_to_all.30 = f32[32,16,256]{2,1,0:T(8,128)S(1)} all-to-all(f32[32,16,256]{2,1,0:T(8,128)S(1)} %bitcast.48), channel_id=1, replica_groups=mesh['leaf'=16,'front'=32] {'front'}, dimensions={0} | all-to-all | bytes 1048576 | tf_op jit(solution)/shard_map/all_to_all | solution.py:20
  35.6 21.5 %all_to_all.31 = f32[32,16,256]{2,1,0:T(8,128)} all-to-all(f32[32,16,256]{2,1,0:T(8,128)S(1)} %broadcast_in_dim.31), channel_id=1, replica_groups=mesh['leaf'=16,'front'=32] {'front'}, dimensions={0} | all-to-all | bytes 1048576 | tf_op jit(solution)/shard_map/all_to_all | solution.py:20
  58.3 5.6 %all-to-all-start = ((f32[32,64,128]{2,1,0:T(8,128)}), f32[32,64,128]{2,1,0:T(8,128)S(1)}, u32[]{:S(2)}, u32[]{:S(2)}) async-start(f32[32,64,128]{2,1,0:T(8,128)} %broadcast_in_dim.16), calls=%async_computation | async-start | bytes 2097152 | tf_op jit(solution)/shard_map/all_to_all | solution.py:20
  65.8 25.2 %all-to-all-done = f32[32,64,128]{2,1,0:T(8,128)S(1)} async-done(((f32[32,64,128]{2,1,0:T(8,128)}), f32[32,64,128]{2,1,0:T(8,128)S(1)}, u32[]{:S(2)}, u32[]{:S(2)}) %all-to-all-start) | async-done | bytes 1048608 | tf_op jit(solution)/shard_map/all_to_all | solution.py:20
  90.9 2.3 fusion.3
  94.3 14.2 %all_to_all.32 = f32[32,2,512]{2,1,0:T(2,128)S(1)} all-to-all(f32[32,2,512]{2,1,0:T(2,128)S(1)} %reshape.60), channel_id=1, replica_groups=mesh['leaf'=16,'front'=32] {'front'}, dimensions={0} | all-to-all | bytes 262144 | tf_op jit(solution)/shard_map/all_to_all | solution.py:20
  115.3 4.7 %collective-permute-start.2 = (f32[2,256]{1,0:T(2,128)}, f32[2,256]{1,0:T(2,128)S(1)}, u32[]{:S(2)}, u32[]{:S(2)}) collective-permute-start(f32[2,256]{1,0:T(2,128)} %convolution_add_fusion.15), channel_id=1, source_target_pairs={{0,64},{32,96},{64,128},{96,160},{128,192},{160,224},{192,256},{22... | collective-permute-start | bytes 6152 | tf_op jit(solution)/shard_map/ppermute | solution.py:78
  122.4 5.4 %collective-permute-start.3 = (f32[2,256]{1,0:T(2,128)S(1)}, f32[2,256]{1,0:T(2,128)S(1)}, u32[]{:S(2)}, u32[]{:S(2)}) collective-permute-start(f32[2,256]{1,0:T(2,128)S(1)} %convolution_add_fusion.14), channel_id=1, source_target_pairs={{0,64},{32,96},{64,128},{96,160},{128,192},{160,224},{192,256},{22... | collective-permute-start | bytes 6152 | tf_op jit(solution)/shard_map/ppermute | solution.py:78
  130.1 5.4 %collective-permute-start.4 = (f32[2,256]{1,0:T(2,128)S(1)}, f32[2,256]{1,0:T(2,128)S(1)}, u32[]{:S(2)}, u32[]{:S(2)}) collective-permute-start(f32[2,256]{1,0:T(2,128)S(1)} %convolution_add_fusion.13), channel_id=1, source_target_pairs={{0,64},{32,96},{64,128},{96,160},{128,192},{160,224},{192,256},{22... | collective-permute-start | bytes 6152 | tf_op jit(solution)/shard_map/ppermute | solution.py:78
  137.8 5.4 %collective-permute-start.5 = (f32[2,256]{1,0:T(2,128)S(1)}, f32[2,256]{1,0:T(2,128)S(1)}, u32[]{:S(2)}, u32[]{:S(2)}) collective-permute-start(f32[2,256]{1,0:T(2,128)S(1)} %convolution_add_fusion.12), channel_id=1, source_target_pairs={{0,64},{32,96},{64,128},{96,160},{128,192},{160,224},{192,256},{22... | collective-permute-start | bytes 6152 | tf_op jit(solution)/shard_map/ppermute | solution.py:78
  145.5 5.4 %collective-permute-start.6 = (f32[2,256]{1,0:T(2,128)S(1)}, f32[2,256]{1,0:T(2,128)S(1)}, u32[]{:S(2)}, u32[]{:S(2)}) collective-permute-start(f32[2,256]{1,0:T(2,128)S(1)} %convolution_add_fusion.11), channel_id=1, source_target_pairs={{0,64},{32,96},{64,128},{96,160},{128,192},{160,224},{192,256},{22... | collective-permute-start | bytes 6152 | tf_op jit(solution)/shard_map/ppermute | solution.py:78
  153.2 5.4 %collective-permute-start.7 = (f32[2,256]{1,0:T(2,128)S(1)}, f32[2,256]{1,0:T(2,128)S(1)}, u32[]{:S(2)}, u32[]{:S(2)}) collective-permute-start(f32[2,256]{1,0:T(2,128)S(1)} %convolution_add_fusion.10), channel_id=1, source_target_pairs={{0,64},{32,96},{64,128},{96,160},{128,192},{160,224},{192,256},{22... | collective-permute-start | bytes 6152 | tf_op jit(solution)/shard_map/ppermute | solution.py:78
  160.9 5.5 %collective-permute-start.8 = (f32[2,256]{1,0:T(2,128)S(1)}, f32[2,256]{1,0:T(2,128)S(1)}, u32[]{:S(2)}, u32[]{:S(2)}) collective-permute-start(f32[2,256]{1,0:T(2,128)S(1)} %convolution_add_fusion.9), channel_id=1, source_target_pairs={{0,64},{32,96},{64,128},{96,160},{128,192},{160,224},{192,256},{22... | collective-permute-start | bytes 6152 | tf_op jit(solution)/shard_map/ppermute | solution.py:78
  172.0 5.3 %collective-permute-done.9 = f32[2,256]{1,0:T(2,128)} collective-permute-done((f32[2,256]{1,0:T(2,128)}, f32[2,256]{1,0:T(2,128)}, u32[]{:S(2)}, u32[]{:S(2)}) %collective-permute-start.9) | collective-permute-done | bytes 2080 | tf_op jit(solution)/shard_map/ppermute | solution.py:83
  178.3 2.0 collective-permute-start.10
  180.2 4.8 %collective-permute-done.10 = f32[2,256]{1,0:T(2,128)S(1)} collective-permute-done((f32[2,256]{1,0:T(2,128)S(1)}, f32[2,256]{1,0:T(2,128)S(1)}, u32[]{:S(2)}, u32[]{:S(2)}) %collective-permute-start.10) | collective-permute-done | bytes 2080 | tf_op jit(solution)/shard_map/ppermute | solution.py:83
  187.8 4.8 %collective-permute-done.11 = f32[2,256]{1,0:T(2,128)S(1)} collective-permute-done((f32[2,256]{1,0:T(2,128)S(1)}, f32[2,256]{1,0:T(2,128)S(1)}, u32[]{:S(2)}, u32[]{:S(2)}) %collective-permute-start.11) | collective-permute-done | bytes 2080 | tf_op jit(solution)/shard_map/ppermute | solution.py:83
  195.4 4.8 %collective-permute-done.12 = f32[2,256]{1,0:T(2,128)S(1)} collective-permute-done((f32[2,256]{1,0:T(2,128)S(1)}, f32[2,256]{1,0:T(2,128)S(1)}, u32[]{:S(2)}, u32[]{:S(2)}) %collective-permute-start.12) | collective-permute-done | bytes 2080 | tf_op jit(solution)/shard_map/ppermute | solution.py:83
  203.0 4.8 %collective-permute-done.13 = f32[2,256]{1,0:T(2,128)S(1)} collective-permute-done((f32[2,256]{1,0:T(2,128)S(1)}, f32[2,256]{1,0:T(2,128)S(1)}, u32[]{:S(2)}, u32[]{:S(2)}) %collective-permute-start.13) | collective-permute-done | bytes 2080 | tf_op jit(solution)/shard_map/ppermute | solution.py:83
  211.8 3.6 %collective-permute-done.14 = f32[2,256]{1,0:T(2,128)S(1)} collective-permute-done((f32[2,256]{1,0:T(2,128)S(1)}, f32[2,256]{1,0:T(2,128)S(1)}, u32[]{:S(2)}, u32[]{:S(2)}) %collective-permute-start.14) | collective-permute-done | bytes 2080 | tf_op jit(solution)/shard_map/ppermute | solution.py:83
  218.5 4.5 %collective-permute-done.15 = f32[2,256]{1,0:T(2,128)S(1)} collective-permute-done((f32[2,256]{1,0:T(2,128)S(1)}, f32[2,256]{1,0:T(2,128)S(1)}, u32[]{:S(2)}, u32[]{:S(2)}) %collective-permute-start.15) | collective-permute-done | bytes 2080 | tf_op jit(solution)/shard_map/ppermute | solution.py:83
  224.9 16.2 %all_to_all.33 = f32[32,2,768]{2,1,0:T(2,128)S(1)} all-to-all(f32[32,2,768]{2,1,0:T(2,128)S(1)} %broadcast_in_dim.32), channel_id=1, replica_groups=mesh['leaf'=16,'front'=32] {'front'}, dimensions={0} | all-to-all | bytes 393216 | tf_op jit(solution)/shard_map/all_to_all | solution.py:20
  244.0 5.9 %all-to-all-start.5 = ((f32[32,64,128]{2,1,0:T(8,128)}), f32[32,64,128]{2,1,0:T(8,128)S(1)}, u32[]{:S(2)}, u32[]{:S(2)}) async-start(f32[32,64,128]{2,1,0:T(8,128)} %bitcast.46), calls=%async_computation.5 | async-start | bytes 2097152 | tf_op jit(solution)/shard_map/all_to_all | solution.py:20
  250.6 17.5 %all-to-all-done.5 = f32[32,64,128]{2,1,0:T(8,128)S(1)} async-done(((f32[32,64,128]{2,1,0:T(8,128)}), f32[32,64,128]{2,1,0:T(8,128)S(1)}, u32[]{:S(2)}, u32[]{:S(2)}) %all-to-all-start.5) | async-done | bytes 1048608 | tf_op jit(solution)/shard_map/all_to_all | solution.py:20
  (78 shorter events, 57.5 us)
Async XLA Ops:
  2.0 2.8 %copy-start.1 = (f32[256,128]{1,0:T(8,128)S(1)}, f32[256,128]{1,0:T(8,128)}, u32[]{:S(2)}) copy-start(f32[256,128]{1,0:T(8,128)} %param.8) | copy-start | bytes 393220
  4.7 52.4 %copy-start.5 = (f32[64,128]{1,0:T(8,128)S(1)}, f32[64,128]{1,0:T(8,128)}, u32[]{:S(2)}) copy-start(f32[64,128]{1,0:T(8,128)} %param.6) | copy-start | bytes 98308
  35.6 55.3 %copy-start = (f32[128,4096]{1,0:T(8,128)S(1)}, f32[128,4096]{1,0:T(8,128)}, u32[]{:S(2)}) copy-start(f32[128,4096]{1,0:T(8,128)} %param.7) | copy-start | bytes 6291460
  58.3 32.7 %all-to-all-start = ((f32[32,64,128]{2,1,0:T(8,128)}), f32[32,64,128]{2,1,0:T(8,128)S(1)}, u32[]{:S(2)}, u32[]{:S(2)}) async-start(f32[32,64,128]{2,1,0:T(8,128)} %broadcast_in_dim.16), calls=%async_computation | async-start | bytes 2097152 | tf_op jit(solution)/shard_map/all_to_all | solution.py:20
  63.8 47.8 %collective-permute-start.1 = (f32[512,256]{1,0:T(8,128)}, f32[512,256]{1,0:T(8,128)}, u32[]{:S(2)}, u32[]{:S(2)}) collective-permute-start(f32[512,256]{1,0:T(8,128)} %bitcast.47), channel_id=1, source_target_pairs={{0,32},{32,0},{64,96},{96,64},{128,160},{160,128},{192,224},{224,1... | collective-permute-start | bytes 1572872 | tf_op jit(solution)/shard_map/ppermute | solution.py:59
  93.2 0.6 copy-start.3
  108.6 3.1 %collective-permute-start = (f32[2,512]{1,0:T(2,128)S(1)}, f32[2,512]{1,0:T(2,128)S(1)}, u32[]{:S(2)}, u32[]{:S(2)}) collective-permute-start(f32[2,512]{1,0:T(2,128)S(1)} %reduce_sum.27), channel_id=1, source_target_pairs={{0,32},{32,0},{64,96},{96,64},{128,160},{160,128},{192,224},{224,1... | collective-permute-start | bytes 12296 | tf_op jit(solution)/shard_map/ppermute | solution.py:60
  115.3 6.2 %collective-permute-start.2 = (f32[2,256]{1,0:T(2,128)}, f32[2,256]{1,0:T(2,128)S(1)}, u32[]{:S(2)}, u32[]{:S(2)}) collective-permute-start(f32[2,256]{1,0:T(2,128)} %convolution_add_fusion.15), channel_id=1, source_target_pairs={{0,64},{32,96},{64,128},{96,160},{128,192},{160,224},{192,256},{22... | collective-permute-start | bytes 6152 | tf_op jit(solution)/shard_map/ppermute | solution.py:78
  122.4 6.7 %collective-permute-start.3 = (f32[2,256]{1,0:T(2,128)S(1)}, f32[2,256]{1,0:T(2,128)S(1)}, u32[]{:S(2)}, u32[]{:S(2)}) collective-permute-start(f32[2,256]{1,0:T(2,128)S(1)} %convolution_add_fusion.14), channel_id=1, source_target_pairs={{0,64},{32,96},{64,128},{96,160},{128,192},{160,224},{192,256},{22... | collective-permute-start | bytes 6152 | tf_op jit(solution)/shard_map/ppermute | solution.py:78
  130.1 6.7 %collective-permute-start.4 = (f32[2,256]{1,0:T(2,128)S(1)}, f32[2,256]{1,0:T(2,128)S(1)}, u32[]{:S(2)}, u32[]{:S(2)}) collective-permute-start(f32[2,256]{1,0:T(2,128)S(1)} %convolution_add_fusion.13), channel_id=1, source_target_pairs={{0,64},{32,96},{64,128},{96,160},{128,192},{160,224},{192,256},{22... | collective-permute-start | bytes 6152 | tf_op jit(solution)/shard_map/ppermute | solution.py:78
  137.8 6.7 %collective-permute-start.5 = (f32[2,256]{1,0:T(2,128)S(1)}, f32[2,256]{1,0:T(2,128)S(1)}, u32[]{:S(2)}, u32[]{:S(2)}) collective-permute-start(f32[2,256]{1,0:T(2,128)S(1)} %convolution_add_fusion.12), channel_id=1, source_target_pairs={{0,64},{32,96},{64,128},{96,160},{128,192},{160,224},{192,256},{22... | collective-permute-start | bytes 6152 | tf_op jit(solution)/shard_map/ppermute | solution.py:78
  145.5 6.7 %collective-permute-start.6 = (f32[2,256]{1,0:T(2,128)S(1)}, f32[2,256]{1,0:T(2,128)S(1)}, u32[]{:S(2)}, u32[]{:S(2)}) collective-permute-start(f32[2,256]{1,0:T(2,128)S(1)} %convolution_add_fusion.11), channel_id=1, source_target_pairs={{0,64},{32,96},{64,128},{96,160},{128,192},{160,224},{192,256},{22... | collective-permute-start | bytes 6152 | tf_op jit(solution)/shard_map/ppermute | solution.py:78
  153.2 6.7 %collective-permute-start.7 = (f32[2,256]{1,0:T(2,128)S(1)}, f32[2,256]{1,0:T(2,128)S(1)}, u32[]{:S(2)}, u32[]{:S(2)}) collective-permute-start(f32[2,256]{1,0:T(2,128)S(1)} %convolution_add_fusion.10), channel_id=1, source_target_pairs={{0,64},{32,96},{64,128},{96,160},{128,192},{160,224},{192,256},{22... | collective-permute-start | bytes 6152 | tf_op jit(solution)/shard_map/ppermute | solution.py:78
  160.9 6.8 %collective-permute-start.8 = (f32[2,256]{1,0:T(2,128)S(1)}, f32[2,256]{1,0:T(2,128)S(1)}, u32[]{:S(2)}, u32[]{:S(2)}) collective-permute-start(f32[2,256]{1,0:T(2,128)S(1)} %convolution_add_fusion.9), channel_id=1, source_target_pairs={{0,64},{32,96},{64,128},{96,160},{128,192},{160,224},{192,256},{22... | collective-permute-start | bytes 6152 | tf_op jit(solution)/shard_map/ppermute | solution.py:78
  170.1 7.3 %collective-permute-start.9 = (f32[2,256]{1,0:T(2,128)}, f32[2,256]{1,0:T(2,128)}, u32[]{:S(2)}, u32[]{:S(2)}) collective-permute-start(f32[2,256]{1,0:T(2,128)} %convolution_add_fusion.8), channel_id=1, source_target_pairs={{64,0},{96,32},{128,64},{160,96},{192,128},{224,160},{256,192},{28... | collective-permute-start | bytes 6152 | tf_op jit(solution)/shard_map/ppermute | solution.py:83
  178.3 6.7 %collective-permute-start.10 = (f32[2,256]{1,0:T(2,128)S(1)}, f32[2,256]{1,0:T(2,128)S(1)}, u32[]{:S(2)}, u32[]{:S(2)}) collective-permute-start(f32[2,256]{1,0:T(2,128)S(1)} %convolution_add_fusion.7), channel_id=1, source_target_pairs={{64,0},{96,32},{128,64},{160,96},{192,128},{224,160},{256,192},{28... | collective-permute-start | bytes 6152 | tf_op jit(solution)/shard_map/ppermute | solution.py:83
  185.9 6.7 %collective-permute-start.11 = (f32[2,256]{1,0:T(2,128)S(1)}, f32[2,256]{1,0:T(2,128)S(1)}, u32[]{:S(2)}, u32[]{:S(2)}) collective-permute-start(f32[2,256]{1,0:T(2,128)S(1)} %convolution_add_fusion.6), channel_id=1, source_target_pairs={{64,0},{96,32},{128,64},{160,96},{192,128},{224,160},{256,192},{28... | collective-permute-start | bytes 6152 | tf_op jit(solution)/shard_map/ppermute | solution.py:83
  193.5 6.7 %collective-permute-start.12 = (f32[2,256]{1,0:T(2,128)S(1)}, f32[2,256]{1,0:T(2,128)S(1)}, u32[]{:S(2)}, u32[]{:S(2)}) collective-permute-start(f32[2,256]{1,0:T(2,128)S(1)} %convolution_add_fusion.5), channel_id=1, source_target_pairs={{64,0},{96,32},{128,64},{160,96},{192,128},{224,160},{256,192},{28... | collective-permute-start | bytes 6152 | tf_op jit(solution)/shard_map/ppermute | solution.py:83
  201.1 6.7 %collective-permute-start.13 = (f32[2,256]{1,0:T(2,128)S(1)}, f32[2,256]{1,0:T(2,128)S(1)}, u32[]{:S(2)}, u32[]{:S(2)}) collective-permute-start(f32[2,256]{1,0:T(2,128)S(1)} %convolution_add_fusion.4), channel_id=1, source_target_pairs={{64,0},{96,32},{128,64},{160,96},{192,128},{224,160},{256,192},{28... | collective-permute-start | bytes 6152 | tf_op jit(solution)/shard_map/ppermute | solution.py:83
  208.7 6.7 %collective-permute-start.14 = (f32[2,256]{1,0:T(2,128)S(1)}, f32[2,256]{1,0:T(2,128)S(1)}, u32[]{:S(2)}, u32[]{:S(2)}) collective-permute-start(f32[2,256]{1,0:T(2,128)S(1)} %convolution_add_fusion.3), channel_id=1, source_target_pairs={{64,0},{96,32},{128,64},{160,96},{192,128},{224,160},{256,192},{28... | collective-permute-start | bytes 6152 | tf_op jit(solution)/shard_map/ppermute | solution.py:83
  211.7 29.6 %copy-start.2 = (f32[256,128]{1,0:T(8,128)S(1)}, f32[256,128]{1,0:T(8,128)}, u32[]{:S(2)}) copy-start(f32[256,128]{1,0:T(8,128)} %param.8) | copy-start | bytes 393220
  211.7 29.6 %copy-start.4 = (f32[64,128]{1,0:T(8,128)S(1)}, f32[64,128]{1,0:T(8,128)}, u32[]{:S(2)}) copy-start(f32[64,128]{1,0:T(8,128)} %copy-done.3) | copy-start | bytes 98308
  216.3 6.7 %collective-permute-start.15 = (f32[2,256]{1,0:T(2,128)S(1)}, f32[2,256]{1,0:T(2,128)S(1)}, u32[]{:S(2)}, u32[]{:S(2)}) collective-permute-start(f32[2,256]{1,0:T(2,128)S(1)} %convolution_add_fusion.2), channel_id=1, source_target_pairs={{64,0},{96,32},{128,64},{160,96},{192,128},{224,160},{256,192},{28... | collective-permute-start | bytes 6152 | tf_op jit(solution)/shard_map/ppermute | solution.py:83
  244.0 24.2 %all-to-all-start.5 = ((f32[32,64,128]{2,1,0:T(8,128)}), f32[32,64,128]{2,1,0:T(8,128)S(1)}, u32[]{:S(2)}, u32[]{:S(2)}) async-start(f32[32,64,128]{2,1,0:T(8,128)} %bitcast.46), calls=%async_computation.5 | async-start | bytes 2097152 | tf_op jit(solution)/shard_map/all_to_all | solution.py:20

commit v2 on v1

--- a/solution.py
+++ b/solution.py
@@ -23,6 +23,13 @@
 def gather_front(block):
     count = lax.axis_size("front")
     return exchange(jnp.broadcast_to(block[None], (count, *block.shape)))
+
+
+def gather_line(block):
+    count = lax.axis_size("leaf")
+    lines = [list(range(core, count, 2)) for core in range(2)]
+    copies = jnp.broadcast_to(block[None], (count // 2, *block.shape))
+    return lax.all_to_all(copies, "leaf", 0, 0, tiled=True, axis_index_groups=lines)
 
 
 def scatter_front(total):
@@ -54,8 +61,6 @@
     vectors = scatter_front(product_nt(local_forward, stacked))
 
     swap = [(s, s ^ 1) for s in range(leaf_count)]
-    up = [(s, (s + 2) % leaf_count) for s in range(leaf_count)]
-    down = [(target, source) for source, target in up]
     mate_coupling = lax.ppermute(coupling, "leaf", swap)
     mate_vectors = lax.ppermute(vectors, "leaf", swap)
     low = jnp.where(is_upper, mate_coupling, coupling)
@@ -73,15 +78,22 @@
 
     below_rows = lax.dynamic_slice_in_dim(below_update, front_pos * share, share, 0)
     above_rows = lax.dynamic_slice_in_dim(above_solution, front_pos * share, share, 0)
-    incoming = below_rows
-    for _ in range(leaf_count // 2 - 1):
-        sent = lax.ppermute(u_pair + product_nt(incoming, d_pair), "leaf", up)
-        incoming = jnp.where(leaf_pos < 2, below_rows, sent)
-    w_full = w_pair - product(incoming, g_pair)
-    from_above = above_rows
-    for _ in range(leaf_count // 2 - 1):
-        sent = lax.ppermute(w_full + product(from_above, d_pair), "leaf", down)
-        from_above = jnp.where(leaf_pos >= leaf_count - 2, above_rows, sent)
+    pairs = leaf_count // 2
+    chip = leaf_pos // 2
+    own_half = gather_line(jnp.where(is_upper, g_pair, d_pair))
+    mate_half = lax.ppermute(own_half, "leaf", swap)
+    d_all = jnp.where(is_upper, mate_half, own_half)
+    g_all = jnp.where(is_upper, own_half, mate_half)
+    vec_all = gather_line(jnp.concatenate([u_pair, w_pair], axis=1))
+    into = [below_rows]
+    for y in range(pairs - 1):
+        into.append(vec_all[y, :, :rows] + product_nt(into[-1], d_all[y]))
+    above = [above_rows]
+    for y in range(pairs - 1, 0, -1):
+        w_row = vec_all[y, :, rows:] - product(into[y], g_all[y])
+        above.append(w_row + product(above[-1], d_all[y]))
+    incoming = jnp.take(jnp.stack(into), chip, axis=0)
+    from_above = jnp.take(jnp.stack(above[::-1]), chip, axis=0)
 
     middle = u_low + product_nt(incoming, d_low)
     own_incoming = jnp.where(is_upper, middle, incoming)

time: 271 us -> 258 us (0.952)
  the two profiles are of different devices: /device:TPU:26 before, /device:TPU:2 now
where the time goes in v2:
time: 258 us; the launch traced here: 257 us
  blocking collectives  124 us (48%)
  waiting for transfers between devices  65.1 us (25%)
  starting transfers between devices  26.1 us (10%)
  matrix products  24.9 us (10%)
  local copies, waits for them, and re-layouts  9.68 us (4%)
  other arithmetic  5.63 us (2%)
    all_to_all x3, blocking collectives, exchange(): return lax.all_to_all(blocks, 'front', 0, 0, tiled=True)  65.8 us
    all_to_all x3, waiting for transfers between devices, exchange(): return lax.all_to_all(blocks, 'front', 0, 0, tiled=True)  59.4 us
    all_to_all x1, blocking collectives, gather_line(): lax.all_to_all(copies, 'leaf', 0, 0, tiled=True, axis_index_groups=lines)  58.5 us
    all_to_all x3, starting transfers between devices, exchange(): return lax.all_to_all(blocks, 'front', 0, 0, tiled=True)  17 us
    dot_general x12, matrix products, product_nt(): lax.dot_general(left, right, (((1,), (1,)), ((), ())), precision=exact, p...  14 us
    dot_general x24, matrix products, product(): jnp.dot(left, right, precision=exact, preferred_element_type=jnp.float32)  10.9 us
  transfers between devices with their start and end apart: 7, of which 6 were waited for; matrix products, arithmetic and copies ran while one was open for 5% of the time, Pallas kernels for 0%

profile of v2, /device:TPU:2, one launch (start us, length us, event | category | flops | bytes accessed | tf_op | source)
XLA Modules:
  0.0 256.7 jit_solution(5767966344148392024)
XLA Ops:
  0.6 1.9 copy.13
  4.1 30.1 %all_to_all.40 = f32[32,16,256]{2,1,0:T(8,128)S(1)} all-to-all(f32[32,16,256]{2,1,0:T(8,128)S(1)} %bitcast.218), channel_id=1, replica_groups=mesh['leaf'=16,'front'=32] {'front'}, dimensions={0} | all-to-all | bytes 1048576 | tf_op jit(solution)/shard_map/all_to_all | solution.py:20
  34.3 21.3 %all_to_all.41 = f32[32,16,256]{2,1,0:T(8,128)S(1)} all-to-all(f32[32,16,256]{2,1,0:T(8,128)S(1)} %broadcast_in_dim.52), channel_id=1, replica_groups=mesh['leaf'=16,'front'=32] {'front'}, dimensions={0} | all-to-all | bytes 1048576 | tf_op jit(solution)/shard_map/all_to_all | solution.py:20
  55.6 1.9 collective-permute-start.1
  57.5 1.9 collective-permute-done.1
  61.0 58.5 %all_to_all.42 = f32[8,256,256]{2,1,0:T(8,128)} all-to-all(f32[8,256,256]{2,1,0:T(8,128)S(1)} %broadcast_in_dim.54), channel_id=1, replica_groups={{0,64,128,192,256,320,384,448},{32,96,160,224,288,352,416,480},{1,65,12..., dimensions={0} | all-to-all | bytes 4194304 | tf_op jit(solution)/shard_map/all_to_all | solution.py:32
  120.6 5.6 %all-to-all-start = ((f32[32,64,128]{2,1,0:T(8,128)}), f32[32,64,128]{2,1,0:T(8,128)}, u32[]{:S(2)}, u32[]{:S(2)}) async-start(f32[32,64,128]{2,1,0:T(8,128)} %broadcast_in_dim.29), calls=%async_computation | async-start | bytes 2097152 | tf_op jit(solution)/shard_map/all_to_all | solution.py:20
  126.3 1.9 collective-permute-start.2
  128.2 25.4 %all-to-all-done = f32[32,64,128]{2,1,0:T(8,128)} async-done(((f32[32,64,128]{2,1,0:T(8,128)}), f32[32,64,128]{2,1,0:T(8,128)}, u32[]{:S(2)}, u32[]{:S(2)}) %all-to-all-start) | async-done | bytes 1048608 | tf_op jit(solution)/shard_map/all_to_all | solution.py:20
  153.6 3.5 %fusion.12 = f32[64,128]{1,0:T(8,128)S(1)} fusion(f32[128,4096]{1,0:T(8,128)S(1)} %copy-done, f32[32,64,128]{2,1,0:T(8,128)} %all-to-all-done), kind=kOutput, calls=%fused_computation.34 | convolution fusion | flops 402653184 | bytes 3178496 | tf_op jit(solution)/shard_map/dot_general | solution.py:14
  158.8 5.6 %all-to-all-start.1 = ((f32[32,2,512]{2,1,0:T(2,128)}), f32[32,2,512]{2,1,0:T(2,128)S(1)}, u32[]{:S(2)}, u32[]{:S(2)}) async-start(f32[32,2,512]{2,1,0:T(2,128)} %reshape.63), calls=%async_computation.1 | async-start | bytes 262144 | tf_op jit(solution)/shard_map/all_to_all | solution.py:20
  164.4 8.9 %all-to-all-done.1 = f32[32,2,512]{2,1,0:T(2,128)S(1)} async-done(((f32[32,2,512]{2,1,0:T(2,128)}), f32[32,2,512]{2,1,0:T(2,128)S(1)}, u32[]{:S(2)}, u32[]{:S(2)}) %all-to-all-start.1) | async-done | bytes 131104 | tf_op jit(solution)/shard_map/all_to_all | solution.py:20
  173.3 1.9 collective-permute-start
  177.8 3.3 %all-to-all-start.4 = ((f32[8,2,512]{2,1,0:T(2,128)}), f32[8,2,512]{2,1,0:T(2,128)S(1)}, u32[]{:S(2)}, u32[]{:S(2)}) async-start(f32[8,2,512]{2,1,0:T(2,128)} %broadcast_in_dim.53), calls=%async_computation.4 | async-start | bytes 65536 | tf_op jit(solution)/shard_map/all_to_all | solution.py:32
  181.1 4.6 %broadcast_select_fusion = (f32[8,256,256]{2,1,0:T(8,128)}, f32[8,256,256]{2,1,0:T(8,128)}) fusion(f32[8,256,256]{2,1,0:T(8,128)} %all_to_all.42, f32[8,256,256]{2,1,0:T(8,128)} %collective-permute-done.2, pred[]{:T(512)S(6)} %eq.5), kind=kLoop, calls=%fused_computation.38 | loop fusion | flops 1048576 | bytes 8388609 | tf_op jit(solution)/shard_map/jit(_where)/select_n | solution.py:86
  185.7 3.4 %all-to-all-done.4 = f32[8,2,512]{2,1,0:T(2,128)S(1)} async-done(((f32[8,2,512]{2,1,0:T(2,128)}), f32[8,2,512]{2,1,0:T(2,128)S(1)}, u32[]{:S(2)}, u32[]{:S(2)}) %all-to-all-start.4) | async-done | bytes 32800 | tf_op jit(solution)/shard_map/all_to_all | solution.py:32
  189.1 1.4 constant_dynamic-update-slice_fusion.13
  190.5 1.4 constant_dynamic-update-slice_fusion.12
  193.2 1.3 constant_dynamic-update-slice_fusion.10
  194.5 1.3 constant_dynamic-update-slice_fusion.9
  195.7 1.3 constant_dynamic-update-slice_fusion.8
  207.1 14.4 %all_to_all.43 = f32[32,2,768]{2,1,0:T(2,128)S(1)} all-to-all(f32[32,2,768]{2,1,0:T(2,128)S(1)} %broadcast_in_dim.55), channel_id=1, replica_groups=mesh['leaf'=16,'front'=32] {'front'}, dimensions={0} | all-to-all | bytes 393216 | tf_op jit(solution)/shard_map/all_to_all | solution.py:20
  224.3 5.8 %all-to-all-start.7 = ((f32[32,64,128]{2,1,0:T(8,128)}), f32[32,64,128]{2,1,0:T(8,128)S(1)}, u32[]{:S(2)}, u32[]{:S(2)}) async-start(f32[32,64,128]{2,1,0:T(8,128)} %bitcast.216), calls=%async_computation.7 | async-start | bytes 2097152 | tf_op jit(solution)/shard_map/all_to_all | solution.py:20
  230.8 25.2 %all-to-all-done.7 = f32[32,64,128]{2,1,0:T(8,128)S(1)} async-done(((f32[32,64,128]{2,1,0:T(8,128)}), f32[32,64,128]{2,1,0:T(8,128)S(1)}, u32[]{:S(2)}, u32[]{:S(2)}) %all-to-all-start.7) | async-done | bytes 1048608 | tf_op jit(solution)/shard_map/all_to_all | solution.py:20
  (78 shorter events, 24.1 us)
Async XLA Ops:
  0.6 2.0 copy-start.7
  0.6 2.9 %copy-start.3 = (f32[256,128]{1,0:T(8,128)S(1)}, f32[256,128]{1,0:T(8,128)}, u32[]{:S(2)}) copy-start(f32[256,128]{1,0:T(8,128)} %param.10) | copy-start | bytes 393220
  55.6 3.8 %collective-permute-start.1 = (f32[512,256]{1,0:T(8,128)S(1)}, f32[512,256]{1,0:T(8,128)S(1)}, u32[]{:S(2)}, u32[]{:S(2)}) collective-permute-start(f32[512,256]{1,0:T(8,128)S(1)} %bitcast.217), channel_id=1, source_target_pairs={{0,32},{32,0},{64,96},{96,64},{128,160},{160,128},{192,224},{224,1... | collective-permute-start | bytes 1572872 | tf_op jit(solution)/shard_map/ppermute | solution.py:64
  61.0 58.5 %copy-start.6 = (f32[64,128]{1,0:T(8,128)S(1)}, f32[64,128]{1,0:T(8,128)}, u32[]{:S(2)}) copy-start(f32[64,128]{1,0:T(8,128)} %param.8) | copy-start | bytes 98308
  119.5 34.0 %copy-start = (f32[128,4096]{1,0:T(8,128)S(1)}, f32[128,4096]{1,0:T(8,128)}, u32[]{:S(2)}) copy-start(f32[128,4096]{1,0:T(8,128)} %param.9) | copy-start | bytes 6291460
  120.6 32.9 %all-to-all-start = ((f32[32,64,128]{2,1,0:T(8,128)}), f32[32,64,128]{2,1,0:T(8,128)}, u32[]{:S(2)}, u32[]{:S(2)}) async-start(f32[32,64,128]{2,1,0:T(8,128)} %broadcast_in_dim.29), calls=%async_computation | async-start | bytes 2097152 | tf_op jit(solution)/shard_map/all_to_all | solution.py:20
  126.3 54.9 %collective-permute-start.2 = (f32[8,256,256]{2,1,0:T(8,128)}, f32[8,256,256]{2,1,0:T(8,128)}, u32[]{:S(2)}, u32[]{:S(2)}) collective-permute-start(f32[8,256,256]{2,1,0:T(8,128)} %all_to_all.42), channel_id=1, source_target_pairs={{0,32},{32,0},{64,96},{96,64},{128,160},{160,128},{192,224},{224,1... | collective-permute-start | bytes 6291464 | tf_op jit(solution)/shard_map/ppermute | solution.py:84
  157.1 0.6 copy-start.4
  158.8 14.4 %all-to-all-start.1 = ((f32[32,2,512]{2,1,0:T(2,128)}), f32[32,2,512]{2,1,0:T(2,128)S(1)}, u32[]{:S(2)}, u32[]{:S(2)}) async-start(f32[32,2,512]{2,1,0:T(2,128)} %reshape.63), calls=%async_computation.1 | async-start | bytes 262144 | tf_op jit(solution)/shard_map/all_to_all | solution.py:20
  173.3 3.1 %collective-permute-start = (f32[2,512]{1,0:T(2,128)S(1)}, f32[2,512]{1,0:T(2,128)S(1)}, u32[]{:S(2)}, u32[]{:S(2)}) collective-permute-start(f32[2,512]{1,0:T(2,128)S(1)} %reduce_sum.27), channel_id=1, source_target_pairs={{0,32},{32,0},{64,96},{96,64},{128,160},{160,128},{192,224},{224,1... | collective-permute-start | bytes 12296 | tf_op jit(solution)/shard_map/ppermute | solution.py:65
  177.8 11.3 %all-to-all-start.4 = ((f32[8,2,512]{2,1,0:T(2,128)}), f32[8,2,512]{2,1,0:T(2,128)S(1)}, u32[]{:S(2)}, u32[]{:S(2)}) async-start(f32[8,2,512]{2,1,0:T(2,128)} %broadcast_in_dim.53), calls=%async_computation.4 | async-start | bytes 65536 | tf_op jit(solution)/shard_map/all_to_all | solution.py:32
  189.1 9.9 %copy-start.1 = (f32[8,256,256]{2,1,0:T(8,128)S(1)}, f32[8,256,256]{2,1,0:T(8,128)}, u32[]{:S(2)}) copy-start(f32[8,256,256]{2,1,0:T(8,128)} %get-tuple-element.19) | copy-start | bytes 6291460
  190.5 13.7 %copy-start.2 = (f32[8,256,256]{2,1,0:T(8,128)S(1)}, f32[8,256,256]{2,1,0:T(8,128)}, u32[]{:S(2)}) copy-start(f32[8,256,256]{2,1,0:T(8,128)} %get-tuple-element.18) | copy-start | bytes 6291460
  202.5 19.1 %copy-start.5 = (f32[64,128]{1,0:T(8,128)S(1)}, f32[64,128]{1,0:T(8,128)}, u32[]{:S(2)}) copy-start(f32[64,128]{1,0:T(8,128)} %copy-done.4) | copy-start | bytes 98308
  224.3 31.8 %all-to-all-start.7 = ((f32[32,64,128]{2,1,0:T(8,128)}), f32[32,64,128]{2,1,0:T(8,128)S(1)}, u32[]{:S(2)}, u32[]{:S(2)}) async-start(f32[32,64,128]{2,1,0:T(8,128)} %bitcast.216), calls=%async_computation.7 | async-start | bytes 2097152 | tf_op jit(solution)/shard_map/all_to_all | solution.py:20

commit v3 on v1

v3 whole, which is shorter than its diff:
```python
import jax
import jax.numpy as jnp
from jax import lax
from jax.experimental import pallas as pl
from jax.experimental.pallas import tpu as pltpu
from jax.sharding import PartitionSpec as P

exact = lax.Precision.HIGHEST
x_chips = 4
padded = 8


def product(left, right):
    return jnp.dot(left, right, precision=exact, preferred_element_type=jnp.float32)


def product_nt(left, right):
    return lax.dot_general(
        left, right, (((1,), (1,)), ((), ())), precision=exact, preferred_element_type=jnp.float32
    )


def exchange(blocks, axis="front", groups=None):
    return lax.all_to_all(blocks, axis, 0, 0, tiled=True, axis_index_groups=groups)


def copies(block, count):
    return jnp.broadcast_to(block[None], (count, *block.shape))


def gather_front(block):
    return exchange(copies(block, lax.axis_size("front")))


def scatter_front(total):
    count = lax.axis_size("front")
    pieces = total.reshape(count, total.shape[0] // count, *total.shape[1:])
    return jnp.sum(exchange(pieces), axis=0)


def gather_leaf(block):
    return lax.all_gather(block, "leaf", axis=0)


def gather_leaf_small(block):
    return exchange(copies(block, lax.axis_size("leaf")), "leaf")


def gather_along_z(block):
    count = lax.axis_size("front")
    groups = [list(range(x, count, x_chips)) for x in range(x_chips)]
    wide = jnp.concatenate([block, jnp.zeros((3 * block.shape[0], block.shape[1]), block.dtype)])
    wide = lax.all_gather(wide, "front", axis=0, axis_index_groups=groups)
    return wide[:, : block.shape[0]]


def gather_along_x(planes):
    count = lax.axis_size("front")
    groups = [list(range(first, first + x_chips)) for first in range(0, count, x_chips)]
    whole = exchange(copies(planes, x_chips), "front", groups)
    return whole.transpose(1, 0, 2, 3).reshape(count, *planes.shape[1:])


def split(value):
    head = value.astype(jnp.bfloat16)
    return head, (value - head.astype(jnp.float32)).astype(jnp.bfloat16)


def two_parts(value):
    head, tail = split(value)
    return jnp.concatenate([head.astype(jnp.float32), tail.astype(jnp.float32)]).astype(
        jnp.bfloat16
    )


def dot_parts(parts, head, tail, contract):
    dims = (((1,), (contract,)), ((), ()))
    both = lax.dot_general(parts, head, dims, preferred_element_type=jnp.float32)
    both += lax.dot_general(parts, tail, dims, preferred_element_type=jnp.float32)
    return both[:padded] + both[padded:]


def chain_kernel(
    pos_ref, coupling_ref, vector_ref, below_ref, above_ref, out_ref,
    held, head, tail, vectors, into, above, sems,
):
    sections, share, _ = vector_ref.shape
    rows = below_ref.shape[1]

    def fetch(s):
        return pltpu.make_async_copy(coupling_ref.at[s], held.at[s], sems.at[s])

    for s in range(sections):
        fetch(s).start()
    vectors[...] = jnp.zeros_like(vectors)
    into[0] = jnp.zeros_like(into[0])
    above[sections - 1] = jnp.zeros_like(into[0])
    for s in range(sections):
        vectors[s, :share, :] = vector_ref[s]
    into[0, :share, :] = below_ref[...]
    above[sections - 1, :share, :] = above_ref[...]

    incoming = into[0]
    for s in range(sections):
        fetch(s).wait()
        block_head, block_tail = split(held[s])
        head[s] = block_head[:rows]
        tail[s] = block_tail[:rows]
        result = vectors[s] - dot_parts(two_parts(incoming), block_head, block_tail, 1)
        incoming = result[:, :rows]
        into[s + 1] = incoming
        vectors[s] = result
    from_above = above[sections - 1]
    for s in range(sections - 1, 0, -1):
        taken = dot_parts(two_parts(from_above), head[s], tail[s], 0)
        from_above = vectors[s, :, rows:] - taken
        above[s - 1] = from_above

    own = pos_ref[0]
    kept = jnp.concatenate([above[own], into[own], into[own + 1]], axis=1)[:share]
    for piece in range(out_ref.shape[0]):
        out_ref[piece] = kept


def run_chain(position, coupling_all, vector_all, below_rows, above_rows, targets):
    sections, share, _ = vector_all.shape
    rows = below_rows.shape[1]
    vmem = pl.BlockSpec(memory_space=pltpu.VMEM)
    return pl.pallas_call(
        chain_kernel,
        out_shape=jax.ShapeDtypeStruct((targets, share, 3 * rows), jnp.float32),
        in_specs=[
            pl.BlockSpec(memory_space=pltpu.SMEM),
            pl.BlockSpec(memory_space=pl.ANY),
            vmem,
            vmem,
            vmem,
        ],
        out_specs=vmem,
        scratch_shapes=[
            pltpu.VMEM((sections, 2 * rows, rows), jnp.float32),
            pltpu.VMEM((sections, rows, rows), jnp.bfloat16),
            pltpu.VMEM((sections, rows, rows), jnp.bfloat16),
            pltpu.VMEM((sections, padded, 2 * rows), jnp.float32),
            pltpu.VMEM((sections + 1, padded, rows), jnp.float32),
            pltpu.VMEM((sections, padded, rows), jnp.float32),
            pltpu.SemaphoreType.DMA((sections,)),
        ],
        compiler_params=pltpu.CompilerParams(vmem_limit_bytes=32 * 1024 * 1024),
        cost_estimate=pl.CostEstimate(
            flops=12 * sections * 16 * rows * rows,
            bytes_accessed=8 * sections * rows * rows,
            transcendentals=0,
        ),
        name="chain",
    )(position.reshape(1), coupling_all, vector_all, below_rows, above_rows)


def on_device(right_side, inverse_blocks, panels, receive_rows, below_update, above_solution):
    rhs = right_side.shape[0]
    block = inverse_blocks.shape[0]
    rows = panels.shape[0]
    front_count = lax.axis_size("front")
    front_pos = lax.axis_index("front")
    leaf_pos = lax.axis_index("leaf")
    share = rhs // front_count
    targets = receive_rows[0]

    planes = gather_along_z(right_side)
    picked = jnp.take(inverse_blocks, targets, axis=1)
    stacked = jnp.concatenate([panels, picked.T], axis=0)
    coupling = scatter_front(product(stacked, picked))
    coupling = gather_front(coupling).reshape(2 * rows, rows)
    coupling, planes = lax.optimization_barrier((coupling, planes))
    coupling_all = gather_leaf(coupling)

    section_side = gather_along_x(planes).transpose(1, 0, 2).reshape(rhs, front_count * block)
    local_forward = product_nt(section_side, inverse_blocks)
    vectors = scatter_front(product_nt(local_forward, stacked))
    vector_all = gather_leaf_small(vectors)

    below_rows = lax.dynamic_slice_in_dim(below_update, front_pos * share, share, 0)
    above_rows = lax.dynamic_slice_in_dim(above_solution, front_pos * share, share, 0)
    result = exchange(
        run_chain(leaf_pos, coupling_all, vector_all, below_rows, above_rows, front_count)
    )
    result = result.reshape(rhs, 3 * rows)
    update_share = rows // front_count
    sent_updates = lax.dynamic_slice_in_dim(
        result, 2 * rows + front_pos * update_share, update_share, 1
    )
    reduced = local_forward - product(result[:, : 2 * rows], stacked)
    spread = product(reduced, inverse_blocks)
    spread = spread.reshape(rhs, front_count, block).transpose(1, 0, 2)
    solution = jnp.sum(exchange(spread), axis=0)
    return (solution, sent_updates)


def solution(mesh):
    in_specs = (
        P(None, ("leaf", "front")),
        P(("leaf", "front"), None),
        P("leaf", "front"),
        P("leaf", None),
        P(),
        P(),
    )
    out_specs = (P(None, ("leaf", "front")), P(None, ("leaf", "front")))
    return jax.shard_map(
        on_device, mesh=mesh, in_specs=in_specs, out_specs=out_specs, check_vma=False
    )
```

time: 271 us -> 210 us (0.77)
  the two profiles are of different devices: /device:TPU:26 before, /device:TPU:2 now
where the time goes in v3:
time: 210 us
  waiting for transfers between devices  83.9 us (40%)
  blocking collectives  53 us (25%)
  starting transfers between devices  31.8 us (15%)
  between operations  14.3 us (7%)
  local copies, waits for them, and re-layouts  13 us (6%)
  Pallas kernels  7.12 us (3%)
  matrix products  5.57 us (3%)
    all_to_all x3, blocking collectives, exchange(): lax.all_to_all(blocks, axis, 0, 0, tiled=True, axis_index_groups=groups)  53 us
    all_to_all x4, waiting for transfers between devices, exchange(): lax.all_to_all(blocks, axis, 0, 0, tiled=True, axis_index_groups=groups)  50.5 us
    all_to_all x4, starting transfers between devices, exchange(): lax.all_to_all(blocks, axis, 0, 0, tiled=True, axis_index_groups=groups)  31.7 us
    all_gather x1, waiting for transfers between devices, gather_along_z(): wide = lax.all_gather(wide, 'front', axis=0, axis_index_groups=groups)  26 us
    all_gather x1, waiting for transfers between devices, gather_leaf(): return lax.all_gather(block, 'leaf', axis=0)  7.33 us
    pallas_call x1, Pallas kernels, run_chain(): pl.pallas_call(chain_kernel, out_shape=jax.ShapeDtypeStruct((targets, sha...  7.12 us
    unnamed x14, local copies, waits for them, and re-layouts  6.83 us
  transfers between devices with their start and end apart: 6, of which 5 were waited for; matrix products, arithmetic and copies ran while one was open for 4% of the time, Pallas kernels for 0%

profile of v3, /device:TPU:2, one launch (start us, length us, event | category | flops | bytes accessed | tf_op | source)
XLA Modules:
  0.0 209.5 jit_solution(4062761456051704311)
XLA Ops:
  7.2 1.9 copy.13
  9.2 0.7 gather_fusion
  10.0 1.4 fusion.4
  11.4 13.5 %all-to-all-start = ((f32[32,16,256]{2,1,0:T(8,128)}), f32[32,16,256]{2,1,0:T(8,128)S(1)}, u32[]{:S(2)}, u32[]{:S(2)}) async-start(f32[32,16,256]{2,1,0:T(8,128)} %bitcast.3), calls=%async_computation | async-start | bytes 1048576 | tf_op jit(solution)/shard_map/all_to_all | solution.py:24
  25.7 16.1 %all-to-all-done = f32[32,16,256]{2,1,0:T(8,128)S(1)} async-done(((f32[32,16,256]{2,1,0:T(8,128)}), f32[32,16,256]{2,1,0:T(8,128)S(1)}, u32[]{:S(2)}, u32[]{:S(2)}) %all-to-all-start) | async-done | bytes 524320 | tf_op jit(solution)/shard_map/all_to_all | solution.py:24
  41.8 0.9 broadcast_in_dim.18
  42.7 5.6 %all-to-all-start.1 = ((f32[32,16,256]{2,1,0:T(8,128)}), f32[32,16,256]{2,1,0:T(8,128)S(1)}, u32[]{:S(2)}, u32[]{:S(2)}) async-start(f32[32,16,256]{2,1,0:T(8,128)} %broadcast_in_dim.18), calls=%async_computation.1 | async-start | bytes 1048576 | tf_op jit(solution)/shard_map/all_to_all | solution.py:24
  48.3 26.0 %all-gather.5.cloned.1.call-done = f32[2048,128]{1,0:T(8,128)} async-done(((f32[256,128]{1,0:T(8,128)}), f32[2048,128]{1,0:T(8,128)}) %all-gather.5.cloned.1.call-update) | async-done | bytes 1048592 | tf_op jit(solution)/shard_map/all_gather | solution.py:53
  74.3 1.0 slice.10
  75.3 0.8 copy-done.2
  76.3 17.2 %all_to_all.35 = f32[4,8,64,128]{3,2,1,0:T(8,128)S(1)} all-to-all(f32[4,8,64,128]{3,2,1,0:T(8,128)S(1)} %broadcast_in_dim.32), channel_id=1, replica_groups={{0,1,2,3},{4,5,6,7},{8,9,10,11},{12,13,14,15},{16,17,18,19},{20,21,22,2..., dimensions={0} | all-to-all | bytes 2097152 | tf_op jit(solution)/shard_map/all_to_all | solution.py:24
  93.5 2.3 %fusion = f32[64,128]{1,0:T(8,128)S(1)} fusion(f32[128,4096]{1,0:T(8,128)S(1)} %copy-done.1, f32[32,8,8,128]{3,2,1,0:T(8,128)S(1)} %bitcast.32), kind=kOutput, calls=%fused_computation.3 | convolution fusion | flops 402653184 | bytes 3178496 | tf_op jit(solution)/shard_map/dot_general | solution.py:18
  96.3 15.3 %all_to_all.36 = f32[32,2,512]{2,1,0:T(2,128)S(1)} all-to-all(f32[32,2,512]{2,1,0:T(2,128)S(1)} %reshape.70), channel_id=1, replica_groups=mesh['leaf'=16,'front'=32] {'front'}, dimensions={0} | all-to-all | bytes 262144 | tf_op jit(solution)/shard_map/all_to_all | solution.py:24
  112.3 7.0 %all-to-all-start.4 = ((f32[16,2,512]{2,1,0:T(2,128)}), f32[16,2,512]{2,1,0:T(2,128)S(1)}, u32[]{:S(2)}, u32[]{:S(2)}) async-start(f32[16,2,512]{2,1,0:T(2,128)} %broadcast_in_dim.33), calls=%async_computation.4 | async-start | bytes 131072 | tf_op jit(solution)/shard_map/all_to_all | solution.py:24
  119.4 0.7 constant_dynamic-slice_fusion.1
  120.1 7.8 %all-to-all-done.4.vector_ref = f32[16,2,512]{2,1,0:T(2,128)S(1)} async-done(((f32[16,2,512]{2,1,0:T(2,128)}), f32[16,2,512]{2,1,0:T(2,128)S(1)}, u32[]{:S(2)}, u32[]{:S(2)}) %all-to-all-start.4) | async-done | bytes 65568 | tf_op jit(solution)/shard_map/all_to_all | solution.py:24
  127.9 7.3 %all-gather.7.cloned.1.call-done = f32[8192,256]{1,0:T(8,128)} async-done(((f32[512,256]{1,0:T(8,128)}), f32[8192,256]{1,0:T(8,128)}) %all-gather.7.cloned.1.call-update) | async-done | bytes 8388624 | tf_op jit(solution)/shard_map/all_gather | solution.py:42
  135.3 3.4 %copy-done = f32[8192,256]{1,0:T(8,128)S(1)} copy-done((f32[8192,256]{1,0:T(8,128)S(1)}, f32[8192,256]{1,0:T(8,128)}, u32[]{:S(2)}) %copy-start) | copy-done | bytes 8388632
  138.6 7.1 %chain.1 = f32[32,2,768]{2,1,0:T(2,128)S(1)} custom-call(s32[1]{0:T(128)} %bitcast.9.pos_ref, f32[16,512,256]{2,1,0:T(8,128)S(1)} %bitcast.31, f32[16,2,512]{2,1,0:T(2,128)S(1)} %all-to-all-done.4.vector_ref, f32[2,256]{1,0:T(2,128)S(1)} %get-tuple-element.7.below_ref, f32[2,256]{1,0:T(2,128)S(1)} %get-tuple-element.6.above_ref), custom_call_target="tpu_custom_call" | custom-call | flops 201326592 | bytes 8388608 | tf_op jit(solution)/shard_map/chain/pallas_call | solution.py:129
  145.8 20.5 %all_to_all.37 = f32[32,2,768]{2,1,0:T(2,128)S(1)} all-to-all(f32[32,2,768]{2,1,0:T(2,128)S(1)} %chain.1), channel_id=1, replica_groups=mesh['leaf'=16,'front'=32] {'front'}, dimensions={0} | all-to-all | bytes 393216 | tf_op jit(solution)/shard_map/all_to_all | solution.py:24
  166.7 1.2 convolution_bitcast_fusion
  167.9 1.1 copy.26
  169.0 5.7 %all-to-all-start.6 = ((f32[32,64,128]{2,1,0:T(8,128)}), f32[32,64,128]{2,1,0:T(8,128)S(1)}, u32[]{:S(2)}, u32[]{:S(2)}) async-start(f32[32,64,128]{2,1,0:T(8,128)} %bitcast.30), calls=%async_computation.6 | async-start | bytes 2097152 | tf_op jit(solution)/shard_map/all_to_all | solution.py:24
  175.5 26.6 %all-to-all-done.6 = f32[32,64,128]{2,1,0:T(8,128)S(1)} async-done(((f32[32,64,128]{2,1,0:T(8,128)}), f32[32,64,128]{2,1,0:T(8,128)S(1)}, u32[]{:S(2)}, u32[]{:S(2)}) %all-to-all-start.6) | async-done | bytes 1048608 | tf_op jit(solution)/shard_map/all_to_all | solution.py:24
  (32 shorter events, 4.1 us)
Async XLA Ops:
  7.2 2.0 copy-start.5
  7.2 2.9 %copy-start.3 = (f32[256,128]{1,0:T(8,128)S(1)}, f32[256,128]{1,0:T(8,128)}, u32[]{:S(2)}) copy-start(f32[256,128]{1,0:T(8,128)} %param.8) | copy-start | bytes 393220
  9.1 15.8 %copy-start.4 = (f32[64,128]{1,0:T(8,128)S(1)}, f32[64,128]{1,0:T(8,128)}, u32[]{:S(2)}) copy-start(f32[64,128]{1,0:T(8,128)} %param.6) | copy-start | bytes 98308
  11.4 30.3 %all-to-all-start = ((f32[32,16,256]{2,1,0:T(8,128)}), f32[32,16,256]{2,1,0:T(8,128)S(1)}, u32[]{:S(2)}, u32[]{:S(2)}) async-start(f32[32,16,256]{2,1,0:T(8,128)} %bitcast.3), calls=%async_computation | async-start | bytes 1048576 | tf_op jit(solution)/shard_map/all_to_all | solution.py:24
  24.9 49.4 %all-gather.5.cloned.1.call-start = ((), (), s32[]{:S(2)}) async-start(), calls=%async_computation.7 | async-start | bytes 1179648 | tf_op jit(solution)/shard_map/all_gather | solution.py:53
  42.7 32.6 %all-to-all-start.1 = ((f32[32,16,256]{2,1,0:T(8,128)}), f32[32,16,256]{2,1,0:T(8,128)S(1)}, u32[]{:S(2)}, u32[]{:S(2)}) async-start(f32[32,16,256]{2,1,0:T(8,128)} %broadcast_in_dim.18), calls=%async_computation.1 | async-start | bytes 1048576 | tf_op jit(solution)/shard_map/all_to_all | solution.py:24
  48.2 87.0 %all-gather.7.cloned.1.call-start = ((), (), s32[]{:S(2)}) async-start(), calls=%async_computation.8 | async-start | bytes 8912896 | tf_op jit(solution)/shard_map/all_gather | solution.py:42
  75.3 0.8 copy-start.2
  76.3 17.3 %copy-start.1 = (f32[128,4096]{1,0:T(8,128)S(1)}, f32[128,4096]{1,0:T(8,128)}, u32[]{:S(2)}) copy-start(f32[128,4096]{1,0:T(8,128)} %param.7) | copy-start | bytes 6291460
  112.3 15.6 %all-to-all-start.4 = ((f32[16,2,512]{2,1,0:T(2,128)}), f32[16,2,512]{2,1,0:T(2,128)S(1)}, u32[]{:S(2)}, u32[]{:S(2)}) async-start(f32[16,2,512]{2,1,0:T(2,128)} %broadcast_in_dim.33), calls=%async_computation.4 | async-start | bytes 131072 | tf_op jit(solution)/shard_map/all_to_all | solution.py:24
  135.3 3.4 %copy-start = (f32[8192,256]{1,0:T(8,128)S(1)}, f32[8192,256]{1,0:T(8,128)}, u32[]{:S(2)}) copy-start(f32[8192,256]{1,0:T(8,128)} %all-gather.7.cloned.1.call-done) | copy-start | bytes 25165828
  169.0 33.0 %all-to-all-start.6 = ((f32[32,64,128]{2,1,0:T(8,128)}), f32[32,64,128]{2,1,0:T(8,128)S(1)}, u32[]{:S(2)}, u32[]{:S(2)}) async-start(f32[32,64,128]{2,1,0:T(8,128)} %bitcast.30), calls=%async_computation.6 | async-start | bytes 2097152 | tf_op jit(solution)/shard_map/all_to_all | solution.py:24
Sparse Core Ops, SparseCore 0:
  27.8 46.4 all-gather.4
  76.4 58.7 all-gather.6

commit v4 on v3

v4 whole, which is shorter than its diff:
```python
import jax
import jax.numpy as jnp
from jax import lax
from jax.experimental import pallas as pl
from jax.experimental.pallas import tpu as pltpu
from jax.sharding import PartitionSpec as P

exact = lax.Precision.HIGHEST
x_chips = 4
padded = 8


def product(left, right):
    return jnp.dot(left, right, precision=exact, preferred_element_type=jnp.float32)


def product_nt(left, right):
    return lax.dot_general(
        left, right, (((1,), (1,)), ((), ())), precision=exact, preferred_element_type=jnp.float32
    )


def exchange(blocks, axis="front", groups=None):
    return lax.all_to_all(blocks, axis, 0, 0, tiled=True, axis_index_groups=groups)


def copies(block, count):
    return jnp.broadcast_to(block[None], (count, *block.shape))


def gather_front(block):
    return exchange(copies(block, lax.axis_size("front")))


def scatter_front(total):
    count = lax.axis_size("front")
    pieces = total.reshape(count, total.shape[0] // count, *total.shape[1:])
    return jnp.sum(exchange(pieces), axis=0)


def gather_leaf(block):
    return lax.all_gather(block, "leaf", axis=0)


def gather_leaf_small(block):
    return exchange(copies(block, lax.axis_size("leaf")), "leaf")


def pad_side(block):
    return jnp.concatenate([block, jnp.zeros((3 * block.shape[0], block.shape[1]), block.dtype)])


def gather_along_z(wide, rhs):
    count = lax.axis_size("front")
    groups = [list(range(x, count, x_chips)) for x in range(x_chips)]
    return lax.all_gather(wide, "front", axis=0, axis_index_groups=groups)[:, :rhs]


def gather_along_x(planes):
    count = lax.axis_size("front")
    groups = [list(range(first, first + x_chips)) for first in range(0, count, x_chips)]
    whole = exchange(copies(planes, x_chips), "front", groups)
    return whole.transpose(1, 0, 2, 3).reshape(count, *planes.shape[1:])


def split(value):
    head = value.astype(jnp.bfloat16)
    return head, (value - head.astype(jnp.float32)).astype(jnp.bfloat16)


def two_parts(value):
    head, tail = split(value)
    return jnp.concatenate([head.astype(jnp.float32), tail.astype(jnp.float32)]).astype(
        jnp.bfloat16
    )


def dot_parts(parts, head, tail, contract):
    dims = (((1,), (contract,)), ((), ()))
    both = lax.dot_general(parts, head, dims, preferred_element_type=jnp.float32)
    both += lax.dot_general(parts, tail, dims, preferred_element_type=jnp.float32)
    return both[:padded] + both[padded:]


def chain_kernel(
    pos_ref, coupling_ref, share_ref, low_ref, high_ref, low_vec_ref, high_vec_ref,
    below_ref, above_ref, out_ref, held, head, tail, vectors, into, above, sems,
):
    pairs = held.shape[0]
    share, rows = below_ref.shape

    def fetch(y):
        return pltpu.make_async_copy(coupling_ref.at[y], held.at[y], sems.at[y])

    for y in range(pairs):
        fetch(y).start()
    vectors[...] = jnp.zeros_like(vectors)
    into[0] = jnp.zeros_like(into[0])
    above[pairs - 1] = jnp.zeros_like(into[0])
    for y in range(pairs):
        vectors[y, :share, :] = share_ref[2 * y] + share_ref[2 * y + 1]
    vectors[pairs, :share, :] = low_vec_ref[...]
    vectors[pairs + 1, :share, :] = high_vec_ref[...]
    into[0, :share, :] = below_ref[...]
    above[pairs - 1, :share, :] = above_ref[...]

    low_head, low_tail = split(low_ref[:rows])
    high_head, high_tail = split(high_ref[...])
    incoming = into[0]
    for y in range(pairs):
        fetch(y).wait()
        block_head, block_tail = split(held[y])
        head[y] = block_head[:rows]
        tail[y] = block_tail[:rows]
        result = vectors[y] - dot_parts(two_parts(incoming), block_head, block_tail, 1)
        incoming = result[:, :rows]
        if y + 1 < pairs:
            into[y + 1] = incoming
        vectors[y] = result
    from_above = above[pairs - 1]
    for y in range(pairs - 1, 0, -1):
        taken = dot_parts(two_parts(from_above), head[y], tail[y], 0)
        from_above = vectors[y, :, rows:] - taken
        above[y - 1] = from_above

    chip = pos_ref[0]
    incoming = into[chip]
    from_above = above[chip]
    middle = vectors[pairs, :, :rows] - dot_parts(two_parts(incoming), low_head, low_tail, 1)
    upper = vectors[pairs + 1] - dot_parts(two_parts(middle), high_head, high_tail, 1)
    taken = dot_parts(two_parts(from_above), high_head[:rows], high_tail[:rows], 0)
    middle_above = upper[:, rows:] - taken
    is_upper = pos_ref[1] == 1
    kept = jnp.concatenate(
        [
            jnp.where(is_upper, from_above, middle_above),
            jnp.where(is_upper, middle, incoming),
            jnp.where(is_upper, upper[:, :rows], middle),
        ],
        axis=1,
    )[:share]
    for piece in range(out_ref.shape[0]):
        out_ref[piece] = kept


def run_chain(position, coupling_all, shares, low, high, low_vec, high_vec, below, above, targets):
    share, rows = below.shape
    pairs = coupling_all.shape[0]
    vmem = pl.BlockSpec(memory_space=pltpu.VMEM)
    return pl.pallas_call(
        chain_kernel,
        out_shape=jax.ShapeDtypeStruct((targets, share, 3 * rows), jnp.float32),
        in_specs=[pl.BlockSpec(memory_space=pltpu.SMEM), pl.BlockSpec(memory_space=pl.ANY)]
        + [vmem] * 7,
        out_specs=vmem,
        scratch_shapes=[
            pltpu.VMEM((pairs, 2 * rows, rows), jnp.float32),
            pltpu.VMEM((pairs, rows, rows), jnp.bfloat16),
            pltpu.VMEM((pairs, rows, rows), jnp.bfloat16),
            pltpu.VMEM((pairs + 2, padded, 2 * rows), jnp.float32),
            pltpu.VMEM((pairs, padded, rows), jnp.float32),
            pltpu.VMEM((pairs, padded, rows), jnp.float32),
            pltpu.SemaphoreType.DMA((pairs,)),
        ],
        compiler_params=pltpu.CompilerParams(vmem_limit_bytes=32 * 1024 * 1024),
        cost_estimate=pl.CostEstimate(
            flops=12 * pairs * 16 * rows * rows,
            bytes_accessed=8 * pairs * rows * rows,
            transcendentals=0,
        ),
        name="chain",
    )(position, coupling_all, shares, low, high, low_vec, high_vec, below, above)


def on_device(right_side, inverse_blocks, panels, receive_rows, below_update, above_solution):
    rhs = right_side.shape[0]
    block = inverse_blocks.shape[0]
    rows = panels.shape[0]
    front_count = lax.axis_size("front")
    front_pos = lax.axis_index("front")
    leaf_pos = lax.axis_index("leaf")
    leaf_count = lax.axis_size("leaf")
    is_upper = leaf_pos % 2 == 1
    share = rhs // front_count
    targets = receive_rows[0]

    wide = pad_side(right_side)
    wide, targets = lax.optimization_barrier((wide, targets))
    planes = gather_along_z(wide, rhs)
    picked = jnp.take(inverse_blocks, targets, axis=1)
    stacked = jnp.concatenate([panels, picked.T], axis=0)
    coupling = scatter_front(product(stacked, picked))
    coupling = gather_front(coupling).reshape(2 * rows, rows)

    swap = [(s, s ^ 1) for s in range(leaf_count)]
    mate = lax.ppermute(coupling, "leaf", swap)
    low = jnp.where(is_upper, mate, coupling)
    high = jnp.where(is_upper, coupling, mate)
    c_low, c_high, g_high = (low[:rows], high[:rows], high[rows:])
    lifted = product(g_high, c_low)
    c_pair = -product(c_high, c_low)
    g_pair = low[rows:] + product(c_low.T, lifted)
    pair_half = jnp.where(is_upper, g_pair, c_pair)
    pair_half, planes = lax.optimization_barrier((pair_half, planes))
    coupling_all = gather_leaf(pair_half).reshape(leaf_count // 2, 2 * rows, rows)

    section_side = gather_along_x(planes).transpose(1, 0, 2).reshape(rhs, front_count * block)
    local_forward = product_nt(section_side, inverse_blocks)
    vectors = scatter_front(product_nt(local_forward, stacked))
    mate_vectors = lax.ppermute(vectors, "leaf", swap)
    low_vec = jnp.where(is_upper, mate_vectors, vectors)
    high_vec = jnp.where(is_upper, vectors, mate_vectors)
    u_own, w_own = (vectors[:, :rows], vectors[:, rows:])
    u_moved = -product_nt(u_own, c_high)
    w_moved = product(jnp.where(is_upper, w_own, u_own), jnp.where(is_upper, -c_low, lifted))
    own_share = jnp.concatenate(
        [
            jnp.where(is_upper, u_own, u_moved),
            jnp.where(is_upper, w_moved, w_own + w_moved),
        ],
        axis=1,
    )
    shares = gather_leaf_small(own_share)

    below_rows = lax.dynamic_slice_in_dim(below_update, front_pos * share, share, 0)
    above_rows = lax.dynamic_slice_in_dim(above_solution, front_pos * share, share, 0)
    position = jnp.stack([leaf_pos // 2, leaf_pos % 2])
    result = exchange(
        run_chain(
            position, coupling_all, shares, low, high, low_vec, high_vec,
            below_rows, above_rows, front_count,
        )
    )
    result = result.reshape(rhs, 3 * rows)
    update_share = rows // front_count
    sent_updates = lax.dynamic_slice_in_dim(
        result, 2 * rows + front_pos * update_share, update_share, 1
    )
    reduced = local_forward - product(result[:, : 2 * rows], stacked)
    spread = product(reduced, inverse_blocks)
    spread = spread.reshape(rhs, front_count, block).transpose(1, 0, 2)
    solution = jnp.sum(exchange(spread), axis=0)
    return (solution, sent_updates)


def solution(mesh):
    in_specs = (
        P(None, ("leaf", "front")),
        P(("leaf", "front"), None),
        P("leaf", "front"),
        P("leaf", None),
        P(),
        P(),
    )
    out_specs = (P(None, ("leaf", "front")), P(None, ("leaf", "front")))
    return jax.shard_map(
        on_device, mesh=mesh, in_specs=in_specs, out_specs=out_specs, check_vma=False
    )
```

time: 210 us -> 202 us (0.962)
  waiting for transfers between devices: 83.9 us -> 63.4 us
  starting transfers between devices: 31.8 us -> 36.8 us
  blocking collectives: 53 us -> 57 us
  Pallas kernels: 7.12 us -> 4.52 us
  matrix products: 5.57 us -> 8.16 us
  other arithmetic: 0.91 us -> 3.37 us
    all_gather x1, waiting for transfers between devices: 26 us -> 4.85 us  [gather_along_z(): lax.all_gather(wide, 'front', axis=0, axis_index_groups=groups)[:, :rhs]]
    all_to_all x4, waiting for transfers between devices: 50.5 us -> 57.8 us  [exchange(): lax.all_to_all(blocks, axis, 0, 0, tiled=True, axis_index_groups=groups)]
    all_gather x1, waiting for transfers between devices: 7.33 us -> 0.01 us  [gather_leaf(): return lax.all_gather(block, 'leaf', axis=0)]
    all_to_all x3, blocking collectives: 53 us -> 57 us  [exchange(): lax.all_to_all(blocks, axis, 0, 0, tiled=True, axis_index_groups=groups)]
    ppermute x0 -> x2, starting transfers between devices: none -> 3.82 us  [the longest x1 1.91 us: on_device(): mate_vectors = lax.ppermute(vectors, 'leaf', swap)]
    pallas_call x1, Pallas kernels: 7.12 us -> 4.52 us  [run_chain(): pl.pallas_call(chain_kernel, out_shape=jax.ShapeDtypeStruct((targets, sha...]
    dot_general x3 -> x7, matrix products: 2.89 us -> 5.23 us  [product(): jnp.dot(left, right, precision=exact, preferred_element_type=jnp.float32)]
    unnamed x14 -> x24, local copies, waits for them, and re-layouts: 6.83 us -> 6.08 us
  transfers between devices with their start and end apart: 6 -> 8, of which waited for: 5 -> 5; matrix products, arithmetic and copies ran while one was open for 4% -> 5% of each run, Pallas kernels for 0% -> 0%
where the time goes in v4:
time: 202 us; the launch traced here: 201 us
  waiting for transfers between devices  63.4 us (31%)
  blocking collectives  57 us (28%)
  starting transfers between devices  36.8 us (18%)
  between operations  14.4 us (7%)
  local copies, waits for them, and re-layouts  13.6 us (7%)
  matrix products  8.16 us (4%)
  Pallas kernels  4.52 us (2%)
  other arithmetic  3.37 us (2%)
    all_to_all x4, waiting for transfers between devices, exchange(): lax.all_to_all(blocks, axis, 0, 0, tiled=True, axis_index_groups=groups)  57.8 us
    all_to_all x3, blocking collectives, exchange(): lax.all_to_all(blocks, axis, 0, 0, tiled=True, axis_index_groups=groups)  57 us
    all_to_all x4, starting transfers between devices, exchange(): lax.all_to_all(blocks, axis, 0, 0, tiled=True, axis_index_groups=groups)  32.9 us
    unnamed x24, local copies, waits for them, and re-layouts  6.08 us
    dot_general x7, matrix products, product(): jnp.dot(left, right, precision=exact, preferred_element_type=jnp.float32)  5.23 us
    all_gather x1, waiting for transfers between devices, gather_along_z(): lax.all_gather(wide, 'front', axis=0, axis_index_groups=groups)[:, :rhs]  4.85 us
    pallas_call x1, Pallas kernels, run_chain(): pl.pallas_call(chain_kernel, out_shape=jax.ShapeDtypeStruct((targets, sha...  4.52 us
  transfers between devices with their start and end apart: 8, of which 5 were waited for; matrix products, arithmetic and copies ran while one was open for 5% of the time, Pallas kernels for 0%

profile of v4, /device:TPU:2, one launch (start us, length us, event | category | flops | bytes accessed | tf_op | source)
XLA Modules:
  0.0 201.2 jit_solution(6222828632543367839)
XLA Ops:
  7.2 1.4 concatenate.9
  10.0 1.9 copy.13
  13.4 1.4 fusion.15
  14.8 13.5 %all-to-all-start = ((f32[32,16,256]{2,1,0:T(8,128)}), f32[32,16,256]{2,1,0:T(8,128)S(1)}, u32[]{:S(2)}, u32[]{:S(2)}) async-start(f32[32,16,256]{2,1,0:T(8,128)} %bitcast.1), calls=%async_computation | async-start | bytes 1048576 | tf_op jit(solution)/shard_map/all_to_all | solution.py:24
  29.0 16.0 %all-to-all-done = f32[32,16,256]{2,1,0:T(8,128)S(1)} async-done(((f32[32,16,256]{2,1,0:T(8,128)}), f32[32,16,256]{2,1,0:T(8,128)S(1)}, u32[]{:S(2)}, u32[]{:S(2)}) %all-to-all-start) | async-done | bytes 524320 | tf_op jit(solution)/shard_map/all_to_all | solution.py:24
  45.2 26.1 %all_to_all.35 = f32[32,16,256]{2,1,0:T(8,128)S(1)} all-to-all(f32[32,16,256]{2,1,0:T(8,128)S(1)} %broadcast_in_dim.34), channel_id=1, replica_groups=mesh['leaf'=16,'front'=32] {'front'}, dimensions={0} | all-to-all | bytes 1048576 | tf_op jit(solution)/shard_map/all_to_all | solution.py:24
  71.3 1.9 collective-permute-start
  73.2 4.9 %all-gather.5.cloned.1.call-done = f32[2048,128]{1,0:T(8,128)} async-done(((f32[256,128]{1,0:T(8,128)}), f32[2048,128]{1,0:T(8,128)}) %all-gather.5.cloned.1.call-update) | async-done | bytes 1048592 | tf_op jit(solution)/shard_map/all_gather | solution.py:56
  80.1 1.1 fusion.6
  81.4 15.7 %all_to_all.36 = f32[4,8,64,128]{3,2,1,0:T(8,128)S(1)} all-to-all(f32[4,8,64,128]{3,2,1,0:T(8,128)S(1)} %broadcast_in_dim.35), channel_id=1, replica_groups={{0,1,2,3},{4,5,6,7},{8,9,10,11},{12,13,14,15},{16,17,18,19},{20,21,22,2..., dimensions={0} | all-to-all | bytes 2097152 | tf_op jit(solution)/shard_map/all_to_all | solution.py:24
  97.2 2.3 %fusion.1 = f32[64,128]{1,0:T(8,128)S(1)} fusion(f32[128,4096]{1,0:T(8,128)S(1)} %copy-done.1, f32[32,8,8,128]{3,2,1,0:T(8,128)S(1)} %bitcast.33), kind=kOutput, calls=%fused_computation.6 | convolution fusion | flops 402653184 | bytes 3178496 | tf_op jit(solution)/shard_map/dot_general | solution.py:18
  101.2 6.6 %all-to-all-start.3 = ((f32[32,2,512]{2,1,0:T(2,128)}), f32[32,2,512]{2,1,0:T(2,128)}, u32[]{:S(2)}, u32[]{:S(2)}) async-start(f32[32,2,512]{2,1,0:T(2,128)} %reshape.41), calls=%async_computation.3 | async-start | bytes 262144 | tf_op jit(solution)/shard_map/all_to_all | solution.py:24
  108.7 8.1 %all-to-all-done.3 = f32[32,2,512]{2,1,0:T(2,128)} async-done(((f32[32,2,512]{2,1,0:T(2,128)}), f32[32,2,512]{2,1,0:T(2,128)}, u32[]{:S(2)}, u32[]{:S(2)}) %all-to-all-start.3) | async-done | bytes 131104 | tf_op jit(solution)/shard_map/all_to_all | solution.py:24
  116.8 1.0 reduce_sum.28
  117.7 1.9 collective-permute-start.1
  120.9 7.1 %all-to-all-start.4 = ((f32[16,2,512]{2,1,0:T(2,128)}), f32[16,2,512]{2,1,0:T(2,128)S(1)}, u32[]{:S(2)}, u32[]{:S(2)}) async-start(f32[16,2,512]{2,1,0:T(2,128)} %broadcast_in_dim.36), calls=%async_computation.4 | async-start | bytes 131072 | tf_op jit(solution)/shard_map/all_to_all | solution.py:24
  128.0 7.8 %all-to-all-done.4.share_ref = f32[16,2,512]{2,1,0:T(2,128)S(1)} async-done(((f32[16,2,512]{2,1,0:T(2,128)}), f32[16,2,512]{2,1,0:T(2,128)S(1)}, u32[]{:S(2)}, u32[]{:S(2)}) %all-to-all-start.4) | async-done | bytes 65568 | tf_op jit(solution)/shard_map/all_to_all | solution.py:24
  135.9 2.2 %copy-done = f32[4096,256]{1,0:T(8,128)S(1)} copy-done((f32[4096,256]{1,0:T(8,128)S(1)}, f32[4096,256]{1,0:T(8,128)}, u32[]{:S(2)}) %copy-start) | copy-done | bytes 4194328
  138.1 4.5 %chain.1 = f32[32,2,768]{2,1,0:T(2,128)S(1)} custom-call(s32[2]{0:T(128)S(1)} %pad_add_fusion.pos_ref, f32[8,512,256]{2,1,0:T(8,128)S(1)} %bitcast.32, f32[16,2,512]{2,1,0:T(2,128)S(1)} %all-to-all-done.4.share_ref, f32[512,256]{1,0:T(8,128)S(1)} %get-tuple-element.10.low_ref, f32[512,256]{1,0:T(8,128)S(1)} %get-tuple-element.11.high_ref, ...), custom_call_target="tpu_custom_call" | custom-call | flops 100663296 | bytes 4194304 | tf_op jit(solution)/shard_map/chain/pallas_call | solution.py:150
  142.6 15.2 %all_to_all.37 = f32[32,2,768]{2,1,0:T(2,128)S(1)} all-to-all(f32[32,2,768]{2,1,0:T(2,128)S(1)} %chain.1), channel_id=1, replica_groups=mesh['leaf'=16,'front'=32] {'front'}, dimensions={0} | all-to-all | bytes 393216 | tf_op jit(solution)/shard_map/all_to_all | solution.py:24
  158.3 1.2 convolution_bitcast_fusion
  159.5 1.1 copy.26
  160.6 5.7 %all-to-all-start.6 = ((f32[32,64,128]{2,1,0:T(8,128)}), f32[32,64,128]{2,1,0:T(8,128)S(1)}, u32[]{:S(2)}, u32[]{:S(2)}) async-start(f32[32,64,128]{2,1,0:T(8,128)} %bitcast.31), calls=%async_computation.6 | async-start | bytes 2097152 | tf_op jit(solution)/shard_map/all_to_all | solution.py:24
  167.8 25.9 %all-to-all-done.6 = f32[32,64,128]{2,1,0:T(8,128)S(1)} async-done(((f32[32,64,128]{2,1,0:T(8,128)}), f32[32,64,128]{2,1,0:T(8,128)S(1)}, u32[]{:S(2)}, u32[]{:S(2)}) %all-to-all-start.6) | async-done | bytes 1048608 | tf_op jit(solution)/shard_map/all_to_all | solution.py:24
  (55 shorter events, 12.3 us)
Async XLA Ops:
  10.0 3.5 %copy-start.5 = (f32[256,128]{1,0:T(8,128)S(1)}, f32[256,128]{1,0:T(8,128)}, u32[]{:S(2)}) copy-start(f32[256,128]{1,0:T(8,128)} %param.8) | copy-start | bytes 393220
  12.8 0.6 copy-start.2
  14.8 30.3 %all-to-all-start = ((f32[32,16,256]{2,1,0:T(8,128)}), f32[32,16,256]{2,1,0:T(8,128)S(1)}, u32[]{:S(2)}, u32[]{:S(2)}) async-start(f32[32,16,256]{2,1,0:T(8,128)} %bitcast.1), calls=%async_computation | async-start | bytes 1048576 | tf_op jit(solution)/shard_map/all_to_all | solution.py:24
  28.3 49.8 %all-gather.5.cloned.1.call-start = ((), (), s32[]{:S(2)}) async-start(), calls=%async_computation.7 | async-start | bytes 1179648 | tf_op jit(solution)/shard_map/all_gather | solution.py:56
  29.0 106.9 %all-gather.7.cloned.1.call-start = ((), (), s32[]{:S(2)}) async-start(), calls=%async_computation.8 | async-start | bytes 4456448 | tf_op jit(solution)/shard_map/all_gather | solution.py:42
  71.3 7.8 %collective-permute-start = (f32[512,256]{1,0:T(8,128)S(1)}, f32[512,256]{1,0:T(8,128)S(1)}, u32[]{:S(2)}, u32[]{:S(2)}) collective-permute-start(f32[512,256]{1,0:T(8,128)S(1)} %bitcast.34), channel_id=1, source_target_pairs={{0,32},{32,0},{64,96},{96,64},{128,160},{160,128},{192,224},{224,1... | collective-permute-start | bytes 1572872 | tf_op jit(solution)/shard_map/ppermute | solution.py:196
  81.4 15.8 %copy-start.1 = (f32[128,4096]{1,0:T(8,128)S(1)}, f32[128,4096]{1,0:T(8,128)}, u32[]{:S(2)}) copy-start(f32[128,4096]{1,0:T(8,128)} %param.7) | copy-start | bytes 6291460
  97.2 2.9 %copy-start.3 = (f32[256,128]{1,0:T(8,128)S(1)}, f32[256,128]{1,0:T(8,128)}, u32[]{:S(2)}) copy-start(f32[256,128]{1,0:T(8,128)} %copy-done.2) | copy-start | bytes 393220
  97.2 2.9 %copy-start.6 = (f32[256,128]{1,0:T(8,128)S(1)}, f32[256,128]{1,0:T(8,128)}, u32[]{:S(2)}) copy-start(f32[256,128]{1,0:T(8,128)} %param.8) | copy-start | bytes 393220
  99.5 0.6 copy-start.9
  101.2 15.6 %all-to-all-start.3 = ((f32[32,2,512]{2,1,0:T(2,128)}), f32[32,2,512]{2,1,0:T(2,128)}, u32[]{:S(2)}, u32[]{:S(2)}) async-start(f32[32,2,512]{2,1,0:T(2,128)} %reshape.41), calls=%async_computation.3 | async-start | bytes 262144 | tf_op jit(solution)/shard_map/all_to_all | solution.py:24
  117.7 10.2 %collective-permute-start.1 = (f32[2,512]{1,0:T(2,128)S(1)}, f32[2,512]{1,0:T(2,128)S(1)}, u32[]{:S(2)}, u32[]{:S(2)}) collective-permute-start(f32[2,512]{1,0:T(2,128)S(1)} %reduce_sum.28), channel_id=1, source_target_pairs={{0,32},{32,0},{64,96},{96,64},{128,160},{160,128},{192,224},{224,1... | collective-permute-start | bytes 12296 | tf_op jit(solution)/shard_map/ppermute | solution.py:210
  120.9 15.0 %all-to-all-start.4 = ((f32[16,2,512]{2,1,0:T(2,128)}), f32[16,2,512]{2,1,0:T(2,128)S(1)}, u32[]{:S(2)}, u32[]{:S(2)}) async-start(f32[16,2,512]{2,1,0:T(2,128)} %broadcast_in_dim.36), calls=%async_computation.4 | async-start | bytes 131072 | tf_op jit(solution)/shard_map/all_to_all | solution.py:24
  135.9 2.2 %copy-start = (f32[4096,256]{1,0:T(8,128)S(1)}, f32[4096,256]{1,0:T(8,128)}, u32[]{:S(2)}) copy-start(f32[4096,256]{1,0:T(8,128)} %all-gather.7.cloned.1.call-done) | copy-start | bytes 12582916
  138.1 19.9 %copy-start.4 = (f32[256,128]{1,0:T(8,128)S(1)}, f32[256,128]{1,0:T(8,128)}, u32[]{:S(2)}) copy-start(f32[256,128]{1,0:T(8,128)} %copy-done.2) | copy-start | bytes 393220
  138.1 19.9 %copy-start.7 = (f32[256,128]{1,0:T(8,128)S(1)}, f32[256,128]{1,0:T(8,128)}, u32[]{:S(2)}) copy-start(f32[256,128]{1,0:T(8,128)} %param.8) | copy-start | bytes 393220
  138.1 19.9 %copy-start.10 = (f32[64,128]{1,0:T(8,128)S(1)}, f32[64,128]{1,0:T(8,128)}, u32[]{:S(2)}) copy-start(f32[64,128]{1,0:T(8,128)} %copy-done.9) | copy-start | bytes 98308
  158.0 2.6 %copy-start.8 = (f32[64,768]{1,0:T(8,128)}, f32[64,768]{1,0:T(8,128)S(1)}, u32[]{:S(2)}) copy-start(f32[64,768]{1,0:T(8,128)S(1)} %reshape.42) | copy-start | bytes 589828
  160.6 33.1 %all-to-all-start.6 = ((f32[32,64,128]{2,1,0:T(8,128)}), f32[32,64,128]{2,1,0:T(8,128)S(1)}, u32[]{:S(2)}, u32[]{:S(2)}) async-start(f32[32,64,128]{2,1,0:T(8,128)} %bitcast.31), calls=%async_computation.6 | async-start | bytes 2097152 | tf_op jit(solution)/shard_map/all_to_all | solution.py:24
Sparse Core Ops, SparseCore 0:
  31.2 46.8 all-gather.4
  81.4 43.1 all-gather.6

commit v5 on v4

--- a/solution.py
+++ b/solution.py
@@ -1,3 +1,5 @@
+import functools
+
 import jax
 import jax.numpy as jnp
 from jax import lax
@@ -46,21 +48,26 @@
     return exchange(copies(block, lax.axis_size("leaf")), "leaf")
 
 
-def pad_side(block):
-    return jnp.concatenate([block, jnp.zeros((3 * block.shape[0], block.shape[1]), block.dtype)])
-
-
-def gather_along_z(wide, rhs):
-    count = lax.axis_size("front")
-    groups = [list(range(x, count, x_chips)) for x in range(x_chips)]
-    return lax.all_gather(wide, "front", axis=0, axis_index_groups=groups)[:, :rhs]
-
-
-def gather_along_x(planes):
+def gather_along_x(block):
     count = lax.axis_size("front")
     groups = [list(range(first, first + x_chips)) for first in range(0, count, x_chips)]
-    whole = exchange(copies(planes, x_chips), "front", groups)
-    return whole.transpose(1, 0, 2, 3).reshape(count, *planes.shape[1:])
+    return lax.all_gather(block, "front", axis=0, axis_index_groups=groups)
+
+
+def ring_along_z(block):
+    count = lax.axis_size("front")
+    turns = count // x_chips
+    later = [(f, (f + x_chips) % count) for f in range(count)]
+    earlier = [(target, source) for source, target in later]
+    pieces = [(0, block)]
+    behind = ahead = block
+    for step in range(1, turns // 2 + 1):
+        behind = lax.ppermute(behind, "front", later)
+        pieces.append((turns - step, behind))
+        if step < turns - step:
+            ahead = lax.ppermute(ahead, "front", earlier)
+            pieces.append((step, ahead))
+    return pieces
 
 
 def split(value):
@@ -80,6 +87,63 @@
     both = lax.dot_general(parts, head, dims, preferred_element_type=jnp.float32)
     both += lax.dot_general(parts, tail, dims, preferred_element_type=jnp.float32)
     return both[:padded] + both[padded:]
+
+
+def forward_kernel(offsets, pos_ref, inverse_ref, stacked_ref, *refs):
+    pieces, (forward_ref, vector_ref) = refs[:-2], refs[-2:]
+    planes, rhs, block = pieces[0].shape
+    width = planes * block
+    total = jnp.zeros((2 * rhs, 2 * block), jnp.float32)
+    for offset, piece in zip(offsets, pieces):
+        place = lax.rem(pos_ref[0] + offset, len(offsets))
+        columns = pl.ds(pl.multiple_of(place * width, width), width)
+        side = jnp.concatenate([piece[x] for x in range(planes)], axis=1)
+        total += lax.dot_general(
+            two_parts(side),
+            two_parts(inverse_ref[:, columns]),
+            (((1,), (1,)), ((), ())),
+            preferred_element_type=jnp.float32,
+        )
+    forward = fold(total, rhs, block)
+    forward_ref[...] = forward
+    vectors = lax.dot_general(
+        two_parts(forward),
+        two_parts(stacked_ref[...]),
+        (((1,), (1,)), ((), ())),
+        preferred_element_type=jnp.float32,
+    )
+    vectors = fold(vectors, rhs, stacked_ref.shape[0])
+    share = vector_ref.shape[1]
+    for piece in range(vector_ref.shape[0]):
+        vector_ref[piece] = vectors[piece * share : (piece + 1) * share]
+
+
+def fold(parts, rows, columns):
+    small = parts[rows:, columns:] + (parts[rows:, :columns] + parts[:rows, columns:])
+    return small + parts[:rows, :columns]
+
+
+def run_forward(z_pos, pieces, inverse_blocks, stacked, targets):
+    offsets = [offset for offset, _ in pieces]
+    rhs = pieces[0][1].shape[1]
+    block = inverse_blocks.shape[0]
+    vmem = pl.BlockSpec(memory_space=pltpu.VMEM)
+    return pl.pallas_call(
+        functools.partial(forward_kernel, offsets),
+        out_shape=(
+            jax.ShapeDtypeStruct((rhs, block), jnp.float32),
+            jax.ShapeDtypeStruct((targets, rhs // targets, stacked.shape[0]), jnp.float32),
+        ),
+        in_specs=[pl.BlockSpec(memory_space=pltpu.SMEM)] + [vmem] * (2 + len(pieces)),
+        out_specs=(vmem, vmem),
+        compiler_params=pltpu.CompilerParams(vmem_limit_bytes=32 * 1024 * 1024),
+        cost_estimate=pl.CostEstimate(
+            flops=8 * rhs * block * inverse_blocks.shape[1],
+            bytes_accessed=4 * inverse_blocks.size + 4 * rhs * inverse_blocks.shape[1],
+            transcendentals=0,
+        ),
+        name="forward",
+    )(z_pos.reshape(1), inverse_blocks, stacked, *[piece for _, piece in pieces])
 
 
 def chain_kernel(
@@ -184,9 +248,7 @@
     share = rhs // front_count
     targets = receive_rows[0]
 
-    wide = pad_side(right_side)
-    wide, targets = lax.optimization_barrier((wide, targets))
-    planes = gather_along_z(wide, rhs)
+    pieces = ring_along_z(gather_along_x(right_side))
     picked = jnp.take(inverse_blocks, targets, axis=1)
     stacked = jnp.concatenate([panels, picked.T], axis=0)
     coupling = scatter_front(product(stacked, picked))
@@ -201,12 +263,12 @@
     c_pair = -product(c_high, c_low)
     g_pair = low[rows:] + product(c_low.T, lifted)
     pair_half = jnp.where(is_upper, g_pair, c_pair)
-    pair_half, planes = lax.optimization_barrier((pair_half, planes))
     coupling_all = gather_leaf(pair_half).reshape(leaf_count // 2, 2 * rows, rows)
 
-    section_side = gather_along_x(planes).transpose(1, 0, 2).reshape(rhs, front_count * block)
-    local_forward = product_nt(section_side, inverse_blocks)
-    vectors = scatter_front(product_nt(local_forward, stacked))
+    local_forward, vectors = run_forward(
+        front_pos // x_chips, pieces, inverse_blocks, stacked, front_count
+    )
+    vectors = jnp.sum(exchange(vectors), axis=0)
     mate_vectors = lax.ppermute(vectors, "leaf", swap)
     low_vec = jnp.where(is_upper, mate_vectors, vectors)
     high_vec = jnp.where(is_upper, vectors, mate_vectors)

time: 202 us -> 219 us (1.084)
  blocking collectives: 57 us -> 78.6 us
  waiting for transfers between devices: 63.4 us -> 51.5 us
  starting transfers between devices: 36.8 us -> 45 us
  matrix products: 8.16 us -> 5.63 us
  Pallas kernels: 4.52 us -> 6.74 us
    ppermute x0 -> x7, starting transfers between devices: none -> 23 us  [the longest x3 14.8 us: ring_along_z(): ahead = lax.ppermute(ahead, 'front', earlier)]
    all_to_all x4 -> x3, waiting for transfers between devices: 57.8 us -> 41.8 us  [exchange(): lax.all_to_all(blocks, axis, 0, 0, tiled=True, axis_index_groups=groups)]
    all_to_all x4 -> x3, starting transfers between devices: 32.9 us -> 18.2 us  [exchange(): lax.all_to_all(blocks, axis, 0, 0, tiled=True, axis_index_groups=groups)]
    all_gather x0 -> x1, blocking collectives: none -> 12 us  [gather_along_x(): return lax.all_gather(block, 'front', axis=0, axis_index_groups=groups)]
    all_to_all x3, blocking collectives: 57 us -> 66.6 us  [exchange(): lax.all_to_all(blocks, axis, 0, 0, tiled=True, axis_index_groups=groups)]
    ppermute x0 -> x7, waiting for transfers between devices: none -> 7.91 us  [the longest x4 7.9 us: ring_along_z(): behind = lax.ppermute(behind, 'front', later)]
    all_gather x1 -> x0, waiting for transfers between devices: 4.85 us -> none  [gather_along_z(): lax.all_gather(wide, 'front', axis=0, axis_index_groups=groups)[:, :rhs]]
    unnamed x24 -> x30, local copies, waits for them, and re-layouts: 6.08 us -> 8.76 us
  transfers between devices with their start and end apart: 8 -> 13, of which waited for: 5 -> 8; matrix products, arithmetic and copies ran while one was open for 5% -> 3% of each run, Pallas kernels for 0% -> 1%
where the time goes in v5:
time: 219 us; the launch traced here: 218 us
  blocking collectives  78.6 us (36%)
  waiting for transfers between devices  51.5 us (24%)
  starting transfers between devices  45 us (21%)
  between operations  14.4 us (7%)
  local copies, waits for them, and re-layouts  13 us (6%)
  Pallas kernels  6.74 us (3%)
  matrix products  5.63 us (3%)
  other arithmetic  3.45 us (2%)
    all_to_all x3, blocking collectives, exchange(): lax.all_to_all(blocks, axis, 0, 0, tiled=True, axis_index_groups=groups)  66.6 us
    all_to_all x3, waiting for transfers between devices, exchange(): lax.all_to_all(blocks, axis, 0, 0, tiled=True, axis_index_groups=groups)  41.8 us
    all_to_all x3, starting transfers between devices, exchange(): lax.all_to_all(blocks, axis, 0, 0, tiled=True, axis_index_groups=groups)  18.2 us
    ppermute x3, starting transfers between devices, ring_along_z(): ahead = lax.ppermute(ahead, 'front', earlier)  14.8 us
    all_gather x1, blocking collectives, gather_along_x(): return lax.all_gather(block, 'front', axis=0, axis_index_groups=groups)  12 us
    unnamed x30, local copies, waits for them, and re-layouts  8.76 us
    ppermute x4, starting transfers between devices, ring_along_z(): behind = lax.ppermute(behind, 'front', later)  8.23 us
    ppermute x4, waiting for transfers between devices, ring_along_z(): behind = lax.ppermute(behind, 'front', later)  7.9 us
  transfers between devices with their start and end apart: 13, of which 8 were waited for; matrix products, arithmetic and copies ran while one was open for 3% of the time, Pallas kernels for 1%

profile of v5, /device:TPU:2, one launch (start us, length us, event | category | flops | bytes accessed | tf_op | source)
XLA Modules:
  0.0 218.4 jit_solution(6099226920179917587)
XLA Ops:
  8.6 1.9 copy.12
  12.1 30.1 %all_to_all.30 = f32[32,16,256]{2,1,0:T(8,128)S(1)} all-to-all(f32[32,16,256]{2,1,0:T(8,128)S(1)} %bitcast.29), channel_id=1, replica_groups=mesh['leaf'=16,'front'=32] {'front'}, dimensions={0} | all-to-all | bytes 1048576 | tf_op jit(solution)/shard_map/all_to_all | solution.py:26
  42.3 21.3 %all_to_all.31 = f32[32,16,256]{2,1,0:T(8,128)S(1)} all-to-all(f32[32,16,256]{2,1,0:T(8,128)S(1)} %broadcast_in_dim.24), channel_id=1, replica_groups=mesh['leaf'=16,'front'=32] {'front'}, dimensions={0} | all-to-all | bytes 1048576 | tf_op jit(solution)/shard_map/all_to_all | solution.py:26
  63.5 1.9 collective-permute-start.7
  70.3 12.0 %all-gather = f32[256,128]{1,0:T(8,128)S(1)} all-gather(f32[64,128]{1,0:T(8,128)S(1)} %copy-done.13), channel_id=2, replica_groups={{0,1,2,3},{4,5,6,7},{8,9,10,11},{12,13,14,15},{16,17,18,19},{20,21,22,2..., dimensions={0}, use_global_device_ids=true | all-gather | bytes 163840 | tf_op jit(solution)/shard_map/all_gather | solution.py:54
  82.2 2.5 %collective-permute-start = (f32[4,64,128]{2,1,0:T(8,128)S(1)}, f32[4,64,128]{2,1,0:T(8,128)S(1)}, u32[]{:S(2)}, u32[]{:S(2)}) collective-permute-start(f32[4,64,128]{2,1,0:T(8,128)S(1)} %bitcast.25), channel_id=1, source_target_pairs={{0,4},{1,5},{2,6},{3,7},{4,8},{5,9},{6,10},{7,11},{8,12},{9,13},{1... | collective-permute-start | bytes 393224 | tf_op jit(solution)/shard_map/ppermute | solution.py:65
  84.8 4.5 %collective-permute-start.1 = (f32[4,64,128]{2,1,0:T(8,128)S(1)}, f32[4,64,128]{2,1,0:T(8,128)S(1)}, u32[]{:S(2)}, u32[]{:S(2)}) collective-permute-start(f32[4,64,128]{2,1,0:T(8,128)S(1)} %bitcast.26), channel_id=1, source_target_pairs={{4,0},{5,1},{6,2},{7,3},{8,4},{9,5},{10,6},{11,7},{12,8},{13,9},{1... | collective-permute-start | bytes 393224 | tf_op jit(solution)/shard_map/ppermute | solution.py:68
  90.3 1.9 collective-permute-start.2
  92.2 5.1 %collective-permute-start.3 = (f32[4,64,128]{2,1,0:T(8,128)S(1)}, f32[4,64,128]{2,1,0:T(8,128)}, u32[]{:S(2)}, u32[]{:S(2)}) collective-permute-start(f32[4,64,128]{2,1,0:T(8,128)S(1)} %collective-permute-done.1.refs_2_), channel_id=1, source_target_pairs={{4,0},{5,1},{6,2},{7,3},{8,4},{9,5},{10,6},{11,7},{12,8},{13,9},{1... | collective-permute-start | bytes 393224 | tf_op jit(solution)/shard_map/ppermute | solution.py:68
  98.4 1.9 collective-permute-start.4
  100.9 5.1 %collective-permute-start.5 = (f32[4,64,128]{2,1,0:T(8,128)}, f32[4,64,128]{2,1,0:T(8,128)}, u32[]{:S(2)}, u32[]{:S(2)}) collective-permute-start(f32[4,64,128]{2,1,0:T(8,128)} %collective-permute-done.3.refs_4_), channel_id=1, source_target_pairs={{4,0},{5,1},{6,2},{7,3},{8,4},{9,5},{10,6},{11,7},{12,8},{13,9},{1... | collective-permute-start | bytes 393224 | tf_op jit(solution)/shard_map/ppermute | solution.py:68
  106.5 1.9 collective-permute-start.6
  109.5 5.4 %collective-permute-done.6.refs_7_ = f32[4,64,128]{2,1,0:T(8,128)} collective-permute-done((f32[4,64,128]{2,1,0:T(8,128)}, f32[4,64,128]{2,1,0:T(8,128)}, u32[]{:S(2)}, u32[]{:S(2)}) %collective-permute-start.6) | collective-permute-done | bytes 131104 | tf_op jit(solution)/shard_map/ppermute | solution.py:65
  115.8 2.2 %forward.1 = (f32[64,128]{1,0:T(8,128)S(1)}, f32[32,2,512]{2,1,0:T(2,128)S(1)}) custom-call(s32[1]{0:T(128)} %bitcast.pos_ref, f32[128,4096]{1,0:T(8,128)S(1)} %copy-done, f32[512,128]{1,0:T(8,128)S(1)} %pad_maximum_fusion.stacked_ref, f32[4,64,128]{2,1,0:T(8,128)S(1)} %bitcast.27, f32[4,64,128]{2,1,0:T(8,128)S(1)} %collective-permute-done.refs_1_, ...), custom_call_target="tpu_custom_call" | custom-call | flops 268435456 | bytes 3145728 | tf_op jit(solution)/shard_map/forward/pallas_call | solution.py:131
  119.3 5.3 %all-to-all-start.2 = ((f32[32,2,512]{2,1,0:T(2,128)}), f32[32,2,512]{2,1,0:T(2,128)S(1)}, u32[]{:S(2)}, u32[]{:S(2)}) async-start(f32[32,2,512]{2,1,0:T(2,128)} %copy-done.4), calls=%async_computation.2 | async-start | bytes 262144 | tf_op jit(solution)/shard_map/all_to_all | solution.py:26
  125.4 8.0 %all-to-all-done.2 = f32[32,2,512]{2,1,0:T(2,128)S(1)} async-done(((f32[32,2,512]{2,1,0:T(2,128)}), f32[32,2,512]{2,1,0:T(2,128)S(1)}, u32[]{:S(2)}, u32[]{:S(2)}) %all-to-all-start.2) | async-done | bytes 131104 | tf_op jit(solution)/shard_map/all_to_all | solution.py:26
  133.5 1.9 collective-permute-start.8
  137.6 7.2 %all-to-all-start.3 = ((f32[16,2,512]{2,1,0:T(2,128)}), f32[16,2,512]{2,1,0:T(2,128)S(1)}, u32[]{:S(2)}, u32[]{:S(2)}) async-start(f32[16,2,512]{2,1,0:T(2,128)} %broadcast_in_dim.25), calls=%async_computation.3 | async-start | bytes 131072 | tf_op jit(solution)/shard_map/all_to_all | solution.py:26
  144.8 7.8 %all-to-all-done.3.share_ref = f32[16,2,512]{2,1,0:T(2,128)S(1)} async-done(((f32[16,2,512]{2,1,0:T(2,128)}), f32[16,2,512]{2,1,0:T(2,128)S(1)}, u32[]{:S(2)}, u32[]{:S(2)}) %all-to-all-start.3) | async-done | bytes 65568 | tf_op jit(solution)/shard_map/all_to_all | solution.py:26
  152.7 2.2 %copy-done.1 = f32[4096,256]{1,0:T(8,128)S(1)} copy-done((f32[4096,256]{1,0:T(8,128)S(1)}, f32[4096,256]{1,0:T(8,128)}, u32[]{:S(2)}) %copy-start.1) | copy-done | bytes 4194328
  154.9 4.5 %chain.1 = f32[32,2,768]{2,1,0:T(2,128)S(1)} custom-call(s32[2]{0:T(128)S(1)} %pad_add_fusion.pos_ref, f32[8,512,256]{2,1,0:T(8,128)S(1)} %bitcast.24, f32[16,2,512]{2,1,0:T(2,128)S(1)} %all-to-all-done.3.share_ref, f32[512,256]{1,0:T(8,128)S(1)} %get-tuple-element.6.low_ref, f32[512,256]{1,0:T(8,128)S(1)} %get-tuple-element.7.high_ref, ...), custom_call_target="tpu_custom_call" | custom-call | flops 100663296 | bytes 4194304 | tf_op jit(solution)/shard_map/chain/pallas_call | solution.py:214
  159.4 15.2 %all_to_all.32 = f32[32,2,768]{2,1,0:T(2,128)S(1)} all-to-all(f32[32,2,768]{2,1,0:T(2,128)S(1)} %chain.1), channel_id=1, replica_groups=mesh['leaf'=16,'front'=32] {'front'}, dimensions={0} | all-to-all | bytes 393216 | tf_op jit(solution)/shard_map/all_to_all | solution.py:26
  177.8 5.7 %all-to-all-start.5 = ((f32[32,64,128]{2,1,0:T(8,128)}), f32[32,64,128]{2,1,0:T(8,128)S(1)}, u32[]{:S(2)}, u32[]{:S(2)}) async-start(f32[32,64,128]{2,1,0:T(8,128)} %bitcast.23), calls=%async_computation.5 | async-start | bytes 2097152 | tf_op jit(solution)/shard_map/all_to_all | solution.py:26
  185.0 25.9 %all-to-all-done.5 = f32[32,64,128]{2,1,0:T(8,128)S(1)} async-done(((f32[32,64,128]{2,1,0:T(8,128)}), f32[32,64,128]{2,1,0:T(8,128)S(1)}, u32[]{:S(2)}, u32[]{:S(2)}) %all-to-all-start.5) | async-done | bytes 1048608 | tf_op jit(solution)/shard_map/all_to_all | solution.py:26
  (66 shorter events, 22.3 us)
Async XLA Ops:
  7.2 145.5 %all-gather.4.cloned.1.call-start = ((), (), s32[]{:S(2)}) async-start(), calls=%async_computation.6 | async-start | bytes 4456448 | tf_op jit(solution)/shard_map/all_gather | solution.py:44
  8.6 2.8 %copy-start.10 = (f32[256,128]{1,0:T(8,128)S(1)}, f32[256,128]{1,0:T(8,128)}, u32[]{:S(2)}) copy-start(f32[256,128]{1,0:T(8,128)} %param.8) | copy-start | bytes 393220
  11.4 0.7 copy-start.8
  63.5 3.8 %collective-permute-start.7 = (f32[512,256]{1,0:T(8,128)S(1)}, f32[512,256]{1,0:T(8,128)S(1)}, u32[]{:S(2)}, u32[]{:S(2)}) collective-permute-start(f32[512,256]{1,0:T(8,128)S(1)} %bitcast.28), channel_id=1, source_target_pairs={{0,32},{32,0},{64,96},{96,64},{128,160},{160,128},{192,224},{224,1... | collective-permute-start | bytes 1572872 | tf_op jit(solution)/shard_map/ppermute | solution.py:258
  65.5 4.8 %copy-start.13 = (f32[64,128]{1,0:T(8,128)S(1)}, f32[64,128]{1,0:T(8,128)}, u32[]{:S(2)}) copy-start(f32[64,128]{1,0:T(8,128)} %param.6) | copy-start | bytes 98308
  67.4 47.5 %copy-start = (f32[128,4096]{1,0:T(8,128)S(1)}, f32[128,4096]{1,0:T(8,128)}, u32[]{:S(2)}) copy-start(f32[128,4096]{1,0:T(8,128)} %inverse_ref.1) | copy-start | bytes 6291460
  67.8 0.7 copy-start.7
  82.2 8.1 %collective-permute-start = (f32[4,64,128]{2,1,0:T(8,128)S(1)}, f32[4,64,128]{2,1,0:T(8,128)S(1)}, u32[]{:S(2)}, u32[]{:S(2)}) collective-permute-start(f32[4,64,128]{2,1,0:T(8,128)S(1)} %bitcast.25), channel_id=1, source_target_pairs={{0,4},{1,5},{2,6},{3,7},{4,8},{5,9},{6,10},{7,11},{8,12},{9,13},{1... | collective-permute-start | bytes 393224 | tf_op jit(solution)/shard_map/ppermute | solution.py:65
  84.8 7.5 %collective-permute-start.1 = (f32[4,64,128]{2,1,0:T(8,128)S(1)}, f32[4,64,128]{2,1,0:T(8,128)S(1)}, u32[]{:S(2)}, u32[]{:S(2)}) collective-permute-start(f32[4,64,128]{2,1,0:T(8,128)S(1)} %bitcast.26), channel_id=1, source_target_pairs={{4,0},{5,1},{6,2},{7,3},{8,4},{9,5},{10,6},{11,7},{12,8},{13,9},{1... | collective-permute-start | bytes 393224 | tf_op jit(solution)/shard_map/ppermute | solution.py:68
  90.3 8.1 %collective-permute-start.2 = (f32[4,64,128]{2,1,0:T(8,128)S(1)}, f32[4,64,128]{2,1,0:T(8,128)S(1)}, u32[]{:S(2)}, u32[]{:S(2)}) collective-permute-start(f32[4,64,128]{2,1,0:T(8,128)S(1)} %collective-permute-done.refs_1_), channel_id=1, source_target_pairs={{0,4},{1,5},{2,6},{3,7},{4,8},{5,9},{6,10},{7,11},{8,12},{9,13},{1... | collective-permute-start | bytes 393224 | tf_op jit(solution)/shard_map/ppermute | solution.py:65
  92.2 8.7 %collective-permute-start.3 = (f32[4,64,128]{2,1,0:T(8,128)S(1)}, f32[4,64,128]{2,1,0:T(8,128)}, u32[]{:S(2)}, u32[]{:S(2)}) collective-permute-start(f32[4,64,128]{2,1,0:T(8,128)S(1)} %collective-permute-done.1.refs_2_), channel_id=1, source_target_pairs={{4,0},{5,1},{6,2},{7,3},{8,4},{9,5},{10,6},{11,7},{12,8},{13,9},{1... | collective-permute-start | bytes 393224 | tf_op jit(solution)/shard_map/ppermute | solution.py:68
  98.4 8.2 %collective-permute-start.4 = (f32[4,64,128]{2,1,0:T(8,128)S(1)}, f32[4,64,128]{2,1,0:T(8,128)}, u32[]{:S(2)}, u32[]{:S(2)}) collective-permute-start(f32[4,64,128]{2,1,0:T(8,128)S(1)} %collective-permute-done.2.refs_3_), channel_id=1, source_target_pairs={{0,4},{1,5},{2,6},{3,7},{4,8},{5,9},{6,10},{7,11},{8,12},{9,13},{1... | collective-permute-start | bytes 393224 | tf_op jit(solution)/shard_map/ppermute | solution.py:65
  100.9 8.5 %collective-permute-start.5 = (f32[4,64,128]{2,1,0:T(8,128)}, f32[4,64,128]{2,1,0:T(8,128)}, u32[]{:S(2)}, u32[]{:S(2)}) collective-permute-start(f32[4,64,128]{2,1,0:T(8,128)} %collective-permute-done.3.refs_4_), channel_id=1, source_target_pairs={{4,0},{5,1},{6,2},{7,3},{8,4},{9,5},{10,6},{11,7},{12,8},{13,9},{1... | collective-permute-start | bytes 393224 | tf_op jit(solution)/shard_map/ppermute | solution.py:68
  106.5 8.4 %collective-permute-start.6 = (f32[4,64,128]{2,1,0:T(8,128)}, f32[4,64,128]{2,1,0:T(8,128)}, u32[]{:S(2)}, u32[]{:S(2)}) collective-permute-start(f32[4,64,128]{2,1,0:T(8,128)} %collective-permute-done.4.refs_5_), channel_id=1, source_target_pairs={{0,4},{1,5},{2,6},{3,7},{4,8},{5,9},{6,10},{7,11},{8,12},{9,13},{1... | collective-permute-start | bytes 393224 | tf_op jit(solution)/shard_map/ppermute | solution.py:65
  114.9 0.9 copy-start.3
  119.3 14.2 %all-to-all-start.2 = ((f32[32,2,512]{2,1,0:T(2,128)}), f32[32,2,512]{2,1,0:T(2,128)S(1)}, u32[]{:S(2)}, u32[]{:S(2)}) async-start(f32[32,2,512]{2,1,0:T(2,128)} %copy-done.4), calls=%async_computation.2 | async-start | bytes 262144 | tf_op jit(solution)/shard_map/all_to_all | solution.py:26
  133.5 11.3 %collective-permute-start.8 = (f32[2,512]{1,0:T(2,128)S(1)}, f32[2,512]{1,0:T(2,128)S(1)}, u32[]{:S(2)}, u32[]{:S(2)}) collective-permute-start(f32[2,512]{1,0:T(2,128)S(1)} %reduce_sum.28), channel_id=1, source_target_pairs={{0,32},{32,0},{64,96},{96,64},{128,160},{160,128},{192,224},{224,1... | collective-permute-start | bytes 12296 | tf_op jit(solution)/shard_map/ppermute | solution.py:272
  137.6 15.1 %all-to-all-start.3 = ((f32[16,2,512]{2,1,0:T(2,128)}), f32[16,2,512]{2,1,0:T(2,128)S(1)}, u32[]{:S(2)}, u32[]{:S(2)}) async-start(f32[16,2,512]{2,1,0:T(2,128)} %broadcast_in_dim.25), calls=%async_computation.3 | async-start | bytes 131072 | tf_op jit(solution)/shard_map/all_to_all | solution.py:26
  152.7 2.2 %copy-start.1 = (f32[4096,256]{1,0:T(8,128)S(1)}, f32[4096,256]{1,0:T(8,128)}, u32[]{:S(2)}) copy-start(f32[4096,256]{1,0:T(8,128)} %all-gather.4.cloned.1.call-done) | copy-start | bytes 12582916
  154.9 19.9 %copy-start.9 = (f32[256,128]{1,0:T(8,128)S(1)}, f32[256,128]{1,0:T(8,128)}, u32[]{:S(2)}) copy-start(f32[256,128]{1,0:T(8,128)} %copy-done.8) | copy-start | bytes 393220
  154.9 19.9 %copy-start.11 = (f32[256,128]{1,0:T(8,128)S(1)}, f32[256,128]{1,0:T(8,128)}, u32[]{:S(2)}) copy-start(f32[256,128]{1,0:T(8,128)} %param.8) | copy-start | bytes 393220
  154.9 20.6 %copy-start.6 = (f32[64,128]{1,0:T(8,128)S(1)}, f32[64,128]{1,0:T(8,128)}, u32[]{:S(2)}) copy-start(f32[64,128]{1,0:T(8,128)} %copy-done.5) | copy-start | bytes 98308
  174.8 0.7 copy-start.12
  177.8 33.1 %all-to-all-start.5 = ((f32[32,64,128]{2,1,0:T(8,128)}), f32[32,64,128]{2,1,0:T(8,128)S(1)}, u32[]{:S(2)}, u32[]{:S(2)}) async-start(f32[32,64,128]{2,1,0:T(8,128)} %bitcast.23), calls=%async_computation.5 | async-start | bytes 2097152 | tf_op jit(solution)/shard_map/all_to_all | solution.py:26
  (3 other events, 1.9 us)
Sparse Core Ops, SparseCore 0:
  70.4 41.2 all-gather.3

commit v6 on v5

--- a/solution.py
+++ b/solution.py
@@ -10,6 +10,7 @@
 exact = lax.Precision.HIGHEST
 x_chips = 4
 padded = 8
+early = 5
 
 
 def product(left, right):
@@ -59,15 +60,17 @@
     turns = count // x_chips
     later = [(f, (f + x_chips) % count) for f in range(count)]
     earlier = [(target, source) for source, target in later]
-    pieces = [(0, block)]
+    offsets, pieces = [0], [block]
     behind = ahead = block
     for step in range(1, turns // 2 + 1):
         behind = lax.ppermute(behind, "front", later)
-        pieces.append((turns - step, behind))
+        offsets.append(turns - step)
+        pieces.append(behind)
         if step < turns - step:
             ahead = lax.ppermute(ahead, "front", earlier)
-            pieces.append((step, ahead))
-    return pieces
+            offsets.append(step)
+            pieces.append(ahead)
+    return offsets, pieces
 
 
 def split(value):
@@ -123,9 +126,8 @@
     return small + parts[:rows, :columns]
 
 
-def run_forward(z_pos, pieces, inverse_blocks, stacked, targets):
-    offsets = [offset for offset, _ in pieces]
-    rhs = pieces[0][1].shape[1]
+def run_forward(z_pos, offsets, pieces, inverse_blocks, stacked, targets):
+    rhs = pieces[0].shape[1]
     block = inverse_blocks.shape[0]
     vmem = pl.BlockSpec(memory_space=pltpu.VMEM)
     return pl.pallas_call(
@@ -143,7 +145,7 @@
             transcendentals=0,
         ),
         name="forward",
-    )(z_pos.reshape(1), inverse_blocks, stacked, *[piece for _, piece in pieces])
+    )(z_pos.reshape(1), inverse_blocks, stacked, *pieces)
 
 
 def chain_kernel(
@@ -248,11 +250,14 @@
     share = rhs // front_count
     targets = receive_rows[0]
 
-    pieces = ring_along_z(gather_along_x(right_side))
+    plane = gather_along_x(right_side)
     picked = jnp.take(inverse_blocks, targets, axis=1)
     stacked = jnp.concatenate([panels, picked.T], axis=0)
     coupling = scatter_front(product(stacked, picked))
+    coupling, plane = lax.optimization_barrier((coupling, plane))
+    offsets, pieces = ring_along_z(plane)
     coupling = gather_front(coupling).reshape(2 * rows, rows)
+    coupling, *pieces[:early] = lax.optimization_barrier((coupling, *pieces[:early]))
 
     swap = [(s, s ^ 1) for s in range(leaf_count)]
     mate = lax.ppermute(coupling, "leaf", swap)
@@ -266,7 +271,7 @@
     coupling_all = gather_leaf(pair_half).reshape(leaf_count // 2, 2 * rows, rows)
 
     local_forward, vectors = run_forward(
-        front_pos // x_chips, pieces, inverse_blocks, stacked, front_count
+        front_pos // x_chips, offsets, pieces, inverse_blocks, stacked, front_count
     )
     vectors = jnp.sum(exchange(vectors), axis=0)
     mate_vectors = lax.ppermute(vectors, "leaf", swap)

time: 219 us -> 210 us (0.959)
  blocking collectives: 78.6 us -> 28.3 us
  starting transfers between devices: 45 us -> 67.1 us
  waiting for transfers between devices: 51.5 us -> 68 us
    all_to_all x3 -> x1, blocking collectives: 66.6 us -> 15.3 us  [exchange(): lax.all_to_all(blocks, axis, 0, 0, tiled=True, axis_index_groups=groups)]
    all_to_all x3 -> x5, starting transfers between devices: 18.2 us -> 41.9 us  [exchange(): lax.all_to_all(blocks, axis, 0, 0, tiled=True, axis_index_groups=groups)]
    ppermute x3, waiting for transfers between devices: 0.01 us -> 9.16 us  [ring_along_z(): ahead = lax.ppermute(ahead, 'front', earlier)]
    all_to_all x3 -> x5, waiting for transfers between devices: 41.8 us -> 45.5 us  [exchange(): lax.all_to_all(blocks, axis, 0, 0, tiled=True, axis_index_groups=groups)]
    ppermute x4, waiting for transfers between devices: 7.9 us -> 11.5 us  [ring_along_z(): behind = lax.ppermute(behind, 'front', later)]
  transfers between devices with their start and end apart: 13 -> 15, of which waited for: 8 -> 10; matrix products, arithmetic and copies ran while one was open for 3% -> 3% of each run, Pallas kernels for 1% -> 1%
where the time goes in v6:
time: 210 us; the launch traced here: 209 us
  waiting for transfers between devices  68 us (32%)
  starting transfers between devices  67.1 us (32%)
  blocking collectives  28.3 us (13%)
  local copies, waits for them, and re-layouts  14.4 us (7%)
  between operations  14.4 us (7%)
  Pallas kernels  6.74 us (3%)
  matrix products  6.44 us (3%)
  other arithmetic  3.45 us (2%)
    all_to_all x5, waiting for transfers between devices, exchange(): lax.all_to_all(blocks, axis, 0, 0, tiled=True, axis_index_groups=groups)  45.5 us
    all_to_all x5, starting transfers between devices, exchange(): lax.all_to_all(blocks, axis, 0, 0, tiled=True, axis_index_groups=groups)  41.9 us
    all_to_all x1, blocking collectives, exchange(): lax.all_to_all(blocks, axis, 0, 0, tiled=True, axis_index_groups=groups)  15.3 us
    ppermute x3, starting transfers between devices, ring_along_z(): ahead = lax.ppermute(ahead, 'front', earlier)  13.3 us
    all_gather x1, blocking collectives, gather_along_x(): return lax.all_gather(block, 'front', axis=0, axis_index_groups=groups)  13.1 us
    ppermute x4, waiting for transfers between devices, ring_along_z(): behind = lax.ppermute(behind, 'front', later)  11.5 us
    unnamed x30, local copies, waits for them, and re-layouts  9.39 us
    ppermute x3, waiting for transfers between devices, ring_along_z(): ahead = lax.ppermute(ahead, 'front', earlier)  9.16 us
  transfers between devices with their start and end apart: 15, of which 10 were waited for; matrix products, arithmetic and copies ran while one was open for 3% of the time, Pallas kernels for 1%

profile of v6, /device:TPU:2, one launch (start us, length us, event | category | flops | bytes accessed | tf_op | source)
XLA Modules:
  0.0 209.0 jit_solution(5430763202662110345)
XLA Ops:
  8.6 1.9 copy.12
  13.4 13.5 %all-to-all-start = ((f32[32,16,256]{2,1,0:T(8,128)}), f32[32,16,256]{2,1,0:T(8,128)S(1)}, u32[]{:S(2)}, u32[]{:S(2)}) async-start(f32[32,16,256]{2,1,0:T(8,128)} %bitcast.4), calls=%async_computation | async-start | bytes 1048576 | tf_op jit(solution)/shard_map/all_to_all | solution.py:27
  26.9 13.1 %all-gather = f32[256,128]{1,0:T(8,128)S(1)} all-gather(f32[64,128]{1,0:T(8,128)S(1)} %copy-done.13), channel_id=2, replica_groups={{0,1,2,3},{4,5,6,7},{8,9,10,11},{12,13,14,15},{16,17,18,19},{20,21,22,2..., dimensions={0}, use_global_device_ids=true | all-gather | bytes 163840 | tf_op jit(solution)/shard_map/all_gather | solution.py:55
  39.9 3.8 %all-to-all-done = f32[32,16,256]{2,1,0:T(8,128)S(1)} async-done(((f32[32,16,256]{2,1,0:T(8,128)}), f32[32,16,256]{2,1,0:T(8,128)S(1)}, u32[]{:S(2)}, u32[]{:S(2)}) %all-to-all-start) | async-done | bytes 524320 | tf_op jit(solution)/shard_map/all_to_all | solution.py:27
  44.6 5.6 %all-to-all-start.1 = ((f32[32,16,256]{2,1,0:T(8,128)}), f32[32,16,256]{2,1,0:T(8,128)S(1)}, u32[]{:S(2)}, u32[]{:S(2)}) async-start(f32[32,16,256]{2,1,0:T(8,128)} %broadcast_in_dim.24), calls=%async_computation.1 | async-start | bytes 1048576 | tf_op jit(solution)/shard_map/all_to_all | solution.py:27
  50.2 4.7 %collective-permute-start.1 = (f32[4,64,128]{2,1,0:T(8,128)S(1)}, f32[4,64,128]{2,1,0:T(8,128)S(1)}, u32[]{:S(2)}, u32[]{:S(2)}) collective-permute-start(f32[4,64,128]{2,1,0:T(8,128)S(1)} %bitcast.23), channel_id=1, source_target_pairs={{4,0},{5,1},{6,2},{7,3},{8,4},{9,5},{10,6},{11,7},{12,8},{13,9},{1... | collective-permute-start | bytes 393224 | tf_op jit(solution)/shard_map/ppermute | solution.py:70
  54.9 1.9 collective-permute-start
  56.8 8.2 %collective-permute-done.1.refs_2_ = f32[4,64,128]{2,1,0:T(8,128)S(1)} collective-permute-done((f32[4,64,128]{2,1,0:T(8,128)S(1)}, f32[4,64,128]{2,1,0:T(8,128)S(1)}, u32[]{:S(2)}, u32[]{:S(2)}) %collective-permute-start.1) | collective-permute-done | bytes 131104 | tf_op jit(solution)/shard_map/ppermute | solution.py:70
  65.0 3.5 %collective-permute-start.3 = (f32[4,64,128]{2,1,0:T(8,128)S(1)}, f32[4,64,128]{2,1,0:T(8,128)S(1)}, u32[]{:S(2)}, u32[]{:S(2)}) collective-permute-start(f32[4,64,128]{2,1,0:T(8,128)S(1)} %collective-permute-done.1.refs_2_), channel_id=1, source_target_pairs={{4,0},{5,1},{6,2},{7,3},{8,4},{9,5},{10,6},{11,7},{12,8},{13,9},{1... | collective-permute-start | bytes 393224 | tf_op jit(solution)/shard_map/ppermute | solution.py:70
  68.5 2.3 %collective-permute-start.2 = (f32[4,64,128]{2,1,0:T(8,128)S(1)}, f32[4,64,128]{2,1,0:T(8,128)}, u32[]{:S(2)}, u32[]{:S(2)}) collective-permute-start(f32[4,64,128]{2,1,0:T(8,128)S(1)} %collective-permute-done.refs_1_), channel_id=1, source_target_pairs={{0,4},{1,5},{2,6},{3,7},{4,8},{5,9},{6,10},{7,11},{8,12},{9,13},{1... | collective-permute-start | bytes 393224 | tf_op jit(solution)/shard_map/ppermute | solution.py:66
  72.5 4.2 %collective-permute-done.2.refs_3_ = f32[4,64,128]{2,1,0:T(8,128)} collective-permute-done((f32[4,64,128]{2,1,0:T(8,128)S(1)}, f32[4,64,128]{2,1,0:T(8,128)}, u32[]{:S(2)}, u32[]{:S(2)}) %collective-permute-start.2) | collective-permute-done | bytes 131104 | tf_op jit(solution)/shard_map/ppermute | solution.py:66
  83.4 1.9 collective-permute-start.4
  85.4 5.1 %collective-permute-start.5 = (f32[4,64,128]{2,1,0:T(8,128)}, f32[4,64,128]{2,1,0:T(8,128)}, u32[]{:S(2)}, u32[]{:S(2)}) collective-permute-start(f32[4,64,128]{2,1,0:T(8,128)} %copy-done.2), channel_id=1, source_target_pairs={{4,0},{5,1},{6,2},{7,3},{8,4},{9,5},{10,6},{11,7},{12,8},{13,9},{1... | collective-permute-start | bytes 393224 | tf_op jit(solution)/shard_map/ppermute | solution.py:70
  95.3 5.4 %collective-permute-done.6.refs_7_ = f32[4,64,128]{2,1,0:T(8,128)} collective-permute-done((f32[4,64,128]{2,1,0:T(8,128)}, f32[4,64,128]{2,1,0:T(8,128)}, u32[]{:S(2)}, u32[]{:S(2)}) %collective-permute-start.6) | collective-permute-done | bytes 131104 | tf_op jit(solution)/shard_map/ppermute | solution.py:66
  101.7 2.2 %forward.1 = (f32[64,128]{1,0:T(8,128)S(1)}, f32[32,2,512]{2,1,0:T(2,128)S(1)}) custom-call(s32[1]{0:T(128)} %bitcast.pos_ref, f32[128,4096]{1,0:T(8,128)S(1)} %copy-done, f32[512,128]{1,0:T(8,128)S(1)} %pad_maximum_fusion.stacked_ref, f32[4,64,128]{2,1,0:T(8,128)S(1)} %bitcast.25, f32[4,64,128]{2,1,0:T(8,128)S(1)} %collective-permute-done.refs_1_, ...), custom_call_target="tpu_custom_call" | custom-call | flops 268435456 | bytes 3145728 | tf_op jit(solution)/shard_map/forward/pallas_call | solution.py:133
  105.2 10.0 %all-to-all-start.2 = ((f32[32,2,512]{2,1,0:T(2,128)}), f32[32,2,512]{2,1,0:T(2,128)S(1)}, u32[]{:S(2)}, u32[]{:S(2)}) async-start(f32[32,2,512]{2,1,0:T(2,128)} %copy-done.4), calls=%async_computation.2 | async-start | bytes 262144 | tf_op jit(solution)/shard_map/all_to_all | solution.py:27
  115.9 8.0 %all-to-all-done.2 = f32[32,2,512]{2,1,0:T(2,128)S(1)} async-done(((f32[32,2,512]{2,1,0:T(2,128)}), f32[32,2,512]{2,1,0:T(2,128)S(1)}, u32[]{:S(2)}, u32[]{:S(2)}) %all-to-all-start.2) | async-done | bytes 131104 | tf_op jit(solution)/shard_map/all_to_all | solution.py:27
  128.1 7.2 %all-to-all-start.3 = ((f32[16,2,512]{2,1,0:T(2,128)}), f32[16,2,512]{2,1,0:T(2,128)S(1)}, u32[]{:S(2)}, u32[]{:S(2)}) async-start(f32[16,2,512]{2,1,0:T(2,128)} %broadcast_in_dim.25), calls=%async_computation.3 | async-start | bytes 131072 | tf_op jit(solution)/shard_map/all_to_all | solution.py:27
  135.4 7.8 %all-to-all-done.3.share_ref = f32[16,2,512]{2,1,0:T(2,128)S(1)} async-done(((f32[16,2,512]{2,1,0:T(2,128)}), f32[16,2,512]{2,1,0:T(2,128)S(1)}, u32[]{:S(2)}, u32[]{:S(2)}) %all-to-all-start.3) | async-done | bytes 65568 | tf_op jit(solution)/shard_map/all_to_all | solution.py:27
  143.2 2.2 %copy-done.1 = f32[4096,256]{1,0:T(8,128)S(1)} copy-done((f32[4096,256]{1,0:T(8,128)S(1)}, f32[4096,256]{1,0:T(8,128)}, u32[]{:S(2)}) %copy-start.1) | copy-done | bytes 4194328
  145.4 4.5 %chain.1 = f32[32,2,768]{2,1,0:T(2,128)S(1)} custom-call(s32[2]{0:T(128)S(1)} %pad_add_fusion.pos_ref, f32[8,512,256]{2,1,0:T(8,128)S(1)} %bitcast.22, f32[16,2,512]{2,1,0:T(2,128)S(1)} %all-to-all-done.3.share_ref, f32[512,256]{1,0:T(8,128)S(1)} %get-tuple-element.22.low_ref, f32[512,256]{1,0:T(8,128)S(1)} %get-tuple-element.23.high_ref, ...), custom_call_target="tpu_custom_call" | custom-call | flops 100663296 | bytes 4194304 | tf_op jit(solution)/shard_map/chain/pallas_call | solution.py:216
  149.9 15.3 %all_to_all.30 = f32[32,2,768]{2,1,0:T(2,128)S(1)} all-to-all(f32[32,2,768]{2,1,0:T(2,128)S(1)} %chain.1), channel_id=1, replica_groups=mesh['leaf'=16,'front'=32] {'front'}, dimensions={0} | all-to-all | bytes 393216 | tf_op jit(solution)/shard_map/all_to_all | solution.py:27
  168.4 5.7 %all-to-all-start.5 = ((f32[32,64,128]{2,1,0:T(8,128)}), f32[32,64,128]{2,1,0:T(8,128)S(1)}, u32[]{:S(2)}, u32[]{:S(2)}) async-start(f32[32,64,128]{2,1,0:T(8,128)} %bitcast.21), calls=%async_computation.5 | async-start | bytes 2097152 | tf_op jit(solution)/shard_map/all_to_all | solution.py:27
  175.6 25.9 %all-to-all-done.5 = f32[32,64,128]{2,1,0:T(8,128)S(1)} async-done(((f32[32,64,128]{2,1,0:T(8,128)}), f32[32,64,128]{2,1,0:T(8,128)S(1)}, u32[]{:S(2)}, u32[]{:S(2)}) %all-to-all-start.5) | async-done | bytes 1048608 | tf_op jit(solution)/shard_map/all_to_all | solution.py:27
  (68 shorter events, 30.7 us)
Async XLA Ops:
  8.5 3.5 %copy-start.10 = (f32[256,128]{1,0:T(8,128)S(1)}, f32[256,128]{1,0:T(8,128)}, u32[]{:S(2)}) copy-start(f32[256,128]{1,0:T(8,128)} %param.8) | copy-start | bytes 393220
  10.5 16.4 %copy-start.13 = (f32[64,128]{1,0:T(8,128)S(1)}, f32[64,128]{1,0:T(8,128)}, u32[]{:S(2)}) copy-start(f32[64,128]{1,0:T(8,128)} %param.6) | copy-start | bytes 98308
  13.4 30.3 %all-to-all-start = ((f32[32,16,256]{2,1,0:T(8,128)}), f32[32,16,256]{2,1,0:T(8,128)S(1)}, u32[]{:S(2)}, u32[]{:S(2)}) async-start(f32[32,16,256]{2,1,0:T(8,128)} %bitcast.4), calls=%async_computation | async-start | bytes 1048576 | tf_op jit(solution)/shard_map/all_to_all | solution.py:27
  44.6 32.1 %all-to-all-start.1 = ((f32[32,16,256]{2,1,0:T(8,128)}), f32[32,16,256]{2,1,0:T(8,128)S(1)}, u32[]{:S(2)}, u32[]{:S(2)}) async-start(f32[32,16,256]{2,1,0:T(8,128)} %broadcast_in_dim.24), calls=%async_computation.1 | async-start | bytes 1048576 | tf_op jit(solution)/shard_map/all_to_all | solution.py:27
  50.2 93.0 %all-gather.4.cloned.1.call-start = ((), (), s32[]{:S(2)}) async-start(), calls=%async_computation.6 | async-start | bytes 4456448 | tf_op jit(solution)/shard_map/all_gather | solution.py:45
  50.2 14.8 %collective-permute-start.1 = (f32[4,64,128]{2,1,0:T(8,128)S(1)}, f32[4,64,128]{2,1,0:T(8,128)S(1)}, u32[]{:S(2)}, u32[]{:S(2)}) collective-permute-start(f32[4,64,128]{2,1,0:T(8,128)S(1)} %bitcast.23), channel_id=1, source_target_pairs={{4,0},{5,1},{6,2},{7,3},{8,4},{9,5},{10,6},{11,7},{12,8},{13,9},{1... | collective-permute-start | bytes 393224 | tf_op jit(solution)/shard_map/ppermute | solution.py:70
  54.9 13.6 %collective-permute-start = (f32[4,64,128]{2,1,0:T(8,128)S(1)}, f32[4,64,128]{2,1,0:T(8,128)S(1)}, u32[]{:S(2)}, u32[]{:S(2)}) collective-permute-start(f32[4,64,128]{2,1,0:T(8,128)S(1)} %bitcast.24), channel_id=1, source_target_pairs={{0,4},{1,5},{2,6},{3,7},{4,8},{5,9},{6,10},{7,11},{8,12},{9,13},{1... | collective-permute-start | bytes 393224 | tf_op jit(solution)/shard_map/ppermute | solution.py:66
  65.0 6.8 %collective-permute-start.3 = (f32[4,64,128]{2,1,0:T(8,128)S(1)}, f32[4,64,128]{2,1,0:T(8,128)S(1)}, u32[]{:S(2)}, u32[]{:S(2)}) collective-permute-start(f32[4,64,128]{2,1,0:T(8,128)S(1)} %collective-permute-done.1.refs_2_), channel_id=1, source_target_pairs={{4,0},{5,1},{6,2},{7,3},{8,4},{9,5},{10,6},{11,7},{12,8},{13,9},{1... | collective-permute-start | bytes 393224 | tf_op jit(solution)/shard_map/ppermute | solution.py:70
  68.5 8.2 %collective-permute-start.2 = (f32[4,64,128]{2,1,0:T(8,128)S(1)}, f32[4,64,128]{2,1,0:T(8,128)}, u32[]{:S(2)}, u32[]{:S(2)}) collective-permute-start(f32[4,64,128]{2,1,0:T(8,128)S(1)} %collective-permute-done.refs_1_), channel_id=1, source_target_pairs={{0,4},{1,5},{2,6},{3,7},{4,8},{5,9},{6,10},{7,11},{8,12},{9,13},{1... | collective-permute-start | bytes 393224 | tf_op jit(solution)/shard_map/ppermute | solution.py:66
  76.7 3.8 %collective-permute-start.7 = (f32[512,256]{1,0:T(8,128)S(1)}, f32[512,256]{1,0:T(8,128)S(1)}, u32[]{:S(2)}, u32[]{:S(2)}) collective-permute-start(f32[512,256]{1,0:T(8,128)S(1)} %bitcast.26), channel_id=1, source_target_pairs={{0,32},{32,0},{64,96},{96,64},{128,160},{160,128},{192,224},{224,1... | collective-permute-start | bytes 1572872 | tf_op jit(solution)/shard_map/ppermute | solution.py:263
  80.6 20.2 %copy-start = (f32[128,4096]{1,0:T(8,128)S(1)}, f32[128,4096]{1,0:T(8,128)}, u32[]{:S(2)}) copy-start(f32[128,4096]{1,0:T(8,128)} %inverse_ref.1) | copy-start | bytes 6291460
  81.0 0.7 copy-start.7
  83.4 9.0 %collective-permute-start.4 = (f32[4,64,128]{2,1,0:T(8,128)}, f32[4,64,128]{2,1,0:T(8,128)}, u32[]{:S(2)}, u32[]{:S(2)}) collective-permute-start(f32[4,64,128]{2,1,0:T(8,128)} %collective-permute-done.2.refs_3_), channel_id=1, source_target_pairs={{0,4},{1,5},{2,6},{3,7},{4,8},{5,9},{6,10},{7,11},{8,12},{9,13},{1... | collective-permute-start | bytes 393224 | tf_op jit(solution)/shard_map/ppermute | solution.py:66
  85.4 10.0 %collective-permute-start.5 = (f32[4,64,128]{2,1,0:T(8,128)}, f32[4,64,128]{2,1,0:T(8,128)}, u32[]{:S(2)}, u32[]{:S(2)}) collective-permute-start(f32[4,64,128]{2,1,0:T(8,128)} %copy-done.2), channel_id=1, source_target_pairs={{4,0},{5,1},{6,2},{7,3},{8,4},{9,5},{10,6},{11,7},{12,8},{13,9},{1... | collective-permute-start | bytes 393224 | tf_op jit(solution)/shard_map/ppermute | solution.py:70
  92.4 8.4 %collective-permute-start.6 = (f32[4,64,128]{2,1,0:T(8,128)}, f32[4,64,128]{2,1,0:T(8,128)}, u32[]{:S(2)}, u32[]{:S(2)}) collective-permute-start(f32[4,64,128]{2,1,0:T(8,128)} %collective-permute-done.4.refs_5_), channel_id=1, source_target_pairs={{0,4},{1,5},{2,6},{3,7},{4,8},{5,9},{6,10},{7,11},{8,12},{9,13},{1... | collective-permute-start | bytes 393224 | tf_op jit(solution)/shard_map/ppermute | solution.py:66
  100.8 0.9 copy-start.3
  105.2 18.8 %all-to-all-start.2 = ((f32[32,2,512]{2,1,0:T(2,128)}), f32[32,2,512]{2,1,0:T(2,128)S(1)}, u32[]{:S(2)}, u32[]{:S(2)}) async-start(f32[32,2,512]{2,1,0:T(2,128)} %copy-done.4), calls=%async_computation.2 | async-start | bytes 262144 | tf_op jit(solution)/shard_map/all_to_all | solution.py:27
  124.0 11.3 %collective-permute-start.8 = (f32[2,512]{1,0:T(2,128)S(1)}, f32[2,512]{1,0:T(2,128)S(1)}, u32[]{:S(2)}, u32[]{:S(2)}) collective-permute-start(f32[2,512]{1,0:T(2,128)S(1)} %reduce_sum.28), channel_id=1, source_target_pairs={{0,32},{32,0},{64,96},{96,64},{128,160},{160,128},{192,224},{224,1... | collective-permute-start | bytes 12296 | tf_op jit(solution)/shard_map/ppermute | solution.py:277
  128.1 15.1 %all-to-all-start.3 = ((f32[16,2,512]{2,1,0:T(2,128)}), f32[16,2,512]{2,1,0:T(2,128)S(1)}, u32[]{:S(2)}, u32[]{:S(2)}) async-start(f32[16,2,512]{2,1,0:T(2,128)} %broadcast_in_dim.25), calls=%async_computation.3 | async-start | bytes 131072 | tf_op jit(solution)/shard_map/all_to_all | solution.py:27
  143.2 2.2 %copy-start.1 = (f32[4096,256]{1,0:T(8,128)S(1)}, f32[4096,256]{1,0:T(8,128)}, u32[]{:S(2)}) copy-start(f32[4096,256]{1,0:T(8,128)} %all-gather.4.cloned.1.call-done) | copy-start | bytes 12582916
  145.4 19.9 %copy-start.9 = (f32[256,128]{1,0:T(8,128)S(1)}, f32[256,128]{1,0:T(8,128)}, u32[]{:S(2)}) copy-start(f32[256,128]{1,0:T(8,128)} %copy-done.8) | copy-start | bytes 393220
  145.4 20.0 %copy-start.11 = (f32[256,128]{1,0:T(8,128)S(1)}, f32[256,128]{1,0:T(8,128)}, u32[]{:S(2)}) copy-start(f32[256,128]{1,0:T(8,128)} %param.8) | copy-start | bytes 393220
  145.4 20.6 %copy-start.6 = (f32[64,128]{1,0:T(8,128)S(1)}, f32[64,128]{1,0:T(8,128)}, u32[]{:S(2)}) copy-start(f32[64,128]{1,0:T(8,128)} %copy-done.5) | copy-start | bytes 98308
  168.4 33.1 %all-to-all-start.5 = ((f32[32,64,128]{2,1,0:T(8,128)}), f32[32,64,128]{2,1,0:T(8,128)S(1)}, u32[]{:S(2)}, u32[]{:S(2)}) async-start(f32[32,64,128]{2,1,0:T(8,128)} %bitcast.21), calls=%async_computation.5 | async-start | bytes 2097152 | tf_op jit(solution)/shard_map/all_to_all | solution.py:27
  (5 other events, 3.2 us)
Sparse Core Ops, SparseCore 0:
  83.5 45.6 all-gather.3

commit v7 on v5

--- a/solution.py
+++ b/solution.py
@@ -1,5 +1,3 @@
-import functools
-
 import jax
 import jax.numpy as jnp
 from jax import lax
@@ -34,12 +32,6 @@
     return exchange(copies(block, lax.axis_size("front")))
 
 
-def scatter_front(total):
-    count = lax.axis_size("front")
-    pieces = total.reshape(count, total.shape[0] // count, *total.shape[1:])
-    return jnp.sum(exchange(pieces), axis=0)
-
-
 def gather_leaf(block):
     return lax.all_gather(block, "leaf", axis=0)
 
@@ -51,23 +43,7 @@
 def gather_along_x(block):
     count = lax.axis_size("front")
     groups = [list(range(first, first + x_chips)) for first in range(0, count, x_chips)]
-    return lax.all_gather(block, "front", axis=0, axis_index_groups=groups)
-
-
-def ring_along_z(block):
-    count = lax.axis_size("front")
-    turns = count // x_chips
-    later = [(f, (f + x_chips) % count) for f in range(count)]
-    earlier = [(target, source) for source, target in later]
-    pieces = [(0, block)]
-    behind = ahead = block
-    for step in range(1, turns // 2 + 1):
-        behind = lax.ppermute(behind, "front", later)
-        pieces.append((turns - step, behind))
-        if step < turns - step:
-            ahead = lax.ppermute(ahead, "front", earlier)
-            pieces.append((step, ahead))
-    return pieces
+    return exchange(copies(block, x_chips), "front", groups)
 
 
 def split(value):
@@ -89,28 +65,37 @@
     return both[:padded] + both[padded:]
 
 
-def forward_kernel(offsets, pos_ref, inverse_ref, stacked_ref, *refs):
-    pieces, (forward_ref, vector_ref) = refs[:-2], refs[-2:]
-    planes, rhs, block = pieces[0].shape
-    width = planes * block
+def fold(parts, rows, columns):
+    small = parts[rows:, columns:] + (parts[rows:, :columns] + parts[:rows, columns:])
+    return small + parts[:rows, :columns]
+
+
+def two_columns(value):
+    head, tail = split(value)
+    return jnp.concatenate([head, tail], axis=1)
+
+
+def forward_kernel(side_ref, inverse_ref, stacked_ref, forward_ref, vector_ref):
+    chunks, blocks, chunk, block = side_ref.shape
+    rhs = chunks * chunk
+    group = 4
+    nt = (((1,), (1,)), ((), ()))
     total = jnp.zeros((2 * rhs, 2 * block), jnp.float32)
-    for offset, piece in zip(offsets, pieces):
-        place = lax.rem(pos_ref[0] + offset, len(offsets))
-        columns = pl.ds(pl.multiple_of(place * width, width), width)
-        side = jnp.concatenate([piece[x] for x in range(planes)], axis=1)
+    for first in range(0, blocks, group):
+        side = jnp.concatenate(
+            [
+                jnp.concatenate([side_ref[c, first + j] for j in range(group)], axis=1)
+                for c in range(chunks)
+            ]
+        )
+        weights = two_parts(inverse_ref[:, first * block : (first + group) * block])
         total += lax.dot_general(
-            two_parts(side),
-            two_parts(inverse_ref[:, columns]),
-            (((1,), (1,)), ((), ())),
-            preferred_element_type=jnp.float32,
+            two_parts(side), weights, nt, preferred_element_type=jnp.float32
         )
     forward = fold(total, rhs, block)
     forward_ref[...] = forward
     vectors = lax.dot_general(
-        two_parts(forward),
-        two_parts(stacked_ref[...]),
-        (((1,), (1,)), ((), ())),
-        preferred_element_type=jnp.float32,
+        two_parts(forward), two_parts(stacked_ref[...]), nt, preferred_element_type=jnp.float32
     )
     vectors = fold(vectors, rhs, stacked_ref.shape[0])
     share = vector_ref.shape[1]
@@ -118,32 +103,63 @@
         vector_ref[piece] = vectors[piece * share : (piece + 1) * share]
 
 
-def fold(parts, rows, columns):
-    small = parts[rows:, columns:] + (parts[rows:, :columns] + parts[:rows, columns:])
-    return small + parts[:rows, :columns]
-
-
-def run_forward(z_pos, pieces, inverse_blocks, stacked, targets):
-    offsets = [offset for offset, _ in pieces]
-    rhs = pieces[0][1].shape[1]
+def run_forward(side, inverse_blocks, stacked, targets):
+    rhs = side.shape[0] * side.shape[2]
     block = inverse_blocks.shape[0]
     vmem = pl.BlockSpec(memory_space=pltpu.VMEM)
     return pl.pallas_call(
-        functools.partial(forward_kernel, offsets),
+        forward_kernel,
         out_shape=(
             jax.ShapeDtypeStruct((rhs, block), jnp.float32),
             jax.ShapeDtypeStruct((targets, rhs // targets, stacked.shape[0]), jnp.float32),
         ),
-        in_specs=[pl.BlockSpec(memory_space=pltpu.SMEM)] + [vmem] * (2 + len(pieces)),
+        in_specs=[vmem] * 3,
         out_specs=(vmem, vmem),
+        compiler_params=pltpu.CompilerParams(vmem_limit_bytes=32 * 1024 * 1024),
+        cost_estimate=pl.CostEstimate(
+            flops=8 * rhs * block * inverse_blocks.shape[1],
+            bytes_accessed=4 * inverse_blocks.size + 4 * side.size,
+            transcendentals=0,
+        ),
+        name="forward",
+    )(side, inverse_blocks, stacked)
+
+
+def spread_kernel(result_ref, forward_ref, stacked_ref, inverse_ref, out_ref, held):
+    share = result_ref.shape[1]
+    rhs, block = forward_ref.shape
+    for piece in range(result_ref.shape[0]):
+        held[piece * share : (piece + 1) * share, :] = result_ref[piece, :, : held.shape[1]]
+    taken = jnp.dot(
+        two_parts(held[...]), two_columns(stacked_ref[...]), preferred_element_type=jnp.float32
+    )
+    reduced = two_parts(forward_ref[...] - fold(taken, rhs, block))
+    group = 2
+    for first in range(0, out_ref.shape[0], group):
+        weights = two_columns(inverse_ref[:, first * block : (first + group) * block])
+        parts = jnp.dot(reduced, weights, preferred_element_type=jnp.float32)
+        parts = fold(parts, rhs, group * block)
+        for j in range(group):
+            out_ref[first + j] = parts[:, j * block : (j + 1) * block]
+
+
+def run_spread(result, forward, stacked, inverse_blocks):
+    rhs, block = forward.shape
+    vmem = pl.BlockSpec(memory_space=pltpu.VMEM)
+    return pl.pallas_call(
+        spread_kernel,
+        out_shape=jax.ShapeDtypeStruct((inverse_blocks.shape[1] // block, rhs, block), jnp.float32),
+        in_specs=[vmem] * 4,
+        out_specs=vmem,
+        scratch_shapes=[pltpu.VMEM((rhs, stacked.shape[0]), jnp.float32)],
         compiler_params=pltpu.CompilerParams(vmem_limit_bytes=32 * 1024 * 1024),
         cost_estimate=pl.CostEstimate(
             flops=8 * rhs * block * inverse_blocks.shape[1],
             bytes_accessed=4 * inverse_blocks.size + 4 * rhs * inverse_blocks.shape[1],
             transcendentals=0,
         ),
-        name="forward",
-    )(z_pos.reshape(1), inverse_blocks, stacked, *[piece for _, piece in pieces])
+        name="spread",
+    )(result, forward, stacked, inverse_blocks)
 
 
 def chain_kernel(
@@ -214,7 +230,7 @@
     return pl.pallas_call(
         chain_kernel,
         out_shape=jax.ShapeDtypeStruct((targets, share, 3 * rows), jnp.float32),
-        in_specs=[pl.BlockSpec(memory_space=pltpu.SMEM), pl.BlockSpec(memory_space=pl.ANY)]
+        in_specs=[pl.BlockSpec(memory_space=pltpu.SMEM), pl.BlockSpec(memory_space=pltpu.HBM)]
         + [vmem] * 7,
         out_specs=vmem,
         scratch_shapes=[
@@ -248,10 +264,15 @@
     share = rhs // front_count
     targets = receive_rows[0]
 
-    pieces = ring_along_z(gather_along_x(right_side))
+    chunk = rhs // x_chips
+    slice_rows = 2 * rows // front_count
     picked = jnp.take(inverse_blocks, targets, axis=1)
     stacked = jnp.concatenate([panels, picked.T], axis=0)
-    coupling = scatter_front(product(stacked, picked))
+    own_coupling = product(stacked, picked).reshape(front_count, slice_rows, rows)
+    own_chunks = jnp.tile(right_side.reshape(x_chips, chunk, block), (front_count // x_chips, 1, 1))
+    arrived = exchange(jnp.concatenate([own_coupling, own_chunks], axis=2))
+    coupling = jnp.sum(arrived[:, :, :rows], axis=0)
+    side_chunk = arrived[:, :, rows:]
     coupling = gather_front(coupling).reshape(2 * rows, rows)
 
     swap = [(s, s ^ 1) for s in range(leaf_count)]
@@ -263,10 +284,11 @@
     c_pair = -product(c_high, c_low)
     g_pair = low[rows:] + product(c_low.T, lifted)
     pair_half = jnp.where(is_upper, g_pair, c_pair)
+    pair_half, side_chunk = lax.optimization_barrier((pair_half, side_chunk))
     coupling_all = gather_leaf(pair_half).reshape(leaf_count // 2, 2 * rows, rows)
 
     local_forward, vectors = run_forward(
-        front_pos // x_chips, pieces, inverse_blocks, stacked, front_count
+        gather_along_x(side_chunk), inverse_blocks, stacked, front_count
     )
     vectors = jnp.sum(exchange(vectors), axis=0)
     mate_vectors = lax.ppermute(vectors, "leaf", swap)
@@ -293,15 +315,11 @@
             below_rows, above_rows, front_count,
         )
     )
-    result = result.reshape(rhs, 3 * rows)
+    spread = run_spread(result, local_forward, stacked, inverse_blocks)
+    solution = jnp.sum(exchange(spread), axis=0)
     update_share = rows // front_count
-    sent_updates = lax.dynamic_slice_in_dim(
-        result, 2 * rows + front_pos * update_share, update_share, 1
-    )
-    reduced = local_forward - product(result[:, : 2 * rows], stacked)
-    spread = product(reduced, inverse_blocks)
-    spread = spread.reshape(rhs, front_count, block).transpose(1, 0, 2)
-    solution = jnp.sum(exchange(spread), axis=0)
+    updates = result[:, :, 2 * rows :].reshape(rhs, rows)
+    sent_updates = lax.dynamic_slice_in_dim(updates, front_pos * update_share, update_share, 1)
     return (solution, sent_updates)
 
 

time: 219 us -> 198 us (0.904)
  starting transfers between devices: 45 us -> 27.8 us
  blocking collectives: 78.6 us -> 72 us
  waiting for transfers between devices: 51.5 us -> 57.8 us
  local copies, waits for them, and re-layouts: 13 us -> 8.23 us
  Pallas kernels: 6.74 us -> 9.5 us
    ppermute x7 -> x0, starting transfers between devices: 23 us -> none  [the longest x3 14.8 us: ring_along_z(): ahead = lax.ppermute(ahead, 'front', earlier)]
    all_to_all x3 -> x4, waiting for transfers between devices: 41.8 us -> 56 us  [exchange(): lax.all_to_all(blocks, axis, 0, 0, tiled=True, axis_index_groups=groups)]
    all_gather x1 -> x0, blocking collectives: 12 us -> none  [gather_along_x(): return lax.all_gather(block, 'front', axis=0, axis_index_groups=groups)]
    ppermute x7 -> x0, waiting for transfers between devices: 7.91 us -> none  [the longest x4 7.9 us: ring_along_z(): behind = lax.ppermute(behind, 'front', later)]
    all_to_all x3 -> x4, starting transfers between devices: 18.2 us -> 24 us  [exchange(): lax.all_to_all(blocks, axis, 0, 0, tiled=True, axis_index_groups=groups)]
    all_to_all x3, blocking collectives: 66.6 us -> 72 us  [exchange(): lax.all_to_all(blocks, axis, 0, 0, tiled=True, axis_index_groups=groups)]
    unnamed x30 -> x16, local copies, waits for them, and re-layouts: 8.76 us -> 4.82 us
    pallas_call x1 -> x2, Pallas kernels: 2.23 us -> 4.98 us  [the longest x1 3.05 us: run_forward(): pl.pallas_call(forward_kernel, out_shape=(jax.ShapeDtypeStruct((rhs, bloc...]
  transfers between devices with their start and end apart: 13 -> 7, of which waited for: 8 -> 5; matrix products, arithmetic and copies ran while one was open for 3% -> 3% of each run, Pallas kernels for 1% -> 2%
where the time goes in v7:
time: 198 us; the launch traced here: 197 us
  blocking collectives  72 us (36%)
  waiting for transfers between devices  57.8 us (29%)
  starting transfers between devices  27.8 us (14%)
  between operations  14.3 us (7%)
  Pallas kernels  9.5 us (5%)
  local copies, waits for them, and re-layouts  8.23 us (4%)
  matrix products  4.12 us (2%)
  other arithmetic  2.99 us (2%)
    all_to_all x3, blocking collectives, exchange(): lax.all_to_all(blocks, axis, 0, 0, tiled=True, axis_index_groups=groups)  72 us
    all_to_all x4, waiting for transfers between devices, exchange(): lax.all_to_all(blocks, axis, 0, 0, tiled=True, axis_index_groups=groups)  56 us
    all_to_all x4, starting transfers between devices, exchange(): lax.all_to_all(blocks, axis, 0, 0, tiled=True, axis_index_groups=groups)  24 us
    unnamed x16, local copies, waits for them, and re-layouts  4.82 us
    pallas_call x1, Pallas kernels, run_chain(): pl.pallas_call(chain_kernel, out_shape=jax.ShapeDtypeStruct((targets, sha...  4.52 us
  transfers between devices with their start and end apart: 7, of which 5 were waited for; matrix products, arithmetic and copies ran while one was open for 3% of the time, Pallas kernels for 2%

profile of v7, /device:TPU:2, one launch (start us, length us, event | category | flops | bytes accessed | tf_op | source)
XLA Modules:
  0.0 196.8 jit_solution(17595659220570863996)
XLA Ops:
  7.2 1.9 copy.10
  10.8 35.7 %all_to_all.35 = f32[32,16,384]{2,1,0:T(8,128)S(1)} all-to-all(f32[32,16,384]{2,1,0:T(8,128)S(1)} %pad_maximum_fusion), channel_id=1, replica_groups=mesh['leaf'=16,'front'=32] {'front'}, dimensions={0} | all-to-all | bytes 1572864 | tf_op jit(solution)/shard_map/all_to_all | solution.py:24
  46.6 21.0 %all_to_all.36 = f32[32,16,256]{2,1,0:T(8,128)S(1)} all-to-all(f32[32,16,256]{2,1,0:T(8,128)S(1)} %broadcast_in_dim.30), channel_id=1, replica_groups=mesh['leaf'=16,'front'=32] {'front'}, dimensions={0} | all-to-all | bytes 1048576 | tf_op jit(solution)/shard_map/all_to_all | solution.py:24
  67.6 1.9 collective-permute-start
  69.6 1.8 collective-permute-done
  72.5 1.1 fusion.3
  73.6 1.1 broadcast_in_dim.31
  74.7 5.5 %all-to-all-start.2 = ((f32[4,32,16,128]{3,2,1,0:T(8,128)}), f32[4,32,16,128]{3,2,1,0:T(8,128)}, u32[]{:S(2)}, u32[]{:S(2)}) async-start(f32[4,32,16,128]{3,2,1,0:T(8,128)} %broadcast_in_dim.31), calls=%async_computation.2 | async-start | bytes 2097152 | tf_op jit(solution)/shard_map/all_to_all | solution.py:24
  80.2 0.9 pad_maximum_fusion.1.stacked_ref
  81.1 13.4 %all-to-all-done.2.side_ref = f32[4,32,16,128]{3,2,1,0:T(8,128)} async-done(((f32[4,32,16,128]{3,2,1,0:T(8,128)}), f32[4,32,16,128]{3,2,1,0:T(8,128)}, u32[]{:S(2)}, u32[]{:S(2)}) %all-to-all-start.2) | async-done | bytes 1048608 | tf_op jit(solution)/shard_map/all_to_all | solution.py:24
  94.5 3.0 %forward.1 = (f32[64,128]{1,0:T(8,128)S(1)}, f32[32,2,512]{2,1,0:T(2,128)}) custom-call(f32[4,32,16,128]{3,2,1,0:T(8,128)} %all-to-all-done.2.side_ref, f32[128,4096]{1,0:T(8,128)S(1)} %copy-done, f32[512,128]{1,0:T(8,128)S(1)} %pad_maximum_fusion.1.stacked_ref), custom_call_target="tpu_custom_call" | custom-call | flops 268435456 | bytes 3145728 | tf_op jit(solution)/shard_map/forward/pallas_call | solution.py:110
  97.6 5.6 %all-to-all-start.3 = ((f32[32,2,512]{2,1,0:T(2,128)}), f32[32,2,512]{2,1,0:T(2,128)}, u32[]{:S(2)}, u32[]{:S(2)}) async-start(f32[32,2,512]{2,1,0:T(2,128)} %get-tuple-element.8), calls=%async_computation.3 | async-start | bytes 262144 | tf_op jit(solution)/shard_map/all_to_all | solution.py:24
  104.0 8.2 %all-to-all-done.3 = f32[32,2,512]{2,1,0:T(2,128)} async-done(((f32[32,2,512]{2,1,0:T(2,128)}), f32[32,2,512]{2,1,0:T(2,128)}, u32[]{:S(2)}, u32[]{:S(2)}) %all-to-all-start.3) | async-done | bytes 131104 | tf_op jit(solution)/shard_map/all_to_all | solution.py:24
  112.2 1.0 reduce_sum.28
  113.1 1.9 collective-permute-start.1
  115.3 1.2 add_select_fusion
  117.2 7.2 %all-to-all-start.4 = ((f32[16,2,512]{2,1,0:T(2,128)}), f32[16,2,512]{2,1,0:T(2,128)S(1)}, u32[]{:S(2)}, u32[]{:S(2)}) async-start(f32[16,2,512]{2,1,0:T(2,128)} %broadcast_in_dim.32), calls=%async_computation.4 | async-start | bytes 131072 | tf_op jit(solution)/shard_map/all_to_all | solution.py:24
  124.5 7.8 %all-to-all-done.4.share_ref = f32[16,2,512]{2,1,0:T(2,128)S(1)} async-done(((f32[16,2,512]{2,1,0:T(2,128)}), f32[16,2,512]{2,1,0:T(2,128)S(1)}, u32[]{:S(2)}, u32[]{:S(2)}) %all-to-all-start.4) | async-done | bytes 65568 | tf_op jit(solution)/shard_map/all_to_all | solution.py:24
  132.3 2.2 %copy-done.1 = f32[4096,256]{1,0:T(8,128)S(1)} copy-done((f32[4096,256]{1,0:T(8,128)S(1)}, f32[4096,256]{1,0:T(8,128)}, u32[]{:S(2)}) %copy-start.1) | copy-done | bytes 4194328
  134.5 4.5 %chain.1 = f32[32,2,768]{2,1,0:T(2,128)S(1)} custom-call(s32[2]{0:T(128)S(1)} %pad_add_fusion.pos_ref, f32[8,512,256]{2,1,0:T(8,128)S(1)} %bitcast.15, f32[16,2,512]{2,1,0:T(2,128)S(1)} %all-to-all-done.4.share_ref, f32[512,256]{1,0:T(8,128)S(1)} %get-tuple-element.10.low_ref, f32[512,256]{1,0:T(8,128)S(1)} %get-tuple-element.11.high_ref, ...), custom_call_target="tpu_custom_call" | custom-call | flops 100663296 | bytes 4194304 | tf_op jit(solution)/shard_map/chain/pallas_call | solution.py:230
  139.1 15.3 %all_to_all.37.result_ref = f32[32,2,768]{2,1,0:T(2,128)S(1)} all-to-all(f32[32,2,768]{2,1,0:T(2,128)S(1)} %chain.1), channel_id=1, replica_groups=mesh['leaf'=16,'front'=32] {'front'}, dimensions={0} | all-to-all | bytes 393216 | tf_op jit(solution)/shard_map/all_to_all | solution.py:24
  154.3 1.9 spread.1
  156.2 5.7 %all-to-all-start.6 = ((f32[32,64,128]{2,1,0:T(8,128)}), f32[32,64,128]{2,1,0:T(8,128)S(1)}, u32[]{:S(2)}, u32[]{:S(2)}) async-start(f32[32,64,128]{2,1,0:T(8,128)} %spread.1), calls=%async_computation.6 | async-start | bytes 2097152 | tf_op jit(solution)/shard_map/all_to_all | solution.py:24
  162.7 26.5 %all-to-all-done.6 = f32[32,64,128]{2,1,0:T(8,128)S(1)} async-done(((f32[32,64,128]{2,1,0:T(8,128)}), f32[32,64,128]{2,1,0:T(8,128)S(1)}, u32[]{:S(2)}, u32[]{:S(2)}) %all-to-all-start.6) | async-done | bytes 1048608 | tf_op jit(solution)/shard_map/all_to_all | solution.py:24
  (43 shorter events, 6.0 us)
Async XLA Ops:
  7.2 2.0 %copy-start.6 = (s32[1,256]{1,0:T(1,128)S(1)}, s32[1,256]{1,0:T(1,128)}, u32[]{:S(2)}) copy-start(s32[1,256]{1,0:T(1,128)} %param.9) | copy-start | bytes 3076
  7.2 2.9 %copy-start.4 = (f32[256,128]{1,0:T(8,128)S(1)}, f32[256,128]{1,0:T(8,128)}, u32[]{:S(2)}) copy-start(f32[256,128]{1,0:T(8,128)} %param.8) | copy-start | bytes 393220
  7.2 125.1 %all-gather.3.cloned.1.call-start = ((), (), s32[]{:S(2)}) async-start(), calls=%async_computation.7 | async-start | bytes 4456448 | tf_op jit(solution)/shard_map/all_gather | solution.py:36
  9.2 1.5 copy-start.5
  46.5 23.1 %copy-start.2 = (f32[32,16,384]{2,1,0:T(8,128)}, f32[32,16,384]{2,1,0:T(8,128)S(1)}, u32[]{:S(2)}) copy-start(f32[32,16,384]{2,1,0:T(8,128)S(1)} %all_to_all.35) | copy-start | bytes 2359300
  67.6 3.8 %collective-permute-start = (f32[512,256]{1,0:T(8,128)S(1)}, f32[512,256]{1,0:T(8,128)S(1)}, u32[]{:S(2)}, u32[]{:S(2)}) collective-permute-start(f32[512,256]{1,0:T(8,128)S(1)} %bitcast.16), channel_id=1, source_target_pairs={{0,32},{32,0},{64,96},{96,64},{128,160},{160,128},{192,224},{224,1... | collective-permute-start | bytes 1572872 | tf_op jit(solution)/shard_map/ppermute | solution.py:279
  71.4 2.2 %slice-start = ((f32[32,16,384]{2,1,0:T(8,128)}), f32[32,16,128]{2,1,0:T(8,128)S(1)}, s32[]{:S(2)}) async-start(f32[32,16,384]{2,1,0:T(8,128)} %copy-done.2), calls=%async_computation.8 | async-start | bytes 524288 | tf_op jit(solution)/shard_map/slice | solution.py:275
  71.9 1.7 copy-start.3
  73.6 20.9 %copy-start = (f32[128,4096]{1,0:T(8,128)S(1)}, f32[128,4096]{1,0:T(8,128)}, u32[]{:S(2)}) copy-start(f32[128,4096]{1,0:T(8,128)} %inverse_ref.3) | copy-start | bytes 6291460
  74.7 19.8 %all-to-all-start.2 = ((f32[4,32,16,128]{3,2,1,0:T(8,128)}), f32[4,32,16,128]{3,2,1,0:T(8,128)}, u32[]{:S(2)}, u32[]{:S(2)}) async-start(f32[4,32,16,128]{3,2,1,0:T(8,128)} %broadcast_in_dim.31), calls=%async_computation.2 | async-start | bytes 2097152 | tf_op jit(solution)/shard_map/all_to_all | solution.py:24
  97.6 14.6 %all-to-all-start.3 = ((f32[32,2,512]{2,1,0:T(2,128)}), f32[32,2,512]{2,1,0:T(2,128)}, u32[]{:S(2)}, u32[]{:S(2)}) async-start(f32[32,2,512]{2,1,0:T(2,128)} %get-tuple-element.8), calls=%async_computation.3 | async-start | bytes 262144 | tf_op jit(solution)/shard_map/all_to_all | solution.py:24
  113.1 11.3 %collective-permute-start.1 = (f32[2,512]{1,0:T(2,128)S(1)}, f32[2,512]{1,0:T(2,128)S(1)}, u32[]{:S(2)}, u32[]{:S(2)}) collective-permute-start(f32[2,512]{1,0:T(2,128)S(1)} %reduce_sum.28), channel_id=1, source_target_pairs={{0,32},{32,0},{64,96},{96,64},{128,160},{160,128},{192,224},{224,1... | collective-permute-start | bytes 12296 | tf_op jit(solution)/shard_map/ppermute | solution.py:294
  117.2 15.1 %all-to-all-start.4 = ((f32[16,2,512]{2,1,0:T(2,128)}), f32[16,2,512]{2,1,0:T(2,128)S(1)}, u32[]{:S(2)}, u32[]{:S(2)}) async-start(f32[16,2,512]{2,1,0:T(2,128)} %broadcast_in_dim.32), calls=%async_computation.4 | async-start | bytes 131072 | tf_op jit(solution)/shard_map/all_to_all | solution.py:24
  132.3 2.2 %copy-start.1 = (f32[4096,256]{1,0:T(8,128)S(1)}, f32[4096,256]{1,0:T(8,128)}, u32[]{:S(2)}) copy-start(f32[4096,256]{1,0:T(8,128)} %all-gather.3.cloned.1.call-done) | copy-start | bytes 12582916
  156.2 33.0 %all-to-all-start.6 = ((f32[32,64,128]{2,1,0:T(8,128)}), f32[32,64,128]{2,1,0:T(8,128)S(1)}, u32[]{:S(2)}, u32[]{:S(2)}) async-start(f32[32,64,128]{2,1,0:T(8,128)} %spread.1), calls=%async_computation.6 | async-start | bytes 2097152 | tf_op jit(solution)/shard_map/all_to_all | solution.py:24
Sparse Core Ops, SparseCore 0:
  73.7 41.2 all-gather.2

commit v8 on v7

--- a/solution.py
+++ b/solution.py
@@ -43,7 +43,7 @@
 def gather_along_x(block):
     count = lax.axis_size("front")
     groups = [list(range(first, first + x_chips)) for first in range(0, count, x_chips)]
-    return exchange(copies(block, x_chips), "front", groups)
+    return lax.all_gather(block, "front", axis=0, axis_index_groups=groups)
 
 
 def split(value):
@@ -163,8 +163,8 @@
 
 
 def chain_kernel(
-    pos_ref, coupling_ref, share_ref, low_ref, high_ref, low_vec_ref, high_vec_ref,
-    below_ref, above_ref, out_ref, held, head, tail, vectors, into, above, sems,
+    pos_ref, coupling_ref, share_ref, low_ref, high_ref, below_ref, above_ref, out_ref,
+    held, head, tail, vectors, into, above, sems,
 ):
     pairs = held.shape[0]
     share, rows = below_ref.shape
@@ -178,9 +178,11 @@
     into[0] = jnp.zeros_like(into[0])
     above[pairs - 1] = jnp.zeros_like(into[0])
     for y in range(pairs):
-        vectors[y, :share, :] = share_ref[2 * y] + share_ref[2 * y + 1]
-    vectors[pairs, :share, :] = low_vec_ref[...]
-    vectors[pairs + 1, :share, :] = high_vec_ref[...]
+        both = share_ref[2 * y] + share_ref[2 * y + 1]
+        vectors[y, :share, :] = both[:, : 2 * rows]
+    chip = pos_ref[0]
+    vectors[pairs, :share, :] = share_ref[2 * chip][:, 2 * rows :]
+    vectors[pairs + 1, :share, :] = share_ref[2 * chip + 1][:, 2 * rows :]
     into[0, :share, :] = below_ref[...]
     above[pairs - 1, :share, :] = above_ref[...]
 
@@ -203,7 +205,6 @@
         from_above = vectors[y, :, rows:] - taken
         above[y - 1] = from_above
 
-    chip = pos_ref[0]
     incoming = into[chip]
     from_above = above[chip]
     middle = vectors[pairs, :, :rows] - dot_parts(two_parts(incoming), low_head, low_tail, 1)
@@ -223,7 +224,7 @@
         out_ref[piece] = kept
 
 
-def run_chain(position, coupling_all, shares, low, high, low_vec, high_vec, below, above, targets):
+def run_chain(position, coupling_all, shares, low, high, below, above, targets):
     share, rows = below.shape
     pairs = coupling_all.shape[0]
     vmem = pl.BlockSpec(memory_space=pltpu.VMEM)
@@ -231,7 +232,7 @@
         chain_kernel,
         out_shape=jax.ShapeDtypeStruct((targets, share, 3 * rows), jnp.float32),
         in_specs=[pl.BlockSpec(memory_space=pltpu.SMEM), pl.BlockSpec(memory_space=pltpu.HBM)]
-        + [vmem] * 7,
+        + [vmem] * 5,
         out_specs=vmem,
         scratch_shapes=[
             pltpu.VMEM((pairs, 2 * rows, rows), jnp.float32),
@@ -242,14 +243,14 @@
             pltpu.VMEM((pairs, padded, rows), jnp.float32),
             pltpu.SemaphoreType.DMA((pairs,)),
         ],
-        compiler_params=pltpu.CompilerParams(vmem_limit_bytes=32 * 1024 * 1024),
+        compiler_params=pltpu.CompilerParams(vmem_limit_bytes=57 * 1024 * 1024),
         cost_estimate=pl.CostEstimate(
             flops=12 * pairs * 16 * rows * rows,
             bytes_accessed=8 * pairs * rows * rows,
             transcendentals=0,
         ),
         name="chain",
-    )(position, coupling_all, shares, low, high, low_vec, high_vec, below, above)
+    )(position, coupling_all, shares, low, high, below, above)
 
 
 def on_device(right_side, inverse_blocks, panels, receive_rows, below_update, above_solution):
@@ -284,16 +285,12 @@
     c_pair = -product(c_high, c_low)
     g_pair = low[rows:] + product(c_low.T, lifted)
     pair_half = jnp.where(is_upper, g_pair, c_pair)
-    pair_half, side_chunk = lax.optimization_barrier((pair_half, side_chunk))
     coupling_all = gather_leaf(pair_half).reshape(leaf_count // 2, 2 * rows, rows)
 
     local_forward, vectors = run_forward(
         gather_along_x(side_chunk), inverse_blocks, stacked, front_count
     )
     vectors = jnp.sum(exchange(vectors), axis=0)
-    mate_vectors = lax.ppermute(vectors, "leaf", swap)
-    low_vec = jnp.where(is_upper, mate_vectors, vectors)
-    high_vec = jnp.where(is_upper, vectors, mate_vectors)
     u_own, w_own = (vectors[:, :rows], vectors[:, rows:])
     u_moved = -product_nt(u_own, c_high)
     w_moved = product(jnp.where(is_upper, w_own, u_own), jnp.where(is_upper, -c_low, lifted))
@@ -301,6 +298,7 @@
         [
             jnp.where(is_upper, u_own, u_moved),
             jnp.where(is_upper, w_moved, w_own + w_moved),
+            vectors,
         ],
         axis=1,
     )
@@ -311,7 +309,7 @@
     position = jnp.stack([leaf_pos // 2, leaf_pos % 2])
     result = exchange(
         run_chain(
-            position, coupling_all, shares, low, high, low_vec, high_vec,
+            position, coupling_all, shares, low, high,
             below_rows, above_rows, front_count,
         )
     )

time: 198 us -> 207 us (1.045)
  waiting for transfers between devices: 57.8 us -> 69.3 us
  starting transfers between devices: 27.8 us -> 20 us
  blocking collectives: 72 us -> 75.7 us
    all_gather x0 -> x1, waiting for transfers between devices: none -> 9.65 us  [gather_along_x(): return lax.all_gather(block, 'front', axis=0, axis_index_groups=groups)]
    all_gather x1, waiting for transfers between devices: 0.01 us -> 8.27 us  [gather_leaf(): return lax.all_gather(block, 'leaf', axis=0)]
    all_to_all x4 -> x3, waiting for transfers between devices: 56 us -> 49.5 us  [exchange(): lax.all_to_all(blocks, axis, 0, 0, tiled=True, axis_index_groups=groups)]
    all_to_all x4 -> x3, starting transfers between devices: 24 us -> 18.1 us  [exchange(): lax.all_to_all(blocks, axis, 0, 0, tiled=True, axis_index_groups=groups)]
    all_to_all x3, blocking collectives: 72 us -> 75.7 us  [exchange(): lax.all_to_all(blocks, axis, 0, 0, tiled=True, axis_index_groups=groups)]
    unnamed x16 -> x20, local copies, waits for them, and re-layouts: 4.82 us -> 3.96 us
  transfers between devices with their start and end apart: 7 -> 6, of which waited for: 5 -> 6; matrix products, arithmetic and copies ran while one was open for 3% -> 5% of each run, Pallas kernels for 2% -> 1%
where the time goes in v8:
time: 207 us; the launch traced here: 206 us
  blocking collectives  75.7 us (37%)
  waiting for transfers between devices  69.3 us (33%)
  starting transfers between devices  20 us (10%)
  between operations  14.3 us (7%)
  Pallas kernels  9.57 us (5%)
  local copies, waits for them, and re-layouts  8.45 us (4%)
  other arithmetic  4.91 us (2%)
  matrix products  4.08 us (2%)
    all_to_all x3, blocking collectives, exchange(): lax.all_to_all(blocks, axis, 0, 0, tiled=True, axis_index_groups=groups)  75.7 us
    all_to_all x3, waiting for transfers between devices, exchange(): lax.all_to_all(blocks, axis, 0, 0, tiled=True, axis_index_groups=groups)  49.5 us
    all_to_all x3, starting transfers between devices, exchange(): lax.all_to_all(blocks, axis, 0, 0, tiled=True, axis_index_groups=groups)  18.1 us
    all_gather x1, waiting for transfers between devices, gather_along_x(): return lax.all_gather(block, 'front', axis=0, axis_index_groups=groups)  9.65 us
    all_gather x1, waiting for transfers between devices, gather_leaf(): return lax.all_gather(block, 'leaf', axis=0)  8.27 us
    pallas_call x1, Pallas kernels, run_chain(): pl.pallas_call(chain_kernel, out_shape=jax.ShapeDtypeStruct((targets, sha...  6.51 us
  transfers between devices with their start and end apart: 6, of which 6 were waited for; matrix products, arithmetic and copies ran while one was open for 5% of the time, Pallas kernels for 1%

profile of v8, /device:TPU:2, one launch (start us, length us, event | category | flops | bytes accessed | tf_op | source)
XLA Modules:
  0.0 206.4 jit_solution(9428045616210436710)
XLA Ops:
  8.6 1.9 copy.12
  12.1 35.7 %all_to_all.30 = f32[32,16,384]{2,1,0:T(8,128)S(1)} all-to-all(f32[32,16,384]{2,1,0:T(8,128)S(1)} %pad_maximum_fusion), channel_id=1, replica_groups=mesh['leaf'=16,'front'=32] {'front'}, dimensions={0} | all-to-all | bytes 1572864 | tf_op jit(solution)/shard_map/all_to_all | solution.py:24
  47.8 0.9 broadcast_in_dim.24
  48.7 5.6 %all-to-all-start.1 = ((f32[32,16,256]{2,1,0:T(8,128)}), f32[32,16,256]{2,1,0:T(8,128)S(1)}, u32[]{:S(2)}, u32[]{:S(2)}) async-start(f32[32,16,256]{2,1,0:T(8,128)} %broadcast_in_dim.24), calls=%async_computation.1 | async-start | bytes 1048576 | tf_op jit(solution)/shard_map/all_to_all | solution.py:24
  55.1 14.8 %all-to-all-done.1 = f32[32,16,256]{2,1,0:T(8,128)S(1)} async-done(((f32[32,16,256]{2,1,0:T(8,128)}), f32[32,16,256]{2,1,0:T(8,128)S(1)}, u32[]{:S(2)}, u32[]{:S(2)}) %all-to-all-start.1) | async-done | bytes 524320 | tf_op jit(solution)/shard_map/all_to_all | solution.py:24
  69.9 1.9 collective-permute-start
  71.9 1.9 collective-permute-done
  74.8 1.1 fusion.3
  76.0 1.0 pad_maximum_fusion.1.stacked_ref
  76.9 9.6 %all-gather.7.cloned.1.call-done = f32[128,16,128]{2,1,0:T(8,128)} async-done(((f32[32,16,128]{2,1,0:T(8,128)}), f32[128,16,128]{2,1,0:T(8,128)}) %all-gather.7.cloned.1.call-update) | async-done | bytes 1048592 | tf_op jit(solution)/shard_map/all_gather | solution.py:46
  86.6 1.2 copy-done.1
  87.8 1.1 forward.1
  89.0 19.3 %all_to_all.31 = f32[32,2,512]{2,1,0:T(2,128)} all-to-all(f32[32,2,512]{2,1,0:T(2,128)S(1)} %get-tuple-element.4), channel_id=1, replica_groups=mesh['leaf'=16,'front'=32] {'front'}, dimensions={0} | all-to-all | bytes 262144 | tf_op jit(solution)/shard_map/all_to_all | solution.py:24
  108.3 1.0 reduce_sum.28
  109.6 1.2 add_select_fusion
  111.5 6.8 %all-to-all-start.3 = ((f32[16,2,1024]{2,1,0:T(2,128)}), f32[16,2,1024]{2,1,0:T(2,128)S(1)}, u32[]{:S(2)}, u32[]{:S(2)}) async-start(f32[16,2,1024]{2,1,0:T(2,128)} %broadcast_in_dim.25), calls=%async_computation.3 | async-start | bytes 262144 | tf_op jit(solution)/shard_map/all_to_all | solution.py:24
  119.0 1.3 constant_dynamic-slice_fusion.1
  120.3 8.2 %all-to-all-done.3.share_ref = f32[16,2,1024]{2,1,0:T(2,128)S(1)} async-done(((f32[16,2,1024]{2,1,0:T(2,128)}), f32[16,2,1024]{2,1,0:T(2,128)S(1)}, u32[]{:S(2)}, u32[]{:S(2)}) %all-to-all-start.3) | async-done | bytes 131104 | tf_op jit(solution)/shard_map/all_to_all | solution.py:24
  128.5 8.3 %all-gather.5.cloned.1.call-done = f32[4096,256]{1,0:T(8,128)} async-done(((f32[256,256]{1,0:T(8,128)}), f32[4096,256]{1,0:T(8,128)}) %all-gather.5.cloned.1.call-update) | async-done | bytes 4194320 | tf_op jit(solution)/shard_map/all_gather | solution.py:36
  136.8 6.5 %chain.1 = f32[32,2,768]{2,1,0:T(2,128)} custom-call(s32[2]{0:T(128)} %pad_add_fusion.pos_ref, f32[8,512,256]{2,1,0:T(8,128)} %bitcast.17, f32[16,2,1024]{2,1,0:T(2,128)} %copy-done.6, f32[512,256]{1,0:T(8,128)} %copy-done.2, f32[512,256]{1,0:T(8,128)} %copy-done.3, f32[2,256]{1,0:T(2,128)} %get-tuple-element.9.below_ref, f32[2,256]{1,0:T(2,128)} %get-tuple-element.8.above_ref), custom_call_target="tpu_custom_call" | custom-call | flops 100663296 | bytes 4194304 | tf_op jit(solution)/shard_map/chain/pallas_call | solution.py:231
  143.3 20.7 %all_to_all.32.result_ref = f32[32,2,768]{2,1,0:T(2,128)S(1)} all-to-all(f32[32,2,768]{2,1,0:T(2,128)} %chain.1), channel_id=1, replica_groups=mesh['leaf'=16,'front'=32] {'front'}, dimensions={0} | all-to-all | bytes 393216 | tf_op jit(solution)/shard_map/all_to_all | solution.py:24
  164.0 1.9 spread.1
  165.9 5.7 %all-to-all-start.5 = ((f32[32,64,128]{2,1,0:T(8,128)}), f32[32,64,128]{2,1,0:T(8,128)S(1)}, u32[]{:S(2)}, u32[]{:S(2)}) async-start(f32[32,64,128]{2,1,0:T(8,128)} %spread.1), calls=%async_computation.5 | async-start | bytes 2097152 | tf_op jit(solution)/shard_map/all_to_all | solution.py:24
  172.4 26.5 %all-to-all-done.5 = f32[32,64,128]{2,1,0:T(8,128)S(1)} async-done(((f32[32,64,128]{2,1,0:T(8,128)}), f32[32,64,128]{2,1,0:T(8,128)S(1)}, u32[]{:S(2)}, u32[]{:S(2)}) %all-to-all-start.5) | async-done | bytes 1048608 | tf_op jit(solution)/shard_map/all_to_all | solution.py:24
  (43 shorter events, 8.0 us)
Async XLA Ops:
  8.5 2.8 %copy-start.7 = (f32[256,128]{1,0:T(8,128)S(1)}, f32[256,128]{1,0:T(8,128)}, u32[]{:S(2)}) copy-start(f32[256,128]{1,0:T(8,128)} %param.8) | copy-start | bytes 393220
  10.5 1.5 copy-start.8
  11.4 0.7 copy-start.5
  48.7 21.2 %all-to-all-start.1 = ((f32[32,16,256]{2,1,0:T(8,128)}), f32[32,16,256]{2,1,0:T(8,128)S(1)}, u32[]{:S(2)}, u32[]{:S(2)}) async-start(f32[32,16,256]{2,1,0:T(8,128)} %broadcast_in_dim.24), calls=%async_computation.1 | async-start | bytes 1048576 | tf_op jit(solution)/shard_map/all_to_all | solution.py:24
  54.3 32.3 %all-gather.7.cloned.1.call-start = ((), (), s32[]{:S(2)}) async-start(), calls=%async_computation.7 | async-start | bytes 1310720 | tf_op jit(solution)/shard_map/all_gather | solution.py:46
  55.1 81.7 %all-gather.5.cloned.1.call-start = ((), (), s32[]{:S(2)}) async-start(), calls=%async_computation.6 | async-start | bytes 4456448 | tf_op jit(solution)/shard_map/all_gather | solution.py:36
  69.9 3.8 %collective-permute-start = (f32[512,256]{1,0:T(8,128)S(1)}, f32[512,256]{1,0:T(8,128)S(1)}, u32[]{:S(2)}, u32[]{:S(2)}) collective-permute-start(f32[512,256]{1,0:T(8,128)S(1)} %bitcast.18), channel_id=1, source_target_pairs={{0,32},{32,0},{64,96},{96,64},{128,160},{160,128},{192,224},{224,1... | collective-permute-start | bytes 1572872 | tf_op jit(solution)/shard_map/ppermute | solution.py:280
  73.8 35.5 %copy-start.3 = (f32[512,256]{1,0:T(8,128)}, f32[512,256]{1,0:T(8,128)S(1)}, u32[]{:S(2)}) copy-start(f32[512,256]{1,0:T(8,128)S(1)} %get-tuple-element.7.high_ref) | copy-start | bytes 1572868
  73.8 35.8 %copy-start.2 = (f32[512,256]{1,0:T(8,128)}, f32[512,256]{1,0:T(8,128)S(1)}, u32[]{:S(2)}) copy-start(f32[512,256]{1,0:T(8,128)S(1)} %get-tuple-element.6.low_ref) | copy-start | bytes 1572868
  73.8 12.8 %copy-start = (f32[128,4096]{1,0:T(8,128)S(1)}, f32[128,4096]{1,0:T(8,128)}, u32[]{:S(2)}) copy-start(f32[128,4096]{1,0:T(8,128)} %inverse_ref.3) | copy-start | bytes 6291460
  74.2 1.7 copy-start.4
  86.6 1.2 copy-start.1
  111.5 17.0 %all-to-all-start.3 = ((f32[16,2,1024]{2,1,0:T(2,128)}), f32[16,2,1024]{2,1,0:T(2,128)S(1)}, u32[]{:S(2)}, u32[]{:S(2)}) async-start(f32[16,2,1024]{2,1,0:T(2,128)} %broadcast_in_dim.25), calls=%async_computation.3 | async-start | bytes 262144 | tf_op jit(solution)/shard_map/all_to_all | solution.py:24
  128.5 8.3 %copy-start.6 = (f32[16,2,1024]{2,1,0:T(2,128)}, f32[16,2,1024]{2,1,0:T(2,128)S(1)}, u32[]{:S(2)}) copy-start(f32[16,2,1024]{2,1,0:T(2,128)S(1)} %all-to-all-done.3.share_ref) | copy-start | bytes 393220
  165.9 33.0 %all-to-all-start.5 = ((f32[32,64,128]{2,1,0:T(8,128)}), f32[32,64,128]{2,1,0:T(8,128)S(1)}, u32[]{:S(2)}, u32[]{:S(2)}) async-start(f32[32,64,128]{2,1,0:T(8,128)} %spread.1), calls=%async_computation.5 | async-start | bytes 2097152 | tf_op jit(solution)/shard_map/all_to_all | solution.py:24
Sparse Core Ops, SparseCore 0:
  57.2 29.3 all-gather.6
  88.7 48.0 all-gather.4

commit v9 on v3

--- a/solution.py
+++ b/solution.py
@@ -8,6 +8,7 @@
 exact = lax.Precision.HIGHEST
 x_chips = 4
 padded = 8
+in_flight = 3
 
 
 def product(left, right):
@@ -32,12 +33,6 @@
     return exchange(copies(block, lax.axis_size("front")))
 
 
-def scatter_front(total):
-    count = lax.axis_size("front")
-    pieces = total.reshape(count, total.shape[0] // count, *total.shape[1:])
-    return jnp.sum(exchange(pieces), axis=0)
-
-
 def gather_leaf(block):
     return lax.all_gather(block, "leaf", axis=0)
 
@@ -46,19 +41,10 @@
     return exchange(copies(block, lax.axis_size("leaf")), "leaf")
 
 
-def gather_along_z(block):
-    count = lax.axis_size("front")
-    groups = [list(range(x, count, x_chips)) for x in range(x_chips)]
-    wide = jnp.concatenate([block, jnp.zeros((3 * block.shape[0], block.shape[1]), block.dtype)])
-    wide = lax.all_gather(wide, "front", axis=0, axis_index_groups=groups)
-    return wide[:, : block.shape[0]]
-
-
-def gather_along_x(planes):
+def gather_along_x(block):
     count = lax.axis_size("front")
     groups = [list(range(first, first + x_chips)) for first in range(0, count, x_chips)]
-    whole = exchange(copies(planes, x_chips), "front", groups)
-    return whole.transpose(1, 0, 2, 3).reshape(count, *planes.shape[1:])
+    return exchange(copies(block, x_chips), "front", groups)
 
 
 def split(value):
@@ -78,6 +64,103 @@
     both = lax.dot_general(parts, head, dims, preferred_element_type=jnp.float32)
     both += lax.dot_general(parts, tail, dims, preferred_element_type=jnp.float32)
     return both[:padded] + both[padded:]
+
+
+def fold(parts, rows, columns):
+    small = parts[rows:, columns:] + (parts[rows:, :columns] + parts[:rows, columns:])
+    return small + parts[:rows, :columns]
+
+
+def two_columns(value):
+    head, tail = split(value)
+    return jnp.concatenate([head, tail], axis=1)
+
+
+def forward_kernel(side_ref, inverse_ref, stacked_ref, forward_ref, vector_ref):
+    chunks, blocks, chunk, block = side_ref.shape
+    rhs = chunks * chunk
+    group = 4
+    nt = (((1,), (1,)), ((), ()))
+    total = jnp.zeros((2 * rhs, 2 * block), jnp.float32)
+    for first in range(0, blocks, group):
+        side = jnp.concatenate(
+            [
+                jnp.concatenate([side_ref[c, first + j] for j in range(group)], axis=1)
+                for c in range(chunks)
+            ]
+        )
+        weights = two_parts(inverse_ref[:, first * block : (first + group) * block])
+        total += lax.dot_general(
+            two_parts(side), weights, nt, preferred_element_type=jnp.float32
+        )
+    forward = fold(total, rhs, block)
+    forward_ref[...] = forward
+    vectors = lax.dot_general(
+        two_parts(forward), two_parts(stacked_ref[...]), nt, preferred_element_type=jnp.float32
+    )
+    vectors = fold(vectors, rhs, stacked_ref.shape[0])
+    share = vector_ref.shape[1]
+    for piece in range(vector_ref.shape[0]):
+        vector_ref[piece] = vectors[piece * share : (piece + 1) * share]
+
+
+def run_forward(side, inverse_blocks, stacked, targets):
+    rhs = side.shape[0] * side.shape[2]
+    block = inverse_blocks.shape[0]
+    vmem = pl.BlockSpec(memory_space=pltpu.VMEM)
+    return pl.pallas_call(
+        forward_kernel,
+        out_shape=(
+            jax.ShapeDtypeStruct((rhs, block), jnp.float32),
+            jax.ShapeDtypeStruct((targets, rhs // targets, stacked.shape[0]), jnp.float32),
+        ),
+        in_specs=[vmem] * 3,
+        out_specs=(vmem, vmem),
+        compiler_params=pltpu.CompilerParams(vmem_limit_bytes=32 * 1024 * 1024),
+        cost_estimate=pl.CostEstimate(
+            flops=8 * rhs * block * inverse_blocks.shape[1],
+            bytes_accessed=4 * inverse_blocks.size + 4 * side.size,
+            transcendentals=0,
+        ),
+        name="forward",
+    )(side, inverse_blocks, stacked)
+
+
+def spread_kernel(result_ref, forward_ref, stacked_ref, inverse_ref, out_ref, held):
+    share = result_ref.shape[1]
+    rhs, block = forward_ref.shape
+    for piece in range(result_ref.shape[0]):
+        held[piece * share : (piece + 1) * share, :] = result_ref[piece, :, : held.shape[1]]
+    taken = jnp.dot(
+        two_parts(held[...]), two_columns(stacked_ref[...]), preferred_element_type=jnp.float32
+    )
+    reduced = two_parts(forward_ref[...] - fold(taken, rhs, block))
+    group = 2
+    for first in range(0, out_ref.shape[0], group):
+        weights = two_columns(inverse_ref[:, first * block : (first + group) * block])
+        parts = jnp.dot(reduced, weights, preferred_element_type=jnp.float32)
+        parts = fold(parts, rhs, group * block)
+        for j in range(group):
+            out_ref[first + j] = parts[:, j * block : (j + 1) * block]
+
+
+def run_spread(result, forward, stacked, inverse_blocks):
+    rhs, block = forward.shape
+    vmem = pl.BlockSpec(memory_space=pltpu.VMEM)
+    return pl.pallas_call(
+        spread_kernel,
+        out_shape=jax.ShapeDtypeStruct((inverse_blocks.shape[1] // block, rhs, block), jnp.float32),
+        in_specs=[vmem] * 4,
+        out_specs=vmem,
+        scratch_shapes=[pltpu.VMEM((rhs, stacked.shape[0]), jnp.float32)],
+        compiler_params=pltpu.CompilerParams(vmem_limit_bytes=32 * 1024 * 1024),
+        cost_estimate=pl.CostEstimate(
+            flops=8 * rhs * block * inverse_blocks.shape[1],
+            bytes_accessed=4 * inverse_blocks.size + 4 * rhs * inverse_blocks.shape[1],
+            transcendentals=0,
+        ),
+        name="spread",
+    )(result, forward, stacked, inverse_blocks)
 
 
 def chain_kernel(
@@ -90,7 +173,7 @@
     def fetch(s):
         return pltpu.make_async_copy(coupling_ref.at[s], held.at[s], sems.at[s])
 
-    for s in range(sections):
+    for s in range(in_flight):
         fetch(s).start()
     vectors[...] = jnp.zeros_like(vectors)
     into[0] = jnp.zeros_like(into[0])
@@ -103,6 +186,8 @@
     incoming = into[0]
     for s in range(sections):
         fetch(s).wait()
+        if s + in_flight < sections:
+            fetch(s + in_flight).start()
         block_head, block_tail = split(held[s])
         head[s] = block_head[:rows]
         tail[s] = block_tail[:rows]
@@ -131,7 +216,7 @@
         out_shape=jax.ShapeDtypeStruct((targets, share, 3 * rows), jnp.float32),
         in_specs=[
             pl.BlockSpec(memory_space=pltpu.SMEM),
-            pl.BlockSpec(memory_space=pl.ANY),
+            pl.BlockSpec(memory_space=pltpu.HBM),
             vmem,
             vmem,
             vmem,
@@ -146,7 +231,7 @@
             pltpu.VMEM((sections, padded, rows), jnp.float32),
             pltpu.SemaphoreType.DMA((sections,)),
         ],
-        compiler_params=pltpu.CompilerParams(vmem_limit_bytes=32 * 1024 * 1024),
+        compiler_params=pltpu.CompilerParams(vmem_limit_bytes=56 * 1024 * 1024),
         cost_estimate=pl.CostEstimate(
             flops=12 * sections * 16 * rows * rows,
             bytes_accessed=8 * sections * rows * rows,
@@ -166,17 +251,23 @@
     share = rhs // front_count
     targets = receive_rows[0]
 
-    planes = gather_along_z(right_side)
+    chunk = rhs // x_chips
+    slice_rows = 2 * rows // front_count
     picked = jnp.take(inverse_blocks, targets, axis=1)
     stacked = jnp.concatenate([panels, picked.T], axis=0)
-    coupling = scatter_front(product(stacked, picked))
+    own_coupling = product(stacked, picked).reshape(front_count, slice_rows, rows)
+    own_chunks = jnp.tile(right_side.reshape(x_chips, chunk, block), (front_count // x_chips, 1, 1))
+    arrived = exchange(jnp.concatenate([own_coupling, own_chunks], axis=2))
+    coupling = jnp.sum(arrived[:, :, :rows], axis=0)
+    side_chunk = arrived[:, :, rows:]
     coupling = gather_front(coupling).reshape(2 * rows, rows)
-    coupling, planes = lax.optimization_barrier((coupling, planes))
+
+    coupling, side_chunk = lax.optimization_barrier((coupling, side_chunk))
     coupling_all = gather_leaf(coupling)
-
-    section_side = gather_along_x(planes).transpose(1, 0, 2).reshape(rhs, front_count * block)
-    local_forward = product_nt(section_side, inverse_blocks)
-    vectors = scatter_front(product_nt(local_forward, stacked))
+    local_forward, vectors = run_forward(
+        gather_along_x(side_chunk), inverse_blocks, stacked, front_count
+    )
+    vectors = jnp.sum(exchange(vectors), axis=0)
     vector_all = gather_leaf_small(vectors)
 
     below_rows = lax.dynamic_slice_in_dim(below_update, front_pos * share, share, 0)
@@ -184,15 +275,11 @@
     result = exchange(
         run_chain(leaf_pos, coupling_all, vector_all, below_rows, above_rows, front_count)
     )
-    result = result.reshape(rhs, 3 * rows)
+    spread = run_spread(result, local_forward, stacked, inverse_blocks)
+    solution = jnp.sum(exchange(spread), axis=0)
     update_share = rows // front_count
-    sent_updates = lax.dynamic_slice_in_dim(
-        result, 2 * rows + front_pos * update_share, update_share, 1
-    )
-    reduced = local_forward - product(result[:, : 2 * rows], stacked)
-    spread = product(reduced, inverse_blocks)
-    spread = spread.reshape(rhs, front_count, block).transpose(1, 0, 2)
-    solution = jnp.sum(exchange(spread), axis=0)
+    updates = result[:, :, 2 * rows :].reshape(rhs, rows)
+    sent_updates = lax.dynamic_slice_in_dim(updates, front_pos * update_share, update_share, 1)
     return (solution, sent_updates)
 
 

time: 210 us -> 201 us (0.957)
  blocking collectives: 53 us -> 71.2 us
  waiting for transfers between devices: 83.9 us -> 66.5 us
  starting transfers between devices: 31.8 us -> 23.3 us
  Pallas kernels: 7.12 us -> 13.9 us
  matrix products: 5.57 us -> 0.58 us
  local copies, waits for them, and re-layouts: 13 us -> 8.32 us
    all_gather x1 -> x0, waiting for transfers between devices: 26 us -> none  [gather_along_z(): wide = lax.all_gather(wide, 'front', axis=0, axis_index_groups=groups)]
    all_to_all x3, blocking collectives: 53 us -> 71.2 us  [exchange(): lax.all_to_all(blocks, axis, 0, 0, tiled=True, axis_index_groups=groups)]
    all_to_all x4, waiting for transfers between devices: 50.5 us -> 59.1 us  [exchange(): lax.all_to_all(blocks, axis, 0, 0, tiled=True, axis_index_groups=groups)]
    all_to_all x4, starting transfers between devices: 31.7 us -> 23.2 us  [exchange(): lax.all_to_all(blocks, axis, 0, 0, tiled=True, axis_index_groups=groups)]
    pallas_call x1, Pallas kernels: 7.12 us -> 10.8 us  [run_chain(): pl.pallas_call(chain_kernel, out_shape=jax.ShapeDtypeStruct((targets, sha...]
    unnamed x14 -> x16, local copies, waits for them, and re-layouts: 6.83 us -> 3.46 us
    pallas_call x0 -> x2, Pallas kernels: none -> 3.05 us  [the longest x1 1.91 us: run_spread(): pl.pallas_call(spread_kernel, out_shape=jax.ShapeDtypeStruct((inverse_blo...]
    dot_general x2 -> x0, matrix products: 2.68 us -> none  [product_nt(): lax.dot_general(left, right, (((1,), (1,)), ((), ())), precision=exact, p...]
  transfers between devices with their start and end apart: 6 -> 5, of which waited for: 5 -> 5; matrix products, arithmetic and copies ran while one was open for 4% -> 2% of each run, Pallas kernels for 0% -> 1%
where the time goes in v9:
time: 201 us; the launch traced here: 200 us
  blocking collectives  71.2 us (35%)
  waiting for transfers between devices  66.5 us (33%)
  starting transfers between devices  23.3 us (12%)
  between operations  14.2 us (7%)
  Pallas kernels  13.9 us (7%)
  local copies, waits for them, and re-layouts  8.32 us (4%)
    all_to_all x3, blocking collectives, exchange(): lax.all_to_all(blocks, axis, 0, 0, tiled=True, axis_index_groups=groups)  71.2 us
    all_to_all x4, waiting for transfers between devices, exchange(): lax.all_to_all(blocks, axis, 0, 0, tiled=True, axis_index_groups=groups)  59.1 us
    all_to_all x4, starting transfers between devices, exchange(): lax.all_to_all(blocks, axis, 0, 0, tiled=True, axis_index_groups=groups)  23.2 us
    pallas_call x1, Pallas kernels, run_chain(): pl.pallas_call(chain_kernel, out_shape=jax.ShapeDtypeStruct((targets, sha...  10.8 us
    all_gather x1, waiting for transfers between devices, gather_leaf(): return lax.all_gather(block, 'leaf', axis=0)  7.39 us
  transfers between devices with their start and end apart: 5, of which 5 were waited for; matrix products, arithmetic and copies ran while one was open for 2% of the time, Pallas kernels for 1%

profile of v9, /device:TPU:2, one launch (start us, length us, event | category | flops | bytes accessed | tf_op | source)
XLA Modules:
  0.0 199.9 jit_solution(9235455707349352338)
XLA Ops:
  7.2 1.9 copy.10
  9.2 0.7 gather_fusion
  10.8 35.7 %all_to_all.35 = f32[32,16,384]{2,1,0:T(8,128)S(1)} all-to-all(f32[32,16,384]{2,1,0:T(8,128)S(1)} %pad_maximum_fusion), channel_id=1, replica_groups=mesh['leaf'=16,'front'=32] {'front'}, dimensions={0} | all-to-all | bytes 1572864 | tf_op jit(solution)/shard_map/all_to_all | solution.py:25
  46.5 0.9 broadcast_in_dim.30
  47.4 5.6 %all-to-all-start.1 = ((f32[32,16,256]{2,1,0:T(8,128)}), f32[32,16,256]{2,1,0:T(8,128)S(1)}, u32[]{:S(2)}, u32[]{:S(2)}) async-start(f32[32,16,256]{2,1,0:T(8,128)} %broadcast_in_dim.30), calls=%async_computation.1 | async-start | bytes 1048576 | tf_op jit(solution)/shard_map/all_to_all | solution.py:25
  53.0 15.6 %all-to-all-done.1 = f32[32,16,256]{2,1,0:T(8,128)S(1)} async-done(((f32[32,16,256]{2,1,0:T(8,128)}), f32[32,16,256]{2,1,0:T(8,128)S(1)}, u32[]{:S(2)}, u32[]{:S(2)}) %all-to-all-start.1) | async-done | bytes 524320 | tf_op jit(solution)/shard_map/all_to_all | solution.py:25
  68.6 0.8 copy-done.1
  69.4 1.1 broadcast_in_dim.31
  70.6 4.8 %all-to-all-start.2 = ((f32[4,32,16,128]{3,2,1,0:T(8,128)}), f32[4,32,16,128]{3,2,1,0:T(8,128)S(1)}, u32[]{:S(2)}, u32[]{:S(2)}) async-start(f32[4,32,16,128]{3,2,1,0:T(8,128)} %broadcast_in_dim.31), calls=%async_computation.2 | async-start | bytes 2097152 | tf_op jit(solution)/shard_map/all_to_all | solution.py:25
  75.4 1.0 pad_maximum_fusion.1.stacked_ref
  76.4 9.8 %all-to-all-done.2.side_ref = f32[4,32,16,128]{3,2,1,0:T(8,128)S(1)} async-done(((f32[4,32,16,128]{3,2,1,0:T(8,128)}), f32[4,32,16,128]{3,2,1,0:T(8,128)S(1)}, u32[]{:S(2)}, u32[]{:S(2)}) %all-to-all-start.2) | async-done | bytes 1048608 | tf_op jit(solution)/shard_map/all_to_all | solution.py:25
  86.1 1.1 forward.1
  87.3 14.8 %all_to_all.36 = f32[32,2,512]{2,1,0:T(2,128)S(1)} all-to-all(f32[32,2,512]{2,1,0:T(2,128)S(1)} %get-tuple-element.8), channel_id=1, replica_groups=mesh['leaf'=16,'front'=32] {'front'}, dimensions={0} | all-to-all | bytes 262144 | tf_op jit(solution)/shard_map/all_to_all | solution.py:25
  102.8 7.2 %all-to-all-start.4 = ((f32[16,2,512]{2,1,0:T(2,128)}), f32[16,2,512]{2,1,0:T(2,128)S(1)}, u32[]{:S(2)}, u32[]{:S(2)}) async-start(f32[16,2,512]{2,1,0:T(2,128)} %broadcast_in_dim.32), calls=%async_computation.4 | async-start | bytes 131072 | tf_op jit(solution)/shard_map/all_to_all | solution.py:25
  110.0 1.3 constant_dynamic-slice_fusion.1
  111.3 7.2 %all-to-all-done.4.vector_ref = f32[16,2,512]{2,1,0:T(2,128)S(1)} async-done(((f32[16,2,512]{2,1,0:T(2,128)}), f32[16,2,512]{2,1,0:T(2,128)S(1)}, u32[]{:S(2)}, u32[]{:S(2)}) %all-to-all-start.4) | async-done | bytes 65568 | tf_op jit(solution)/shard_map/all_to_all | solution.py:25
  118.6 7.4 %all-gather.3.cloned.1.call-done = f32[8192,256]{1,0:T(8,128)} async-done(((f32[512,256]{1,0:T(8,128)}), f32[8192,256]{1,0:T(8,128)}) %all-gather.3.cloned.1.call-update) | async-done | bytes 8388624 | tf_op jit(solution)/shard_map/all_gather | solution.py:37
  126.0 10.8 %chain.1 = f32[32,2,768]{2,1,0:T(2,128)} custom-call(s32[1]{0:T(128)} %bitcast.pos_ref, f32[16,512,256]{2,1,0:T(8,128)} %bitcast.11, f32[16,2,512]{2,1,0:T(2,128)} %copy-done.4, f32[2,256]{1,0:T(2,128)} %get-tuple-element.11.below_ref, f32[2,256]{1,0:T(2,128)} %get-tuple-element.10.above_ref), custom_call_target="tpu_custom_call" | custom-call | flops 201326592 | bytes 8388608 | tf_op jit(solution)/shard_map/chain/pallas_call | solution.py:214
  136.8 20.7 %all_to_all.37.result_ref = f32[32,2,768]{2,1,0:T(2,128)S(1)} all-to-all(f32[32,2,768]{2,1,0:T(2,128)} %chain.1), channel_id=1, replica_groups=mesh['leaf'=16,'front'=32] {'front'}, dimensions={0} | all-to-all | bytes 393216 | tf_op jit(solution)/shard_map/all_to_all | solution.py:25
  157.5 1.9 spread.1
  159.4 5.7 %all-to-all-start.6 = ((f32[32,64,128]{2,1,0:T(8,128)}), f32[32,64,128]{2,1,0:T(8,128)S(1)}, u32[]{:S(2)}, u32[]{:S(2)}) async-start(f32[32,64,128]{2,1,0:T(8,128)} %spread.1), calls=%async_computation.6 | async-start | bytes 2097152 | tf_op jit(solution)/shard_map/all_to_all | solution.py:25
  165.2 0.7 copy.12
  165.9 26.5 %all-to-all-done.6 = f32[32,64,128]{2,1,0:T(8,128)S(1)} async-done(((f32[32,64,128]{2,1,0:T(8,128)}), f32[32,64,128]{2,1,0:T(8,128)S(1)}, u32[]{:S(2)}, u32[]{:S(2)}) %all-to-all-start.6) | async-done | bytes 1048608 | tf_op jit(solution)/shard_map/all_to_all | solution.py:25
  192.4 0.7 reduce_sum.29
  (29 shorter events, 1.8 us)
Async XLA Ops:
  7.2 2.0 copy-start.6
  7.2 2.9 %copy-start.3 = (f32[256,128]{1,0:T(8,128)S(1)}, f32[256,128]{1,0:T(8,128)}, u32[]{:S(2)}) copy-start(f32[256,128]{1,0:T(8,128)} %param.8) | copy-start | bytes 393220
  9.2 1.5 copy-start.5
  10.1 0.7 copy-start.2
  47.4 21.2 %all-to-all-start.1 = ((f32[32,16,256]{2,1,0:T(8,128)}), f32[32,16,256]{2,1,0:T(8,128)S(1)}, u32[]{:S(2)}, u32[]{:S(2)}) async-start(f32[32,16,256]{2,1,0:T(8,128)} %broadcast_in_dim.30), calls=%async_computation.1 | async-start | bytes 1048576 | tf_op jit(solution)/shard_map/all_to_all | solution.py:25
  52.9 73.0 %all-gather.3.cloned.1.call-start = ((), (), s32[]{:S(2)}) async-start(), calls=%async_computation.7 | async-start | bytes 8912896 | tf_op jit(solution)/shard_map/all_gather | solution.py:37
  68.6 0.8 copy-start.1
  69.4 16.7 %copy-start = (f32[128,4096]{1,0:T(8,128)S(1)}, f32[128,4096]{1,0:T(8,128)}, u32[]{:S(2)}) copy-start(f32[128,4096]{1,0:T(8,128)} %inverse_ref.3) | copy-start | bytes 6291460
  70.6 15.6 %all-to-all-start.2 = ((f32[4,32,16,128]{3,2,1,0:T(8,128)}), f32[4,32,16,128]{3,2,1,0:T(8,128)S(1)}, u32[]{:S(2)}, u32[]{:S(2)}) async-start(f32[4,32,16,128]{3,2,1,0:T(8,128)} %broadcast_in_dim.31), calls=%async_computation.2 | async-start | bytes 2097152 | tf_op jit(solution)/shard_map/all_to_all | solution.py:25
  102.8 15.8 %all-to-all-start.4 = ((f32[16,2,512]{2,1,0:T(2,128)}), f32[16,2,512]{2,1,0:T(2,128)S(1)}, u32[]{:S(2)}, u32[]{:S(2)}) async-start(f32[16,2,512]{2,1,0:T(2,128)} %broadcast_in_dim.32), calls=%async_computation.4 | async-start | bytes 131072 | tf_op jit(solution)/shard_map/all_to_all | solution.py:25
  118.6 7.4 %copy-start.4 = (f32[16,2,512]{2,1,0:T(2,128)}, f32[16,2,512]{2,1,0:T(2,128)S(1)}, u32[]{:S(2)}) copy-start(f32[16,2,512]{2,1,0:T(2,128)S(1)} %all-to-all-done.4.vector_ref) | copy-start | bytes 196612
  159.4 33.0 %all-to-all-start.6 = ((f32[32,64,128]{2,1,0:T(8,128)}), f32[32,64,128]{2,1,0:T(8,128)S(1)}, u32[]{:S(2)}, u32[]{:S(2)}) async-start(f32[32,64,128]{2,1,0:T(8,128)} %spread.1), calls=%async_computation.6 | async-start | bytes 2097152 | tf_op jit(solution)/shard_map/all_to_all | solution.py:25
Sparse Core Ops, SparseCore 0:
  69.5 56.3 all-gather.2

commit v10 on v8

--- a/solution.py
+++ b/solution.py
@@ -43,7 +43,7 @@
 def gather_along_x(block):
     count = lax.axis_size("front")
     groups = [list(range(first, first + x_chips)) for first in range(0, count, x_chips)]
-    return lax.all_gather(block, "front", axis=0, axis_index_groups=groups)
+    return exchange(copies(block, x_chips), "front", groups)
 
 
 def split(value):
@@ -115,7 +115,7 @@
         ),
         in_specs=[vmem] * 3,
         out_specs=(vmem, vmem),
-        compiler_params=pltpu.CompilerParams(vmem_limit_bytes=32 * 1024 * 1024),
+        compiler_params=pltpu.CompilerParams(vmem_limit_bytes=16 * 1024 * 1024),
         cost_estimate=pl.CostEstimate(
             flops=8 * rhs * block * inverse_blocks.shape[1],
             bytes_accessed=4 * inverse_blocks.size + 4 * side.size,
@@ -152,7 +152,7 @@
         in_specs=[vmem] * 4,
         out_specs=vmem,
         scratch_shapes=[pltpu.VMEM((rhs, stacked.shape[0]), jnp.float32)],
-        compiler_params=pltpu.CompilerParams(vmem_limit_bytes=32 * 1024 * 1024),
+        compiler_params=pltpu.CompilerParams(vmem_limit_bytes=16 * 1024 * 1024),
         cost_estimate=pl.CostEstimate(
             flops=8 * rhs * block * inverse_blocks.shape[1],
             bytes_accessed=4 * inverse_blocks.size + 4 * rhs * inverse_blocks.shape[1],
@@ -243,7 +243,7 @@
             pltpu.VMEM((pairs, padded, rows), jnp.float32),
             pltpu.SemaphoreType.DMA((pairs,)),
         ],
-        compiler_params=pltpu.CompilerParams(vmem_limit_bytes=57 * 1024 * 1024),
+        compiler_params=pltpu.CompilerParams(vmem_limit_bytes=(56 * 1024 + 640) * 1024),
         cost_estimate=pl.CostEstimate(
             flops=12 * pairs * 16 * rows * rows,
             bytes_accessed=8 * pairs * rows * rows,
@@ -285,6 +285,7 @@
     c_pair = -product(c_high, c_low)
     g_pair = low[rows:] + product(c_low.T, lifted)
     pair_half = jnp.where(is_upper, g_pair, c_pair)
+    pair_half, side_chunk = lax.optimization_barrier((pair_half, side_chunk))
     coupling_all = gather_leaf(pair_half).reshape(leaf_count // 2, 2 * rows, rows)
 
     local_forward, vectors = run_forward(

time: 207 us -> 197 us (0.952)
  waiting for transfers between devices: 69.3 us -> 49.4 us
  blocking collectives: 75.7 us -> 87.3 us
  other arithmetic: 4.91 us -> 2.66 us
    all_to_all x3 -> x4, blocking collectives: 75.7 us -> 87.3 us  [exchange(): lax.all_to_all(blocks, axis, 0, 0, tiled=True, axis_index_groups=groups)]
    all_gather x1 -> x0, waiting for transfers between devices: 9.65 us -> none  [gather_along_x(): return lax.all_gather(block, 'front', axis=0, axis_index_groups=groups)]
    all_gather x1, waiting for transfers between devices: 8.27 us -> 0.01 us  [gather_leaf(): return lax.all_gather(block, 'leaf', axis=0)]
  transfers between devices with their start and end apart: 6 -> 5, of which waited for: 6 -> 4; matrix products, arithmetic and copies ran while one was open for 5% -> 4% of each run, Pallas kernels for 1% -> 1%
where the time goes in v10:
time: 197 us; the launch traced here: 196 us
  blocking collectives  87.3 us (44%)
  waiting for transfers between devices  49.4 us (25%)
  starting transfers between devices  19.5 us (10%)
  between operations  14.4 us (7%)
  Pallas kernels  9.58 us (5%)
  local copies, waits for them, and re-layouts  8.05 us (4%)
  matrix products  5.16 us (3%)
  other arithmetic  2.66 us (1%)
    all_to_all x4, blocking collectives, exchange(): lax.all_to_all(blocks, axis, 0, 0, tiled=True, axis_index_groups=groups)  87.3 us
    all_to_all x3, waiting for transfers between devices, exchange(): lax.all_to_all(blocks, axis, 0, 0, tiled=True, axis_index_groups=groups)  47.5 us
    all_to_all x3, starting transfers between devices, exchange(): lax.all_to_all(blocks, axis, 0, 0, tiled=True, axis_index_groups=groups)  17.5 us
    pallas_call x1, Pallas kernels, run_chain(): pl.pallas_call(chain_kernel, out_shape=jax.ShapeDtypeStruct((targets, sha...  6.51 us
    unnamed x22, local copies, waits for them, and re-layouts  4.04 us
    dot_general x5, matrix products, product(): jnp.dot(left, right, precision=exact, preferred_element_type=jnp.float32)  3.95 us
  transfers between devices with their start and end apart: 5, of which 4 were waited for; matrix products, arithmetic and copies ran while one was open for 4% of the time, Pallas kernels for 1%

profile of v10, /device:TPU:2, one launch (start us, length us, event | category | flops | bytes accessed | tf_op | source)
XLA Modules:
  0.0 196.0 jit_solution(8366191400233158061)
XLA Ops:
  7.2 1.9 copy.10
  9.2 0.7 gather_fusion
  10.8 35.7 %all_to_all.35 = f32[32,16,384]{2,1,0:T(8,128)S(1)} all-to-all(f32[32,16,384]{2,1,0:T(8,128)S(1)} %pad_maximum_fusion), channel_id=1, replica_groups=mesh['leaf'=16,'front'=32] {'front'}, dimensions={0} | all-to-all | bytes 1572864 | tf_op jit(solution)/shard_map/all_to_all | solution.py:24
  46.6 21.0 %all_to_all.36 = f32[32,16,256]{2,1,0:T(8,128)S(1)} all-to-all(f32[32,16,256]{2,1,0:T(8,128)S(1)} %broadcast_in_dim.30), channel_id=1, replica_groups=mesh['leaf'=16,'front'=32] {'front'}, dimensions={0} | all-to-all | bytes 1048576 | tf_op jit(solution)/shard_map/all_to_all | solution.py:24
  67.6 1.9 collective-permute-start
  69.6 1.9 collective-permute-done
  72.0 0.7 copy-done.4
  73.3 1.1 fusion.3
  74.4 1.1 broadcast_in_dim.31
  75.5 4.8 %all-to-all-start.2 = ((f32[4,32,16,128]{3,2,1,0:T(8,128)}), f32[4,32,16,128]{3,2,1,0:T(8,128)S(1)}, u32[]{:S(2)}, u32[]{:S(2)}) async-start(f32[4,32,16,128]{3,2,1,0:T(8,128)} %broadcast_in_dim.31), calls=%async_computation.2 | async-start | bytes 2097152 | tf_op jit(solution)/shard_map/all_to_all | solution.py:24
  80.3 1.0 pad_maximum_fusion.1.stacked_ref
  81.3 13.2 %all-to-all-done.2.side_ref = f32[4,32,16,128]{3,2,1,0:T(8,128)S(1)} async-done(((f32[4,32,16,128]{3,2,1,0:T(8,128)}), f32[4,32,16,128]{3,2,1,0:T(8,128)S(1)}, u32[]{:S(2)}, u32[]{:S(2)}) %all-to-all-start.2) | async-done | bytes 1048608 | tf_op jit(solution)/shard_map/all_to_all | solution.py:24
  94.5 1.1 forward.1
  95.6 14.0 %all_to_all.37 = f32[32,2,512]{2,1,0:T(2,128)S(1)} all-to-all(f32[32,2,512]{2,1,0:T(2,128)S(1)} %get-tuple-element.8), channel_id=1, replica_groups=mesh['leaf'=16,'front'=32] {'front'}, dimensions={0} | all-to-all | bytes 262144 | tf_op jit(solution)/shard_map/all_to_all | solution.py:24
  109.7 1.2 fusion
  110.9 1.3 add_select_fusion
  112.9 7.2 %all-to-all-start.4 = ((f32[16,2,1024]{2,1,0:T(2,128)}), f32[16,2,1024]{2,1,0:T(2,128)S(1)}, u32[]{:S(2)}, u32[]{:S(2)}) async-start(f32[16,2,1024]{2,1,0:T(2,128)} %broadcast_in_dim.32), calls=%async_computation.4 | async-start | bytes 262144 | tf_op jit(solution)/shard_map/all_to_all | solution.py:24
  120.8 1.3 constant_dynamic-slice_fusion.1
  122.1 6.8 %all-to-all-done.4.share_ref = f32[16,2,1024]{2,1,0:T(2,128)S(1)} async-done(((f32[16,2,1024]{2,1,0:T(2,128)}), f32[16,2,1024]{2,1,0:T(2,128)S(1)}, u32[]{:S(2)}, u32[]{:S(2)}) %all-to-all-start.4) | async-done | bytes 131104 | tf_op jit(solution)/shard_map/all_to_all | solution.py:24
  129.5 6.5 %chain.1 = f32[32,2,768]{2,1,0:T(2,128)} custom-call(s32[2]{0:T(128)} %pad_add_fusion.pos_ref, f32[8,512,256]{2,1,0:T(8,128)} %bitcast.15, f32[16,2,1024]{2,1,0:T(2,128)} %copy-done.6, f32[512,256]{1,0:T(8,128)} %copy-done.1, f32[512,256]{1,0:T(8,128)} %copy-done.2, f32[2,256]{1,0:T(2,128)} %get-tuple-element.13.below_ref, f32[2,256]{1,0:T(2,128)} %get-tuple-element.12.above_ref), custom_call_target="tpu_custom_call" | custom-call | flops 100663296 | bytes 4194304 | tf_op jit(solution)/shard_map/chain/pallas_call | solution.py:231
  136.1 16.6 %all_to_all.38.result_ref = f32[32,2,768]{2,1,0:T(2,128)S(1)} all-to-all(f32[32,2,768]{2,1,0:T(2,128)} %chain.1), channel_id=1, replica_groups=mesh['leaf'=16,'front'=32] {'front'}, dimensions={0} | all-to-all | bytes 393216 | tf_op jit(solution)/shard_map/all_to_all | solution.py:24
  152.7 1.9 spread.1
  154.6 5.5 %all-to-all-start.6 = ((f32[32,64,128]{2,1,0:T(8,128)}), f32[32,64,128]{2,1,0:T(8,128)S(1)}, u32[]{:S(2)}, u32[]{:S(2)}) async-start(f32[32,64,128]{2,1,0:T(8,128)} %spread.1), calls=%async_computation.6 | async-start | bytes 2097152 | tf_op jit(solution)/shard_map/all_to_all | solution.py:24
  161.0 27.5 %all-to-all-done.6 = f32[32,64,128]{2,1,0:T(8,128)S(1)} async-done(((f32[32,64,128]{2,1,0:T(8,128)}), f32[32,64,128]{2,1,0:T(8,128)S(1)}, u32[]{:S(2)}, u32[]{:S(2)}) %all-to-all-start.6) | async-done | bytes 1048608 | tf_op jit(solution)/shard_map/all_to_all | solution.py:24
  (45 shorter events, 5.6 us)
Async XLA Ops:
  7.2 2.0 %copy-start.9 = (s32[1,256]{1,0:T(1,128)S(1)}, s32[1,256]{1,0:T(1,128)}, u32[]{:S(2)}) copy-start(s32[1,256]{1,0:T(1,128)} %param.9) | copy-start | bytes 3076
  7.2 2.9 %copy-start.7 = (f32[256,128]{1,0:T(8,128)S(1)}, f32[256,128]{1,0:T(8,128)}, u32[]{:S(2)}) copy-start(f32[256,128]{1,0:T(8,128)} %param.8) | copy-start | bytes 393220
  7.2 121.7 %all-gather.3.cloned.1.call-start = ((), (), s32[]{:S(2)}) async-start(), calls=%async_computation.7 | async-start | bytes 4456448 | tf_op jit(solution)/shard_map/all_gather | solution.py:36
  9.2 1.5 copy-start.8
  10.1 0.7 copy-start.5
  46.5 25.0 %copy-start.3 = (f32[32,16,384]{2,1,0:T(8,128)}, f32[32,16,384]{2,1,0:T(8,128)S(1)}, u32[]{:S(2)}) copy-start(f32[32,16,384]{2,1,0:T(8,128)S(1)} %all_to_all.35) | copy-start | bytes 2359300
  67.6 3.8 %collective-permute-start = (f32[512,256]{1,0:T(8,128)S(1)}, f32[512,256]{1,0:T(8,128)S(1)}, u32[]{:S(2)}, u32[]{:S(2)}) collective-permute-start(f32[512,256]{1,0:T(8,128)S(1)} %bitcast.16), channel_id=1, source_target_pairs={{0,32},{32,0},{64,96},{96,64},{128,160},{160,128},{192,224},{224,1... | collective-permute-start | bytes 1572872 | tf_op jit(solution)/shard_map/ppermute | solution.py:280
  71.5 1.8 copy-start.1
  71.5 1.8 copy-start.2
  71.6 2.9 %slice-start = ((f32[32,16,384]{2,1,0:T(8,128)}), f32[32,16,128]{2,1,0:T(8,128)S(1)}, s32[]{:S(2)}) async-start(f32[32,16,384]{2,1,0:T(8,128)} %copy-done.3), calls=%async_computation.8 | async-start | bytes 524288 | tf_op jit(solution)/shard_map/slice | solution.py:276
  72.0 0.7 copy-start.4
  74.4 20.1 %copy-start = (f32[128,4096]{1,0:T(8,128)S(1)}, f32[128,4096]{1,0:T(8,128)}, u32[]{:S(2)}) copy-start(f32[128,4096]{1,0:T(8,128)} %inverse_ref.3) | copy-start | bytes 6291460
  75.5 19.0 %all-to-all-start.2 = ((f32[4,32,16,128]{3,2,1,0:T(8,128)}), f32[4,32,16,128]{3,2,1,0:T(8,128)S(1)}, u32[]{:S(2)}, u32[]{:S(2)}) async-start(f32[4,32,16,128]{3,2,1,0:T(8,128)} %broadcast_in_dim.31), calls=%async_computation.2 | async-start | bytes 2097152 | tf_op jit(solution)/shard_map/all_to_all | solution.py:24
  112.9 16.0 %all-to-all-start.4 = ((f32[16,2,1024]{2,1,0:T(2,128)}), f32[16,2,1024]{2,1,0:T(2,128)S(1)}, u32[]{:S(2)}, u32[]{:S(2)}) async-start(f32[16,2,1024]{2,1,0:T(2,128)} %broadcast_in_dim.32), calls=%async_computation.4 | async-start | bytes 262144 | tf_op jit(solution)/shard_map/all_to_all | solution.py:24
  128.9 0.7 copy-start.6
  154.6 33.8 %all-to-all-start.6 = ((f32[32,64,128]{2,1,0:T(8,128)}), f32[32,64,128]{2,1,0:T(8,128)S(1)}, u32[]{:S(2)}, u32[]{:S(2)}) async-start(f32[32,64,128]{2,1,0:T(8,128)} %spread.1), calls=%async_computation.6 | async-start | bytes 2097152 | tf_op jit(solution)/shard_map/all_to_all | solution.py:24
Sparse Core Ops, SparseCore 0:
  74.6 41.1 all-gather.2

commit v11 on v10

--- a/solution.py
+++ b/solution.py
@@ -8,6 +8,7 @@
 exact = lax.Precision.HIGHEST
 x_chips = 4
 padded = 8
+forward_weight = 1000
 
 
 def product(left, right):
@@ -117,7 +118,7 @@
         out_specs=(vmem, vmem),
         compiler_params=pltpu.CompilerParams(vmem_limit_bytes=16 * 1024 * 1024),
         cost_estimate=pl.CostEstimate(
-            flops=8 * rhs * block * inverse_blocks.shape[1],
+            flops=8 * rhs * block * inverse_blocks.shape[1] * forward_weight,
             bytes_accessed=4 * inverse_blocks.size + 4 * side.size,
             transcendentals=0,
         ),
@@ -275,6 +276,8 @@
     coupling = jnp.sum(arrived[:, :, :rows], axis=0)
     side_chunk = arrived[:, :, rows:]
     coupling = gather_front(coupling).reshape(2 * rows, rows)
+    coupling, side_chunk = lax.optimization_barrier((coupling, side_chunk))
+    side = gather_along_x(side_chunk)
 
     swap = [(s, s ^ 1) for s in range(leaf_count)]
     mate = lax.ppermute(coupling, "leaf", swap)
@@ -285,12 +288,9 @@
     c_pair = -product(c_high, c_low)
     g_pair = low[rows:] + product(c_low.T, lifted)
     pair_half = jnp.where(is_upper, g_pair, c_pair)
-    pair_half, side_chunk = lax.optimization_barrier((pair_half, side_chunk))
     coupling_all = gather_leaf(pair_half).reshape(leaf_count // 2, 2 * rows, rows)
 
-    local_forward, vectors = run_forward(
-        gather_along_x(side_chunk), inverse_blocks, stacked, front_count
-    )
+    local_forward, vectors = run_forward(side, inverse_blocks, stacked, front_count)
     vectors = jnp.sum(exchange(vectors), axis=0)
     u_own, w_own = (vectors[:, :rows], vectors[:, rows:])
     u_moved = -product_nt(u_own, c_high)

time: 197 us -> 194 us (0.985)
  blocking collectives: 87.3 us -> 66.5 us
  waiting for transfers between devices: 49.4 us -> 60.5 us
  starting transfers between devices: 19.5 us -> 25.9 us
    all_to_all x4 -> x3, blocking collectives: 87.3 us -> 66.5 us  [exchange(): lax.all_to_all(blocks, axis, 0, 0, tiled=True, axis_index_groups=groups)]
    all_to_all x3 -> x4, waiting for transfers between devices: 47.5 us -> 60.4 us  [exchange(): lax.all_to_all(blocks, axis, 0, 0, tiled=True, axis_index_groups=groups)]
    all_to_all x3 -> x4, starting transfers between devices: 17.5 us -> 24 us  [exchange(): lax.all_to_all(blocks, axis, 0, 0, tiled=True, axis_index_groups=groups)]
  transfers between devices with their start and end apart: 5 -> 6, of which waited for: 4 -> 4; matrix products, arithmetic and copies ran while one was open for 4% -> 5% of each run, Pallas kernels for 1% -> 1%
where the time goes in v11:
time: 194 us
  blocking collectives  66.5 us (34%)
  waiting for transfers between devices  60.5 us (31%)
  starting transfers between devices  25.9 us (13%)
  between operations  14.3 us (7%)
  Pallas kernels  10.9 us (6%)
  local copies, waits for them, and re-layouts  8.91 us (5%)
  matrix products  4.06 us (2%)
  other arithmetic  2.59 us (1%)
    all_to_all x3, blocking collectives, exchange(): lax.all_to_all(blocks, axis, 0, 0, tiled=True, axis_index_groups=groups)  66.5 us
    all_to_all x4, waiting for transfers between devices, exchange(): lax.all_to_all(blocks, axis, 0, 0, tiled=True, axis_index_groups=groups)  60.4 us
    all_to_all x4, starting transfers between devices, exchange(): lax.all_to_all(blocks, axis, 0, 0, tiled=True, axis_index_groups=groups)  24 us
    pallas_call x1, Pallas kernels, run_chain(): pl.pallas_call(chain_kernel, out_shape=jax.ShapeDtypeStruct((targets, sha...  6.51 us
    unnamed x22, local copies, waits for them, and re-layouts  4.05 us
  transfers between devices with their start and end apart: 6, of which 4 were waited for; matrix products, arithmetic and copies ran while one was open for 5% of the time, Pallas kernels for 1%

profile of v11, /device:TPU:2, one launch (start us, length us, event | category | flops | bytes accessed | tf_op | source)
XLA Modules:
  0.0 193.7 jit_solution(12555691025589828968)
XLA Ops:
  7.2 1.9 %copy.10 = f32[128,4096]{0,1:T(8,128)S(1)} copy(f32[128,4096]{1,0:T(8,128)} %inverse_ref.3) | data formatting | bytes 4194304 | tf_op args[1]
  9.2 0.7 gather_fusion
  10.7 35.7 %all_to_all.35 = f32[32,16,384]{2,1,0:T(8,128)S(1)} all-to-all(f32[32,16,384]{2,1,0:T(8,128)S(1)} %pad_maximum_fusion), channel_id=1, replica_groups=mesh['leaf'=16,'front'=32] {'front'}, dimensions={0} | all-to-all | bytes 1572864 | tf_op jit(solution)/shard_map/all_to_all | solution.py:25
  46.5 0.9 broadcast_in_dim.30
  47.4 5.6 %all-to-all-start.1 = ((f32[32,16,256]{2,1,0:T(8,128)}), f32[32,16,256]{2,1,0:T(8,128)S(1)}, u32[]{:S(2)}, u32[]{:S(2)}) async-start(f32[32,16,256]{2,1,0:T(8,128)} %broadcast_in_dim.30), calls=%async_computation.1 | async-start | bytes 1048576 | tf_op jit(solution)/shard_map/all_to_all | solution.py:25
  53.0 15.6 %all-to-all-done.1 = f32[32,16,256]{2,1,0:T(8,128)S(1)} async-done(((f32[32,16,256]{2,1,0:T(8,128)}), f32[32,16,256]{2,1,0:T(8,128)S(1)}, u32[]{:S(2)}, u32[]{:S(2)}) %all-to-all-start.1) | async-done | bytes 524320 | tf_op jit(solution)/shard_map/all_to_all | solution.py:25
  68.6 1.9 collective-permute-start
  70.5 1.1 broadcast_in_dim.31
  71.6 5.5 %all-to-all-start.2 = ((f32[4,32,16,128]{3,2,1,0:T(8,128)}), f32[4,32,16,128]{3,2,1,0:T(8,128)}, u32[]{:S(2)}, u32[]{:S(2)}) async-start(f32[4,32,16,128]{3,2,1,0:T(8,128)} %broadcast_in_dim.31), calls=%async_computation.2 | async-start | bytes 2097152 | tf_op jit(solution)/shard_map/all_to_all | solution.py:25
  77.6 0.7 copy-done.5
  78.9 1.1 fusion.3
  80.0 11.8 %all-to-all-done.2.side_ref = f32[4,32,16,128]{3,2,1,0:T(8,128)} async-done(((f32[4,32,16,128]{3,2,1,0:T(8,128)}), f32[4,32,16,128]{3,2,1,0:T(8,128)}, u32[]{:S(2)}, u32[]{:S(2)}) %all-to-all-start.2) | async-done | bytes 1048608 | tf_op jit(solution)/shard_map/all_to_all | solution.py:25
  91.8 2.4 %forward.1 = (f32[64,128]{1,0:T(8,128)S(1)}, f32[32,2,512]{2,1,0:T(2,128)S(1)}) custom-call(f32[4,32,16,128]{3,2,1,0:T(8,128)} %all-to-all-done.2.side_ref, f32[128,4096]{1,0:T(8,128)S(1)} %copy-done, f32[512,128]{1,0:T(8,128)S(1)} %pad_maximum_fusion.1.stacked_ref), custom_call_target="tpu_custom_call" | custom-call | flops 268435456000 | bytes 3145728 | tf_op jit(solution)/shard_map/forward/pallas_call | solution.py:111
  94.2 14.1 %all_to_all.36 = f32[32,2,512]{2,1,0:T(2,128)} all-to-all(f32[32,2,512]{2,1,0:T(2,128)S(1)} %get-tuple-element.8), channel_id=1, replica_groups=mesh['leaf'=16,'front'=32] {'front'}, dimensions={0} | all-to-all | bytes 262144 | tf_op jit(solution)/shard_map/all_to_all | solution.py:25
  108.3 1.0 reduce_sum.28
  109.6 1.2 add_select_fusion
  111.5 7.2 %all-to-all-start.4 = ((f32[16,2,1024]{2,1,0:T(2,128)}), f32[16,2,1024]{2,1,0:T(2,128)S(1)}, u32[]{:S(2)}, u32[]{:S(2)}) async-start(f32[16,2,1024]{2,1,0:T(2,128)} %broadcast_in_dim.32), calls=%async_computation.4 | async-start | bytes 262144 | tf_op jit(solution)/shard_map/all_to_all | solution.py:25
  119.4 1.3 constant_dynamic-slice_fusion.1
  120.7 6.8 %all-to-all-done.4.share_ref = f32[16,2,1024]{2,1,0:T(2,128)S(1)} async-done(((f32[16,2,1024]{2,1,0:T(2,128)}), f32[16,2,1024]{2,1,0:T(2,128)S(1)}, u32[]{:S(2)}, u32[]{:S(2)}) %all-to-all-start.4) | async-done | bytes 131104 | tf_op jit(solution)/shard_map/all_to_all | solution.py:25
  128.1 6.5 %chain.1 = f32[32,2,768]{2,1,0:T(2,128)} custom-call(s32[2]{0:T(128)} %pad_add_fusion.pos_ref, f32[8,512,256]{2,1,0:T(8,128)} %bitcast.13, f32[16,2,1024]{2,1,0:T(2,128)} %copy-done.6, f32[512,256]{1,0:T(8,128)} %copy-done.1, f32[512,256]{1,0:T(8,128)} %copy-done.3, f32[2,256]{1,0:T(2,128)} %get-tuple-element.13.below_ref, f32[2,256]{1,0:T(2,128)} %get-tuple-element.12.above_ref), custom_call_target="tpu_custom_call" | custom-call | flops 100663296 | bytes 4194304 | tf_op jit(solution)/shard_map/chain/pallas_call | solution.py:232
  134.7 16.6 %all_to_all.37.result_ref = f32[32,2,768]{2,1,0:T(2,128)S(1)} all-to-all(f32[32,2,768]{2,1,0:T(2,128)} %chain.1), channel_id=1, replica_groups=mesh['leaf'=16,'front'=32] {'front'}, dimensions={0} | all-to-all | bytes 393216 | tf_op jit(solution)/shard_map/all_to_all | solution.py:25
  151.3 1.9 %spread.1 = f32[32,64,128]{2,1,0:T(8,128)} custom-call(f32[32,2,768]{2,1,0:T(2,128)S(1)} %all_to_all.37.result_ref, f32[64,128]{1,0:T(8,128)S(1)} %get-tuple-element.9.forward_ref, f32[512,128]{1,0:T(8,128)S(1)} %pad_maximum_fusion.1.stacked_ref, f32[128,4096]{1,0:T(8,128)S(1)} %copy-done), custom_call_target="tpu_custom_call" | custom-call | flops 268435456 | bytes 3145728 | tf_op jit(solution)/shard_map/spread/pallas_call | solution.py:150
  153.3 5.8 %all-to-all-start.6 = ((f32[32,64,128]{2,1,0:T(8,128)}), f32[32,64,128]{2,1,0:T(8,128)S(1)}, u32[]{:S(2)}, u32[]{:S(2)}) async-start(f32[32,64,128]{2,1,0:T(8,128)} %spread.1), calls=%async_computation.6 | async-start | bytes 2097152 | tf_op jit(solution)/shard_map/all_to_all | solution.py:25
  159.9 26.2 %all-to-all-done.6 = f32[32,64,128]{2,1,0:T(8,128)S(1)} async-done(((f32[32,64,128]{2,1,0:T(8,128)}), f32[32,64,128]{2,1,0:T(8,128)S(1)}, u32[]{:S(2)}, u32[]{:S(2)}) %all-to-all-start.6) | async-done | bytes 1048608 | tf_op jit(solution)/shard_map/all_to_all | solution.py:25
  (45 shorter events, 5.8 us)
Async XLA Ops:
  7.2 2.0 %copy-start.9 = (s32[1,256]{1,0:T(1,128)S(1)}, s32[1,256]{1,0:T(1,128)}, u32[]{:S(2)}) copy-start(s32[1,256]{1,0:T(1,128)} %param.9) | copy-start | bytes 3076
  7.2 2.9 %copy-start.7 = (f32[256,128]{1,0:T(8,128)S(1)}, f32[256,128]{1,0:T(8,128)}, u32[]{:S(2)}) copy-start(f32[256,128]{1,0:T(8,128)} %param.8) | copy-start | bytes 393220
  9.1 1.5 copy-start.8
  47.4 21.2 %all-to-all-start.1 = ((f32[32,16,256]{2,1,0:T(8,128)}), f32[32,16,256]{2,1,0:T(8,128)S(1)}, u32[]{:S(2)}, u32[]{:S(2)}) async-start(f32[32,16,256]{2,1,0:T(8,128)} %broadcast_in_dim.30), calls=%async_computation.1 | async-start | bytes 1048576 | tf_op jit(solution)/shard_map/all_to_all | solution.py:25
  68.6 8.5 %collective-permute-start = (f32[512,256]{1,0:T(8,128)S(1)}, f32[512,256]{1,0:T(8,128)S(1)}, u32[]{:S(2)}, u32[]{:S(2)}) collective-permute-start(f32[512,256]{1,0:T(8,128)S(1)} %bitcast.14), channel_id=1, source_target_pairs={{0,32},{32,0},{64,96},{96,64},{128,160},{160,128},{192,224},{224,1... | collective-permute-start | bytes 1572872 | tf_op jit(solution)/shard_map/ppermute | solution.py:283
  71.6 20.2 %all-to-all-start.2 = ((f32[4,32,16,128]{3,2,1,0:T(8,128)}), f32[4,32,16,128]{3,2,1,0:T(8,128)}, u32[]{:S(2)}, u32[]{:S(2)}) async-start(f32[4,32,16,128]{3,2,1,0:T(8,128)} %broadcast_in_dim.31), calls=%async_computation.2 | async-start | bytes 2097152 | tf_op jit(solution)/shard_map/all_to_all | solution.py:25
  77.1 14.7 %copy-start = (f32[128,4096]{1,0:T(8,128)S(1)}, f32[128,4096]{1,0:T(8,128)}, u32[]{:S(2)}) copy-start(f32[128,4096]{1,0:T(8,128)} %inverse_ref.3) | copy-start | bytes 6291460
  77.1 50.4 %all-gather.3.cloned.1.call-start = ((), (), s32[]{:S(2)}) async-start(), calls=%async_computation.7 | async-start | bytes 4456448 | tf_op jit(solution)/shard_map/all_gather | solution.py:37
  77.2 1.7 copy-start.1
  77.2 1.7 copy-start.3
  77.6 0.7 copy-start.5
  91.8 17.5 %copy-start.4 = (f32[512,256]{1,0:T(8,128)S(1)}, f32[512,256]{1,0:T(8,128)}, u32[]{:S(2)}) copy-start(f32[512,256]{1,0:T(8,128)} %copy-done.3) | copy-start | bytes 1572868
  91.8 17.8 %copy-start.2 = (f32[512,256]{1,0:T(8,128)S(1)}, f32[512,256]{1,0:T(8,128)}, u32[]{:S(2)}) copy-start(f32[512,256]{1,0:T(8,128)} %copy-done.1) | copy-start | bytes 1572868
  111.5 16.0 %all-to-all-start.4 = ((f32[16,2,1024]{2,1,0:T(2,128)}), f32[16,2,1024]{2,1,0:T(2,128)S(1)}, u32[]{:S(2)}, u32[]{:S(2)}) async-start(f32[16,2,1024]{2,1,0:T(2,128)} %broadcast_in_dim.32), calls=%async_computation.4 | async-start | bytes 262144 | tf_op jit(solution)/shard_map/all_to_all | solution.py:25
  127.5 0.7 copy-start.6
  153.3 32.9 %all-to-all-start.6 = ((f32[32,64,128]{2,1,0:T(8,128)}), f32[32,64,128]{2,1,0:T(8,128)S(1)}, u32[]{:S(2)}, u32[]{:S(2)}) async-start(f32[32,64,128]{2,1,0:T(8,128)} %spread.1), calls=%async_computation.6 | async-start | bytes 2097152 | tf_op jit(solution)/shard_map/all_to_all | solution.py:25
Sparse Core Ops, SparseCore 0:
  80.1 41.9 all-gather.2

commit v12 on v11

--- a/solution.py
+++ b/solution.py
@@ -35,10 +35,6 @@
 
 def gather_leaf(block):
     return lax.all_gather(block, "leaf", axis=0)
-
-
-def gather_leaf_small(block):
-    return exchange(copies(block, lax.axis_size("leaf")), "leaf")
 
 
 def gather_along_x(block):
@@ -163,9 +159,49 @@
     )(result, forward, stacked, inverse_blocks)
 
 
+def share_kernel(pos_ref, arrived_ref, high_ref, moved_ref, out_ref, held):
+    share, width = arrived_ref.shape[1:]
+    rows = width // 2
+    held[...] = jnp.zeros_like(held)
+    held[:share, :] = jnp.sum(arrived_ref[...], axis=0)
+    vectors = held[...]
+    own_u, own_w = vectors[:, :rows], vectors[:, rows:]
+    is_upper = pos_ref[1] == 1
+    u_moved = -dot_parts(two_parts(own_u), *split(high_ref[...]), 1)
+    turned = two_parts(jnp.where(is_upper, own_w, own_u))
+    w_moved = dot_parts(turned, *split(moved_ref[...]), 0)
+    kept = jnp.concatenate(
+        [
+            jnp.where(is_upper, own_u, u_moved),
+            jnp.where(is_upper, w_moved, own_w + w_moved),
+            vectors,
+        ],
+        axis=1,
+    )[:share]
+    for piece in range(out_ref.shape[0]):
+        out_ref[piece] = kept
+
+
+def run_share(position, arrived, c_high, moved, targets):
+    share, width = arrived.shape[1:]
+    vmem = pl.BlockSpec(memory_space=pltpu.VMEM)
+    return pl.pallas_call(
+        share_kernel,
+        out_shape=jax.ShapeDtypeStruct((targets, share, 2 * width), jnp.float32),
+        in_specs=[pl.BlockSpec(memory_space=pltpu.SMEM)] + [vmem] * 3,
+        out_specs=vmem,
+        scratch_shapes=[pltpu.VMEM((padded, width), jnp.float32)],
+        compiler_params=pltpu.CompilerParams(vmem_limit_bytes=16 * 1024 * 1024),
+        cost_estimate=pl.CostEstimate(
+            flops=128 * width * width, bytes_accessed=8 * width * width, transcendentals=0
+        ),
+        name="share",
+    )(position, arrived, c_high, moved)
+
+
 def chain_kernel(
     pos_ref, coupling_ref, share_ref, low_ref, high_ref, below_ref, above_ref, out_ref,
-    held, head, tail, vectors, into, above, sems,
+    held, own, head, tail, vectors, into, above, sems,
 ):
     pairs = held.shape[0]
     share, rows = below_ref.shape
@@ -175,6 +211,10 @@
 
     for y in range(pairs):
         fetch(y).start()
+    own_low = pltpu.make_async_copy(low_ref, own.at[0], sems.at[pairs])
+    own_high = pltpu.make_async_copy(high_ref, own.at[1], sems.at[pairs + 1])
+    own_low.start()
+    own_high.start()
     vectors[...] = jnp.zeros_like(vectors)
     into[0] = jnp.zeros_like(into[0])
     above[pairs - 1] = jnp.zeros_like(into[0])
@@ -187,8 +227,6 @@
     into[0, :share, :] = below_ref[...]
     above[pairs - 1, :share, :] = above_ref[...]
 
-    low_head, low_tail = split(low_ref[:rows])
-    high_head, high_tail = split(high_ref[...])
     incoming = into[0]
     for y in range(pairs):
         fetch(y).wait()
@@ -206,6 +244,10 @@
         from_above = vectors[y, :, rows:] - taken
         above[y - 1] = from_above
 
+    own_low.wait()
+    own_high.wait()
+    low_head, low_tail = split(own[0, :rows])
+    high_head, high_tail = split(own[1])
     incoming = into[chip]
     from_above = above[chip]
     middle = vectors[pairs, :, :rows] - dot_parts(two_parts(incoming), low_head, low_tail, 1)
@@ -229,20 +271,21 @@
     share, rows = below.shape
     pairs = coupling_all.shape[0]
     vmem = pl.BlockSpec(memory_space=pltpu.VMEM)
+    hbm = pl.BlockSpec(memory_space=pltpu.HBM)
     return pl.pallas_call(
         chain_kernel,
         out_shape=jax.ShapeDtypeStruct((targets, share, 3 * rows), jnp.float32),
-        in_specs=[pl.BlockSpec(memory_space=pltpu.SMEM), pl.BlockSpec(memory_space=pltpu.HBM)]
-        + [vmem] * 5,
+        in_specs=[pl.BlockSpec(memory_space=pltpu.SMEM), hbm, vmem, hbm, hbm, vmem, vmem],
         out_specs=vmem,
         scratch_shapes=[
             pltpu.VMEM((pairs, 2 * rows, rows), jnp.float32),
+            pltpu.VMEM((2, 2 * rows, rows), jnp.float32),
             pltpu.VMEM((pairs, rows, rows), jnp.bfloat16),
             pltpu.VMEM((pairs, rows, rows), jnp.bfloat16),
             pltpu.VMEM((pairs + 2, padded, 2 * rows), jnp.float32),
             pltpu.VMEM((pairs, padded, rows), jnp.float32),
             pltpu.VMEM((pairs, padded, rows), jnp.float32),
-            pltpu.SemaphoreType.DMA((pairs,)),
+            pltpu.SemaphoreType.DMA((pairs + 2,)),
         ],
         compiler_params=pltpu.CompilerParams(vmem_limit_bytes=(56 * 1024 + 640) * 1024),
         cost_estimate=pl.CostEstimate(
@@ -291,23 +334,12 @@
     coupling_all = gather_leaf(pair_half).reshape(leaf_count // 2, 2 * rows, rows)
 
     local_forward, vectors = run_forward(side, inverse_blocks, stacked, front_count)
-    vectors = jnp.sum(exchange(vectors), axis=0)
-    u_own, w_own = (vectors[:, :rows], vectors[:, rows:])
-    u_moved = -product_nt(u_own, c_high)
-    w_moved = product(jnp.where(is_upper, w_own, u_own), jnp.where(is_upper, -c_low, lifted))
-    own_share = jnp.concatenate(
-        [
-            jnp.where(is_upper, u_own, u_moved),
-            jnp.where(is_upper, w_moved, w_own + w_moved),
-            vectors,
-        ],
-        axis=1,
-    )
-    shares = gather_leaf_small(own_share)
+    position = jnp.stack([leaf_pos // 2, leaf_pos % 2])
+    moved = jnp.where(is_upper, -c_low, lifted)
+    shares = exchange(run_share(position, exchange(vectors), c_high, moved, leaf_count), "leaf")
 
     below_rows = lax.dynamic_slice_in_dim(below_update, front_pos * share, share, 0)
     above_rows = lax.dynamic_slice_in_dim(above_solution, front_pos * share, share, 0)
-    position = jnp.stack([leaf_pos // 2, leaf_pos % 2])
     result = exchange(
         run_chain(
             position, coupling_all, shares, low, high,

time: 194 us -> 195 us (level)
  blocking collectives: 66.5 us -> 53.8 us
  waiting for transfers between devices: 60.5 us -> 69.8 us
  starting transfers between devices: 25.9 us -> 31.1 us
  Pallas kernels: 10.9 us -> 12.9 us
    all_to_all x3 -> x2, blocking collectives: 66.5 us -> 53.8 us  [exchange(): lax.all_to_all(blocks, axis, 0, 0, tiled=True, axis_index_groups=groups)]
    all_to_all x4 -> x5, waiting for transfers between devices: 60.4 us -> 69.8 us  [exchange(): lax.all_to_all(blocks, axis, 0, 0, tiled=True, axis_index_groups=groups)]
    all_to_all x4 -> x5, starting transfers between devices: 24 us -> 29.2 us  [exchange(): lax.all_to_all(blocks, axis, 0, 0, tiled=True, axis_index_groups=groups)]
    unnamed x22 -> x18, local copies, waits for them, and re-layouts: 4.05 us -> 3.31 us
  transfers between devices with their start and end apart: 6 -> 7, of which waited for: 4 -> 5; matrix products, arithmetic and copies ran while one was open for 5% -> 3% of each run, Pallas kernels for 1% -> 2%
where the time goes in v12:
time: 195 us; the launch traced here: 194 us
  waiting for transfers between devices  69.8 us (36%)
  blocking collectives  53.8 us (28%)
  starting transfers between devices  31.1 us (16%)
  between operations  14.3 us (7%)
  Pallas kernels  12.9 us (7%)
  local copies, waits for them, and re-layouts  8.44 us (4%)
  matrix products  2.65 us (1%)
    all_to_all x5, waiting for transfers between devices, exchange(): lax.all_to_all(blocks, axis, 0, 0, tiled=True, axis_index_groups=groups)  69.8 us
    all_to_all x2, blocking collectives, exchange(): lax.all_to_all(blocks, axis, 0, 0, tiled=True, axis_index_groups=groups)  53.8 us
    all_to_all x5, starting transfers between devices, exchange(): lax.all_to_all(blocks, axis, 0, 0, tiled=True, axis_index_groups=groups)  29.2 us
    pallas_call x1, Pallas kernels, run_chain(): pl.pallas_call(chain_kernel, out_shape=jax.ShapeDtypeStruct((targets, sha...  6.47 us
  transfers between devices with their start and end apart: 7, of which 5 were waited for; matrix products, arithmetic and copies ran while one was open for 3% of the time, Pallas kernels for 2%

profile of v12, /device:TPU:2, one launch (start us, length us, event | category | flops | bytes accessed | tf_op | source)
XLA Modules:
  0.0 194.2 jit_solution(18189833873819702985)
XLA Ops:
  7.2 1.9 %copy.10 = f32[128,4096]{0,1:T(8,128)S(1)} copy(f32[128,4096]{1,0:T(8,128)} %inverse_ref.3) | data formatting | bytes 4194304 | tf_op args[1]
  9.2 0.7 gather_fusion
  10.7 35.7 %all_to_all.35 = f32[32,16,384]{2,1,0:T(8,128)S(1)} all-to-all(f32[32,16,384]{2,1,0:T(8,128)S(1)} %pad_maximum_fusion), channel_id=1, replica_groups=mesh['leaf'=16,'front'=32] {'front'}, dimensions={0} | all-to-all | bytes 1572864 | tf_op jit(solution)/shard_map/all_to_all | solution.py:25
  46.5 0.9 broadcast_in_dim.24
  47.3 5.6 %all-to-all-start.1 = ((f32[32,16,256]{2,1,0:T(8,128)}), f32[32,16,256]{2,1,0:T(8,128)S(1)}, u32[]{:S(2)}, u32[]{:S(2)}) async-start(f32[32,16,256]{2,1,0:T(8,128)} %broadcast_in_dim.24), calls=%async_computation.1 | async-start | bytes 1048576 | tf_op jit(solution)/shard_map/all_to_all | solution.py:25
  52.9 15.6 %all-to-all-done.1 = f32[32,16,256]{2,1,0:T(8,128)S(1)} async-done(((f32[32,16,256]{2,1,0:T(8,128)}), f32[32,16,256]{2,1,0:T(8,128)S(1)}, u32[]{:S(2)}, u32[]{:S(2)}) %all-to-all-start.1) | async-done | bytes 524320 | tf_op jit(solution)/shard_map/all_to_all | solution.py:25
  68.6 1.9 collective-permute-start
  70.5 1.1 broadcast_in_dim.25
  71.6 5.5 %all-to-all-start.2 = ((f32[4,32,16,128]{3,2,1,0:T(8,128)}), f32[4,32,16,128]{3,2,1,0:T(8,128)}, u32[]{:S(2)}, u32[]{:S(2)}) async-start(f32[4,32,16,128]{3,2,1,0:T(8,128)} %broadcast_in_dim.25), calls=%async_computation.2 | async-start | bytes 2097152 | tf_op jit(solution)/shard_map/all_to_all | solution.py:25
  78.2 1.1 fusion.2
  79.4 12.4 %all-to-all-done.2.side_ref = f32[4,32,16,128]{3,2,1,0:T(8,128)} async-done(((f32[4,32,16,128]{3,2,1,0:T(8,128)}), f32[4,32,16,128]{3,2,1,0:T(8,128)}, u32[]{:S(2)}, u32[]{:S(2)}) %all-to-all-start.2) | async-done | bytes 1048608 | tf_op jit(solution)/shard_map/all_to_all | solution.py:25
  91.8 3.0 %forward.1 = (f32[64,128]{1,0:T(8,128)S(1)}, f32[32,2,512]{2,1,0:T(2,128)}) custom-call(f32[4,32,16,128]{3,2,1,0:T(8,128)} %all-to-all-done.2.side_ref, f32[128,4096]{1,0:T(8,128)S(1)} %copy-done, f32[512,128]{1,0:T(8,128)S(1)} %pad_maximum_fusion.1.stacked_ref), custom_call_target="tpu_custom_call" | custom-call | flops 268435456000 | bytes 3145728 | tf_op jit(solution)/shard_map/forward/pallas_call | solution.py:107
  94.8 5.3 %all-to-all-start.3 = ((f32[32,2,512]{2,1,0:T(2,128)}), f32[32,2,512]{2,1,0:T(2,128)S(1)}, u32[]{:S(2)}, u32[]{:S(2)}) async-start(f32[32,2,512]{2,1,0:T(2,128)} %get-tuple-element.8), calls=%async_computation.3 | async-start | bytes 262144 | tf_op jit(solution)/shard_map/all_to_all | solution.py:25
  100.2 1.0 slice.35.high_ref
  101.2 7.8 %all-to-all-done.3.arrived_ref = f32[32,2,512]{2,1,0:T(2,128)S(1)} async-done(((f32[32,2,512]{2,1,0:T(2,128)}), f32[32,2,512]{2,1,0:T(2,128)S(1)}, u32[]{:S(2)}, u32[]{:S(2)}) %all-to-all-start.3) | async-done | bytes 131104 | tf_op jit(solution)/shard_map/all_to_all | solution.py:25
  109.0 1.5 share.1
  110.5 7.2 %all-to-all-start.4 = ((f32[16,2,1024]{2,1,0:T(2,128)}), f32[16,2,1024]{2,1,0:T(2,128)S(1)}, u32[]{:S(2)}, u32[]{:S(2)}) async-start(f32[16,2,1024]{2,1,0:T(2,128)} %share.1), calls=%async_computation.4 | async-start | bytes 262144 | tf_op jit(solution)/shard_map/all_to_all | solution.py:25
  117.7 1.3 constant_dynamic-slice_fusion.1
  119.1 7.4 %all-to-all-done.4.share_ref = f32[16,2,1024]{2,1,0:T(2,128)S(1)} async-done(((f32[16,2,1024]{2,1,0:T(2,128)}), f32[16,2,1024]{2,1,0:T(2,128)S(1)}, u32[]{:S(2)}, u32[]{:S(2)}) %all-to-all-start.4) | async-done | bytes 131104 | tf_op jit(solution)/shard_map/all_to_all | solution.py:25
  127.2 6.5 %chain.1 = f32[32,2,768]{2,1,0:T(2,128)} custom-call(s32[2]{0:T(128)} %copy-done.1, f32[8,512,256]{2,1,0:T(8,128)} %bitcast.13, f32[16,2,1024]{2,1,0:T(2,128)} %copy-done.4, f32[512,256]{1,0:T(8,128)} %copy-done.2, f32[512,256]{1,0:T(8,128)} %copy-done.3, f32[2,256]{1,0:T(2,128)} %get-tuple-element.15.below_ref, f32[2,256]{1,0:T(2,128)} %get-tuple-element.14.above_ref), custom_call_target="tpu_custom_call" | custom-call | flops 100663296 | bytes 4194304 | tf_op jit(solution)/shard_map/chain/pallas_call | solution.py:275
  133.6 18.1 %all_to_all.36.result_ref = f32[32,2,768]{2,1,0:T(2,128)S(1)} all-to-all(f32[32,2,768]{2,1,0:T(2,128)} %chain.1), channel_id=1, replica_groups=mesh['leaf'=16,'front'=32] {'front'}, dimensions={0} | all-to-all | bytes 393216 | tf_op jit(solution)/shard_map/all_to_all | solution.py:25
  151.7 1.9 %spread.1 = f32[32,64,128]{2,1,0:T(8,128)} custom-call(f32[32,2,768]{2,1,0:T(2,128)S(1)} %all_to_all.36.result_ref, f32[64,128]{1,0:T(8,128)S(1)} %get-tuple-element.9.forward_ref, f32[512,128]{1,0:T(8,128)S(1)} %pad_maximum_fusion.1.stacked_ref, f32[128,4096]{1,0:T(8,128)S(1)} %copy-done), custom_call_target="tpu_custom_call" | custom-call | flops 268435456 | bytes 3145728 | tf_op jit(solution)/shard_map/spread/pallas_call | solution.py:146
  153.7 5.7 %all-to-all-start.6 = ((f32[32,64,128]{2,1,0:T(8,128)}), f32[32,64,128]{2,1,0:T(8,128)S(1)}, u32[]{:S(2)}, u32[]{:S(2)}) async-start(f32[32,64,128]{2,1,0:T(8,128)} %spread.1), calls=%async_computation.6 | async-start | bytes 2097152 | tf_op jit(solution)/shard_map/all_to_all | solution.py:25
  160.2 26.5 %all-to-all-done.6 = f32[32,64,128]{2,1,0:T(8,128)S(1)} async-done(((f32[32,64,128]{2,1,0:T(8,128)}), f32[32,64,128]{2,1,0:T(8,128)S(1)}, u32[]{:S(2)}, u32[]{:S(2)}) %all-to-all-start.6) | async-done | bytes 1048608 | tf_op jit(solution)/shard_map/all_to_all | solution.py:25
  (39 shorter events, 4.2 us)
Async XLA Ops:
  7.2 2.0 %copy-start.7 = (s32[1,256]{1,0:T(1,128)S(1)}, s32[1,256]{1,0:T(1,128)}, u32[]{:S(2)}) copy-start(s32[1,256]{1,0:T(1,128)} %param.9) | copy-start | bytes 3076
  7.2 2.9 %copy-start.5 = (f32[256,128]{1,0:T(8,128)S(1)}, f32[256,128]{1,0:T(8,128)}, u32[]{:S(2)}) copy-start(f32[256,128]{1,0:T(8,128)} %param.8) | copy-start | bytes 393220
  9.1 1.5 copy-start.6
  47.3 21.2 %all-to-all-start.1 = ((f32[32,16,256]{2,1,0:T(8,128)}), f32[32,16,256]{2,1,0:T(8,128)S(1)}, u32[]{:S(2)}, u32[]{:S(2)}) async-start(f32[32,16,256]{2,1,0:T(8,128)} %broadcast_in_dim.24), calls=%async_computation.1 | async-start | bytes 1048576 | tf_op jit(solution)/shard_map/all_to_all | solution.py:25
  68.6 8.5 %collective-permute-start = (f32[512,256]{1,0:T(8,128)S(1)}, f32[512,256]{1,0:T(8,128)S(1)}, u32[]{:S(2)}, u32[]{:S(2)}) collective-permute-start(f32[512,256]{1,0:T(8,128)S(1)} %bitcast.14), channel_id=1, source_target_pairs={{0,32},{32,0},{64,96},{96,64},{128,160},{160,128},{192,224},{224,1... | collective-permute-start | bytes 1572872 | tf_op jit(solution)/shard_map/ppermute | solution.py:326
  71.6 20.2 %all-to-all-start.2 = ((f32[4,32,16,128]{3,2,1,0:T(8,128)}), f32[4,32,16,128]{3,2,1,0:T(8,128)}, u32[]{:S(2)}, u32[]{:S(2)}) async-start(f32[4,32,16,128]{3,2,1,0:T(8,128)} %broadcast_in_dim.25), calls=%async_computation.2 | async-start | bytes 2097152 | tf_op jit(solution)/shard_map/all_to_all | solution.py:25
  77.1 49.4 %all-gather.3.cloned.1.call-start = ((), (), s32[]{:S(2)}) async-start(), calls=%async_computation.7 | async-start | bytes 4456448 | tf_op jit(solution)/shard_map/all_gather | solution.py:37
  77.2 1.0 copy-start.2
  77.2 1.0 copy-start.3
  77.2 14.6 %copy-start = (f32[128,4096]{1,0:T(8,128)S(1)}, f32[128,4096]{1,0:T(8,128)}, u32[]{:S(2)}) copy-start(f32[128,4096]{1,0:T(8,128)} %inverse_ref.3) | copy-start | bytes 6291460
  94.8 14.2 %all-to-all-start.3 = ((f32[32,2,512]{2,1,0:T(2,128)}), f32[32,2,512]{2,1,0:T(2,128)S(1)}, u32[]{:S(2)}, u32[]{:S(2)}) async-start(f32[32,2,512]{2,1,0:T(2,128)} %get-tuple-element.8), calls=%async_computation.3 | async-start | bytes 262144 | tf_op jit(solution)/shard_map/all_to_all | solution.py:25
  100.2 26.3 %copy-start.1 = (s32[2]{0:T(128)}, s32[2]{0:T(128)S(1)}, u32[]{:S(2)}) copy-start(s32[2]{0:T(128)S(1)} %pad_add_fusion.pos_ref) | copy-start | bytes 28
  110.5 16.0 %all-to-all-start.4 = ((f32[16,2,1024]{2,1,0:T(2,128)}), f32[16,2,1024]{2,1,0:T(2,128)S(1)}, u32[]{:S(2)}, u32[]{:S(2)}) async-start(f32[16,2,1024]{2,1,0:T(2,128)} %share.1), calls=%async_computation.4 | async-start | bytes 262144 | tf_op jit(solution)/shard_map/all_to_all | solution.py:25
  126.5 0.7 copy-start.4
  153.7 33.0 %all-to-all-start.6 = ((f32[32,64,128]{2,1,0:T(8,128)}), f32[32,64,128]{2,1,0:T(8,128)S(1)}, u32[]{:S(2)}, u32[]{:S(2)}) async-start(f32[32,64,128]{2,1,0:T(8,128)} %spread.1), calls=%async_computation.6 | async-start | bytes 2097152 | tf_op jit(solution)/shard_map/all_to_all | solution.py:25
Sparse Core Ops, SparseCore 0:
  80.0 41.9 all-gather.2

commit v13 on v12

--- a/solution.py
+++ b/solution.py
@@ -37,10 +37,10 @@
     return lax.all_gather(block, "leaf", axis=0)
 
 
-def gather_along_x(block):
+def turn_along_x(block, steps):
     count = lax.axis_size("front")
-    groups = [list(range(first, first + x_chips)) for first in range(0, count, x_chips)]
-    return exchange(copies(block, x_chips), "front", groups)
+    pairs = [(f, f - f % x_chips + (f + steps) % x_chips) for f in range(count)]
+    return lax.ppermute(block, "front", pairs)
 
 
 def split(value):
@@ -72,8 +72,11 @@
     return jnp.concatenate([head, tail], axis=1)
 
 
-def forward_kernel(side_ref, inverse_ref, stacked_ref, forward_ref, vector_ref):
+def forward_kernel(pos_ref, inverse_ref, stacked_ref, *refs):
+    pieces, (forward_ref, vector_ref, side_ref) = refs[:-3], refs[-3:]
     chunks, blocks, chunk, block = side_ref.shape
+    for steps, piece in enumerate(pieces):
+        side_ref[lax.rem(pos_ref[0] + chunks - steps, chunks)] = piece[...]
     rhs = chunks * chunk
     group = 4
     nt = (((1,), (1,)), ((), ()))
@@ -100,8 +103,9 @@
         vector_ref[piece] = vectors[piece * share : (piece + 1) * share]
 
 
-def run_forward(side, inverse_blocks, stacked, targets):
-    rhs = side.shape[0] * side.shape[2]
+def run_forward(x_pos, pieces, inverse_blocks, stacked, targets):
+    side_shape = (len(pieces), *pieces[0].shape)
+    rhs = side_shape[0] * side_shape[2]
     block = inverse_blocks.shape[0]
     vmem = pl.BlockSpec(memory_space=pltpu.VMEM)
     return pl.pallas_call(
@@ -110,16 +114,17 @@
             jax.ShapeDtypeStruct((rhs, block), jnp.float32),
             jax.ShapeDtypeStruct((targets, rhs // targets, stacked.shape[0]), jnp.float32),
         ),
-        in_specs=[vmem] * 3,
+        in_specs=[pl.BlockSpec(memory_space=pltpu.SMEM)] + [vmem] * (2 + len(pieces)),
         out_specs=(vmem, vmem),
+        scratch_shapes=[pltpu.VMEM(side_shape, jnp.float32)],
         compiler_params=pltpu.CompilerParams(vmem_limit_bytes=16 * 1024 * 1024),
         cost_estimate=pl.CostEstimate(
             flops=8 * rhs * block * inverse_blocks.shape[1] * forward_weight,
-            bytes_accessed=4 * inverse_blocks.size + 4 * side.size,
+            bytes_accessed=4 * inverse_blocks.size + 16 * pieces[0].size,
             transcendentals=0,
         ),
         name="forward",
-    )(side, inverse_blocks, stacked)
+    )(x_pos.reshape(1), inverse_blocks, stacked, *pieces)
 
 
 def spread_kernel(result_ref, forward_ref, stacked_ref, inverse_ref, out_ref, held):
@@ -319,8 +324,8 @@
     coupling = jnp.sum(arrived[:, :, :rows], axis=0)
     side_chunk = arrived[:, :, rows:]
     coupling = gather_front(coupling).reshape(2 * rows, rows)
-    coupling, side_chunk = lax.optimization_barrier((coupling, side_chunk))
-    side = gather_along_x(side_chunk)
+    turned = [turn_along_x(side_chunk, steps) for steps in range(1, x_chips)]
+    coupling, *turned = lax.optimization_barrier((coupling, *turned))
 
     swap = [(s, s ^ 1) for s in range(leaf_count)]
     mate = lax.ppermute(coupling, "leaf", swap)
@@ -333,7 +338,9 @@
     pair_half = jnp.where(is_upper, g_pair, c_pair)
     coupling_all = gather_leaf(pair_half).reshape(leaf_count // 2, 2 * rows, rows)
 
-    local_forward, vectors = run_forward(side, inverse_blocks, stacked, front_count)
+    local_forward, vectors = run_forward(
+        front_pos % x_chips, [side_chunk, *turned], inverse_blocks, stacked, front_count
+    )
     position = jnp.stack([leaf_pos // 2, leaf_pos % 2])
     moved = jnp.where(is_upper, -c_low, lifted)
     shares = exchange(run_share(position, exchange(vectors), c_high, moved, leaf_count), "leaf")

time: 195 us -> 198 us (1.015)
  starting transfers between devices: 31.1 us -> 38.5 us
  waiting for transfers between devices: 69.8 us -> 63.2 us
  blocking collectives: 53.8 us -> 56.1 us
    all_to_all x5 -> x4, waiting for transfers between devices: 69.8 us -> 43.2 us  [exchange(): lax.all_to_all(blocks, axis, 0, 0, tiled=True, axis_index_groups=groups)]
    ppermute x0 -> x3, waiting for transfers between devices: none -> 11.2 us  [turn_along_x(): return lax.ppermute(block, 'front', pairs)]
    ppermute x0 -> x3, starting transfers between devices: none -> 10.4 us  [turn_along_x(): return lax.ppermute(block, 'front', pairs)]
    all_gather x1, waiting for transfers between devices: 0.01 us -> 6.97 us  [gather_leaf(): return lax.all_gather(block, 'leaf', axis=0)]
    all_to_all x5 -> x4, starting transfers between devices: 29.2 us -> 26.1 us  [exchange(): lax.all_to_all(blocks, axis, 0, 0, tiled=True, axis_index_groups=groups)]
    all_to_all x2, blocking collectives: 53.8 us -> 56.1 us  [exchange(): lax.all_to_all(blocks, axis, 0, 0, tiled=True, axis_index_groups=groups)]
    unnamed x18 -> x26, local copies, waits for them, and re-layouts: 3.31 us -> 5.25 us
  transfers between devices with their start and end apart: 7 -> 9, of which waited for: 5 -> 8; matrix products, arithmetic and copies ran while one was open for 3% -> 2% of each run, Pallas kernels for 2% -> 2%
where the time goes in v13:
time: 198 us; the launch traced here: 197 us
  waiting for transfers between devices  63.2 us (32%)
  blocking collectives  56.1 us (28%)
  starting transfers between devices  38.5 us (19%)
  between operations  14.4 us (7%)
  Pallas kernels  11.7 us (6%)
  local copies, waits for them, and re-layouts  9.3 us (5%)
  matrix products  2.66 us (1%)
    all_to_all x2, blocking collectives, exchange(): lax.all_to_all(blocks, axis, 0, 0, tiled=True, axis_index_groups=groups)  56.1 us
    all_to_all x4, waiting for transfers between devices, exchange(): lax.all_to_all(blocks, axis, 0, 0, tiled=True, axis_index_groups=groups)  43.2 us
    all_to_all x4, starting transfers between devices, exchange(): lax.all_to_all(blocks, axis, 0, 0, tiled=True, axis_index_groups=groups)  26.1 us
    ppermute x3, waiting for transfers between devices, turn_along_x(): return lax.ppermute(block, 'front', pairs)  11.2 us
    ppermute x3, starting transfers between devices, turn_along_x(): return lax.ppermute(block, 'front', pairs)  10.4 us
    all_gather x1, waiting for transfers between devices, gather_leaf(): return lax.all_gather(block, 'leaf', axis=0)  6.97 us
    pallas_call x1, Pallas kernels, run_chain(): pl.pallas_call(chain_kernel, out_shape=jax.ShapeDtypeStruct((targets, sha...  6.47 us
    unnamed x26, local copies, waits for them, and re-layouts  5.25 us
  transfers between devices with their start and end apart: 9, of which 8 were waited for; matrix products, arithmetic and copies ran while one was open for 2% of the time, Pallas kernels for 2%

profile of v13, /device:TPU:2, one launch (start us, length us, event | category | flops | bytes accessed | tf_op | source)
XLA Modules:
  0.0 196.9 jit_solution(14154064883940550141)
XLA Ops:
  7.2 1.9 copy.10
  10.7 35.7 %all_to_all.30 = f32[32,16,384]{2,1,0:T(8,128)S(1)} all-to-all(f32[32,16,384]{2,1,0:T(8,128)S(1)} %pad_maximum_fusion), channel_id=1, replica_groups=mesh['leaf'=16,'front'=32] {'front'}, dimensions={0} | all-to-all | bytes 1572864 | tf_op jit(solution)/shard_map/all_to_all | solution.py:25
  47.4 5.6 %all-to-all-start.1 = ((f32[32,16,256]{2,1,0:T(8,128)}), f32[32,16,256]{2,1,0:T(8,128)S(1)}, u32[]{:S(2)}, u32[]{:S(2)}) async-start(f32[32,16,256]{2,1,0:T(8,128)} %broadcast_in_dim.18), calls=%async_computation.1 | async-start | bytes 1048576 | tf_op jit(solution)/shard_map/all_to_all | solution.py:25
  53.0 3.4 %collective-permute-start = (f32[32,16,128]{2,1,0:T(8,128)S(1)}, f32[32,16,128]{2,1,0:T(8,128)S(1)}, u32[]{:S(2)}, u32[]{:S(2)}) collective-permute-start(f32[32,16,128]{2,1,0:T(8,128)S(1)} %slice.31.refs_0_), channel_id=1, source_target_pairs={{0,1},{1,2},{2,3},{3,0},{4,5},{5,6},{6,7},{7,4},{8,9},{9,10},{10,1... | collective-permute-start | bytes 786440 | tf_op jit(solution)/shard_map/ppermute | solution.py:43
  56.4 2.7 %collective-permute-start.1 = (f32[32,16,128]{2,1,0:T(8,128)S(1)}, f32[32,16,128]{2,1,0:T(8,128)S(1)}, u32[]{:S(2)}, u32[]{:S(2)}) collective-permute-start(f32[32,16,128]{2,1,0:T(8,128)S(1)} %slice.31.refs_0_), channel_id=1, source_target_pairs={{0,2},{1,3},{2,0},{3,1},{4,6},{5,7},{6,4},{7,5},{8,10},{9,11},{10,... | collective-permute-start | bytes 786440 | tf_op jit(solution)/shard_map/ppermute | solution.py:43
  59.1 4.3 %collective-permute-start.2 = (f32[32,16,128]{2,1,0:T(8,128)S(1)}, f32[32,16,128]{2,1,0:T(8,128)S(1)}, u32[]{:S(2)}, u32[]{:S(2)}) collective-permute-start(f32[32,16,128]{2,1,0:T(8,128)S(1)} %slice.31.refs_0_), channel_id=1, source_target_pairs={{0,3},{1,0},{2,1},{3,2},{4,7},{5,4},{6,5},{7,6},{8,11},{9,8},{10,9... | collective-permute-start | bytes 786440 | tf_op jit(solution)/shard_map/ppermute | solution.py:43
  63.5 3.9 %collective-permute-done.refs_1_ = f32[32,16,128]{2,1,0:T(8,128)S(1)} collective-permute-done((f32[32,16,128]{2,1,0:T(8,128)S(1)}, f32[32,16,128]{2,1,0:T(8,128)S(1)}, u32[]{:S(2)}, u32[]{:S(2)}) %collective-permute-start) | collective-permute-done | bytes 262176 | tf_op jit(solution)/shard_map/ppermute | solution.py:43
  67.4 3.3 %collective-permute-done.1.refs_2_ = f32[32,16,128]{2,1,0:T(8,128)S(1)} collective-permute-done((f32[32,16,128]{2,1,0:T(8,128)S(1)}, f32[32,16,128]{2,1,0:T(8,128)S(1)}, u32[]{:S(2)}, u32[]{:S(2)}) %collective-permute-start.1) | collective-permute-done | bytes 262176 | tf_op jit(solution)/shard_map/ppermute | solution.py:43
  70.7 4.0 %collective-permute-done.2.refs_3_ = f32[32,16,128]{2,1,0:T(8,128)S(1)} collective-permute-done((f32[32,16,128]{2,1,0:T(8,128)S(1)}, f32[32,16,128]{2,1,0:T(8,128)S(1)}, u32[]{:S(2)}, u32[]{:S(2)}) %collective-permute-start.2) | collective-permute-done | bytes 262176 | tf_op jit(solution)/shard_map/ppermute | solution.py:43
  75.4 1.9 collective-permute-start.3
  77.3 1.8 collective-permute-done.3
  83.3 1.8 forward.1
  85.1 7.7 %all-to-all-start.2 = ((f32[32,2,512]{2,1,0:T(2,128)}), f32[32,2,512]{2,1,0:T(2,128)S(1)}, u32[]{:S(2)}, u32[]{:S(2)}) async-start(f32[32,2,512]{2,1,0:T(2,128)} %get-tuple-element.12), calls=%async_computation.2 | async-start | bytes 262144 | tf_op jit(solution)/shard_map/all_to_all | solution.py:25
  93.8 8.0 %all-to-all-done.2.arrived_ref = f32[32,2,512]{2,1,0:T(2,128)S(1)} async-done(((f32[32,2,512]{2,1,0:T(2,128)}), f32[32,2,512]{2,1,0:T(2,128)S(1)}, u32[]{:S(2)}, u32[]{:S(2)}) %all-to-all-start.2) | async-done | bytes 131104 | tf_op jit(solution)/shard_map/all_to_all | solution.py:25
  101.8 1.5 share.1
  103.3 7.2 %all-to-all-start.3 = ((f32[16,2,1024]{2,1,0:T(2,128)}), f32[16,2,1024]{2,1,0:T(2,128)S(1)}, u32[]{:S(2)}, u32[]{:S(2)}) async-start(f32[16,2,1024]{2,1,0:T(2,128)} %share.1), calls=%async_computation.3 | async-start | bytes 262144 | tf_op jit(solution)/shard_map/all_to_all | solution.py:25
  110.5 1.3 constant_dynamic-slice_fusion.1
  111.8 8.7 %all-to-all-done.3.share_ref = f32[16,2,1024]{2,1,0:T(2,128)S(1)} async-done(((f32[16,2,1024]{2,1,0:T(2,128)}), f32[16,2,1024]{2,1,0:T(2,128)S(1)}, u32[]{:S(2)}, u32[]{:S(2)}) %all-to-all-start.3) | async-done | bytes 131104 | tf_op jit(solution)/shard_map/all_to_all | solution.py:25
  120.6 7.0 %all-gather.3.cloned.1.call-done = f32[4096,256]{1,0:T(8,128)} async-done(((f32[256,256]{1,0:T(8,128)}), f32[4096,256]{1,0:T(8,128)}) %all-gather.3.cloned.1.call-update) | async-done | bytes 4194320 | tf_op jit(solution)/shard_map/all_gather | solution.py:37
  127.5 6.5 %chain.1 = f32[32,2,768]{2,1,0:T(2,128)} custom-call(s32[2]{0:T(128)} %copy-done.1, f32[8,512,256]{2,1,0:T(8,128)} %bitcast.14, f32[16,2,1024]{2,1,0:T(2,128)} %copy-done.8, f32[512,256]{1,0:T(8,128)} %copy-done.6, f32[512,256]{1,0:T(8,128)} %copy-done.7, f32[2,256]{1,0:T(2,128)} %get-tuple-element.19.below_ref, f32[2,256]{1,0:T(2,128)} %get-tuple-element.18.above_ref), custom_call_target="tpu_custom_call" | custom-call | flops 100663296 | bytes 4194304 | tf_op jit(solution)/shard_map/chain/pallas_call | solution.py:280
  134.0 20.4 %all_to_all.31.result_ref = f32[32,2,768]{2,1,0:T(2,128)S(1)} all-to-all(f32[32,2,768]{2,1,0:T(2,128)} %chain.1), channel_id=1, replica_groups=mesh['leaf'=16,'front'=32] {'front'}, dimensions={0} | all-to-all | bytes 393216 | tf_op jit(solution)/shard_map/all_to_all | solution.py:25
  154.5 1.9 spread.1
  156.4 5.6 %all-to-all-start.5 = ((f32[32,64,128]{2,1,0:T(8,128)}), f32[32,64,128]{2,1,0:T(8,128)S(1)}, u32[]{:S(2)}, u32[]{:S(2)}) async-start(f32[32,64,128]{2,1,0:T(8,128)} %spread.1), calls=%async_computation.5 | async-start | bytes 2097152 | tf_op jit(solution)/shard_map/all_to_all | solution.py:25
  162.9 26.5 %all-to-all-done.5 = f32[32,64,128]{2,1,0:T(8,128)S(1)} async-done(((f32[32,64,128]{2,1,0:T(8,128)}), f32[32,64,128]{2,1,0:T(8,128)S(1)}, u32[]{:S(2)}, u32[]{:S(2)}) %all-to-all-start.5) | async-done | bytes 1048608 | tf_op jit(solution)/shard_map/all_to_all | solution.py:25
  (50 shorter events, 9.8 us)
Async XLA Ops:
  7.2 2.0 %copy-start.11 = (s32[1,256]{1,0:T(1,128)S(1)}, s32[1,256]{1,0:T(1,128)}, u32[]{:S(2)}) copy-start(s32[1,256]{1,0:T(1,128)} %param.9) | copy-start | bytes 3076
  7.2 2.9 %copy-start.9 = (f32[256,128]{1,0:T(8,128)S(1)}, f32[256,128]{1,0:T(8,128)}, u32[]{:S(2)}) copy-start(f32[256,128]{1,0:T(8,128)} %param.8) | copy-start | bytes 393220
  9.1 1.5 copy-start.10
  47.4 28.0 %all-to-all-start.1 = ((f32[32,16,256]{2,1,0:T(8,128)}), f32[32,16,256]{2,1,0:T(8,128)S(1)}, u32[]{:S(2)}, u32[]{:S(2)}) async-start(f32[32,16,256]{2,1,0:T(8,128)} %broadcast_in_dim.18), calls=%async_computation.1 | async-start | bytes 1048576 | tf_op jit(solution)/shard_map/all_to_all | solution.py:25
  52.9 74.6 %all-gather.3.cloned.1.call-start = ((), (), s32[]{:S(2)}) async-start(), calls=%async_computation.6 | async-start | bytes 4456448 | tf_op jit(solution)/shard_map/all_gather | solution.py:37
  53.0 14.4 %collective-permute-start = (f32[32,16,128]{2,1,0:T(8,128)S(1)}, f32[32,16,128]{2,1,0:T(8,128)S(1)}, u32[]{:S(2)}, u32[]{:S(2)}) collective-permute-start(f32[32,16,128]{2,1,0:T(8,128)S(1)} %slice.31.refs_0_), channel_id=1, source_target_pairs={{0,1},{1,2},{2,3},{3,0},{4,5},{5,6},{6,7},{7,4},{8,9},{9,10},{10,1... | collective-permute-start | bytes 786440 | tf_op jit(solution)/shard_map/ppermute | solution.py:43
  56.4 14.3 %collective-permute-start.1 = (f32[32,16,128]{2,1,0:T(8,128)S(1)}, f32[32,16,128]{2,1,0:T(8,128)S(1)}, u32[]{:S(2)}, u32[]{:S(2)}) collective-permute-start(f32[32,16,128]{2,1,0:T(8,128)S(1)} %slice.31.refs_0_), channel_id=1, source_target_pairs={{0,2},{1,3},{2,0},{3,1},{4,6},{5,7},{6,4},{7,5},{8,10},{9,11},{10,... | collective-permute-start | bytes 786440 | tf_op jit(solution)/shard_map/ppermute | solution.py:43
  59.1 15.5 %collective-permute-start.2 = (f32[32,16,128]{2,1,0:T(8,128)S(1)}, f32[32,16,128]{2,1,0:T(8,128)S(1)}, u32[]{:S(2)}, u32[]{:S(2)}) collective-permute-start(f32[32,16,128]{2,1,0:T(8,128)S(1)} %slice.31.refs_0_), channel_id=1, source_target_pairs={{0,3},{1,0},{2,1},{3,2},{4,7},{5,4},{6,5},{7,6},{8,11},{9,8},{10,9... | collective-permute-start | bytes 786440 | tf_op jit(solution)/shard_map/ppermute | solution.py:43
  70.7 8.6 %copy-start.2 = (f32[32,16,128]{2,1,0:T(8,128)}, f32[32,16,128]{2,1,0:T(8,128)S(1)}, u32[]{:S(2)}) copy-start(f32[32,16,128]{2,1,0:T(8,128)S(1)} %collective-permute-done.1.refs_2_) | copy-start | bytes 786436
  74.7 0.7 copy-start.4
  75.4 3.8 %collective-permute-start.3 = (f32[512,256]{1,0:T(8,128)S(1)}, f32[512,256]{1,0:T(8,128)S(1)}, u32[]{:S(2)}, u32[]{:S(2)}) collective-permute-start(f32[512,256]{1,0:T(8,128)S(1)} %bitcast.15), channel_id=1, source_target_pairs={{0,32},{32,0},{64,96},{96,64},{128,160},{160,128},{192,224},{224,1... | collective-permute-start | bytes 1572872 | tf_op jit(solution)/shard_map/ppermute | solution.py:331
  79.2 1.0 copy-start.6
  79.2 1.0 copy-start.7
  79.2 2.2 %copy-start = (f32[128,4096]{1,0:T(8,128)S(1)}, f32[128,4096]{1,0:T(8,128)}, u32[]{:S(2)}) copy-start(f32[128,4096]{1,0:T(8,128)} %inverse_ref.3) | copy-start | bytes 6291460
  81.4 1.0 copy-start.3
  82.4 0.9 copy-start.5
  85.1 16.7 %all-to-all-start.2 = ((f32[32,2,512]{2,1,0:T(2,128)}), f32[32,2,512]{2,1,0:T(2,128)S(1)}, u32[]{:S(2)}, u32[]{:S(2)}) async-start(f32[32,2,512]{2,1,0:T(2,128)} %get-tuple-element.12), calls=%async_computation.2 | async-start | bytes 262144 | tf_op jit(solution)/shard_map/all_to_all | solution.py:25
  92.8 34.7 %copy-start.1 = (s32[2]{0:T(128)}, s32[2]{0:T(128)S(1)}, u32[]{:S(2)}) copy-start(s32[2]{0:T(128)S(1)} %pad_add_fusion.pos_ref) | copy-start | bytes 28
  103.3 17.2 %all-to-all-start.3 = ((f32[16,2,1024]{2,1,0:T(2,128)}), f32[16,2,1024]{2,1,0:T(2,128)S(1)}, u32[]{:S(2)}, u32[]{:S(2)}) async-start(f32[16,2,1024]{2,1,0:T(2,128)} %share.1), calls=%async_computation.3 | async-start | bytes 262144 | tf_op jit(solution)/shard_map/all_to_all | solution.py:25
  120.6 7.0 %copy-start.8 = (f32[16,2,1024]{2,1,0:T(2,128)}, f32[16,2,1024]{2,1,0:T(2,128)S(1)}, u32[]{:S(2)}) copy-start(f32[16,2,1024]{2,1,0:T(2,128)S(1)} %all-to-all-done.3.share_ref) | copy-start | bytes 393220
  156.4 33.0 %all-to-all-start.5 = ((f32[32,64,128]{2,1,0:T(8,128)}), f32[32,64,128]{2,1,0:T(8,128)S(1)}, u32[]{:S(2)}, u32[]{:S(2)}) async-start(f32[32,64,128]{2,1,0:T(8,128)} %spread.1), calls=%async_computation.5 | async-start | bytes 2097152 | tf_op jit(solution)/shard_map/all_to_all | solution.py:25
Sparse Core Ops, SparseCore 0:
  81.5 45.9 all-gather.2

commit v14 on v13

--- a/solution.py
+++ b/solution.py
@@ -8,7 +8,6 @@
 exact = lax.Precision.HIGHEST
 x_chips = 4
 padded = 8
-forward_weight = 1000
 
 
 def product(left, right):
@@ -119,7 +118,7 @@
         scratch_shapes=[pltpu.VMEM(side_shape, jnp.float32)],
         compiler_params=pltpu.CompilerParams(vmem_limit_bytes=16 * 1024 * 1024),
         cost_estimate=pl.CostEstimate(
-            flops=8 * rhs * block * inverse_blocks.shape[1] * forward_weight,
+            flops=8 * rhs * block * inverse_blocks.shape[1],
             bytes_accessed=4 * inverse_blocks.size + 16 * pieces[0].size,
             transcendentals=0,
         ),
@@ -324,8 +323,6 @@
     coupling = jnp.sum(arrived[:, :, :rows], axis=0)
     side_chunk = arrived[:, :, rows:]
     coupling = gather_front(coupling).reshape(2 * rows, rows)
-    turned = [turn_along_x(side_chunk, steps) for steps in range(1, x_chips)]
-    coupling, *turned = lax.optimization_barrier((coupling, *turned))
 
     swap = [(s, s ^ 1) for s in range(leaf_count)]
     mate = lax.ppermute(coupling, "leaf", swap)
@@ -336,6 +333,8 @@
     c_pair = -product(c_high, c_low)
     g_pair = low[rows:] + product(c_low.T, lifted)
     pair_half = jnp.where(is_upper, g_pair, c_pair)
+    pair_half, side_chunk = lax.optimization_barrier((pair_half, side_chunk))
+    turned = [turn_along_x(side_chunk, steps) for steps in range(1, x_chips)]
     coupling_all = gather_leaf(pair_half).reshape(leaf_count // 2, 2 * rows, rows)
 
     local_forward, vectors = run_forward(

time: 198 us -> 197 us (level)
  blocking collectives: 56.1 us -> 73.4 us
  waiting for transfers between devices: 63.2 us -> 53.7 us
  starting transfers between devices: 38.5 us -> 30.8 us
  local copies, waits for them, and re-layouts: 9.3 us -> 6.59 us
    all_to_all x2 -> x3, blocking collectives: 56.1 us -> 73.4 us  [exchange(): lax.all_to_all(blocks, axis, 0, 0, tiled=True, axis_index_groups=groups)]
    all_to_all x4 -> x3, starting transfers between devices: 26.1 us -> 18.5 us  [exchange(): lax.all_to_all(blocks, axis, 0, 0, tiled=True, axis_index_groups=groups)]
    all_gather x1, waiting for transfers between devices: 6.97 us -> 0.01 us  [gather_leaf(): return lax.all_gather(block, 'leaf', axis=0)]
    ppermute x3, waiting for transfers between devices: 11.2 us -> 9.07 us  [turn_along_x(): return lax.ppermute(block, 'front', pairs)]
    unnamed x26 -> x20, local copies, waits for them, and re-layouts: 5.25 us -> 3.35 us
    all_to_all x4 -> x3, waiting for transfers between devices: 43.2 us -> 42.8 us  [exchange(): lax.all_to_all(blocks, axis, 0, 0, tiled=True, axis_index_groups=groups)]
  transfers between devices with their start and end apart: 9 -> 8, of which waited for: 8 -> 6; matrix products, arithmetic and copies ran while one was open for 2% -> 2% of each run, Pallas kernels for 2% -> 2%
where the time goes in v14:
time: 197 us; the launch traced here: 196 us
  blocking collectives  73.4 us (37%)
  waiting for transfers between devices  53.7 us (27%)
  starting transfers between devices  30.8 us (16%)
  between operations  14.4 us (7%)
  Pallas kernels  12.7 us (6%)
  local copies, waits for them, and re-layouts  6.59 us (3%)
  matrix products  2.66 us (1%)
  other arithmetic  2.06 us (1%)
    all_to_all x3, blocking collectives, exchange(): lax.all_to_all(blocks, axis, 0, 0, tiled=True, axis_index_groups=groups)  73.4 us
    all_to_all x3, waiting for transfers between devices, exchange(): lax.all_to_all(blocks, axis, 0, 0, tiled=True, axis_index_groups=groups)  42.8 us
    all_to_all x3, starting transfers between devices, exchange(): lax.all_to_all(blocks, axis, 0, 0, tiled=True, axis_index_groups=groups)  18.5 us
    ppermute x3, starting transfers between devices, turn_along_x(): return lax.ppermute(block, 'front', pairs)  10.4 us
    ppermute x3, waiting for transfers between devices, turn_along_x(): return lax.ppermute(block, 'front', pairs)  9.07 us
    pallas_call x1, Pallas kernels, run_chain(): pl.pallas_call(chain_kernel, out_shape=jax.ShapeDtypeStruct((targets, sha...  6.47 us
  transfers between devices with their start and end apart: 8, of which 6 were waited for; matrix products, arithmetic and copies ran while one was open for 2% of the time, Pallas kernels for 2%

profile of v14, /device:TPU:2, one launch (start us, length us, event | category | flops | bytes accessed | tf_op | source)
XLA Modules:
  0.0 196.3 jit_solution(722745122818998596)
XLA Ops:
  7.2 1.9 copy.10
  10.8 35.7 %all_to_all.30 = f32[32,16,384]{2,1,0:T(8,128)S(1)} all-to-all(f32[32,16,384]{2,1,0:T(8,128)S(1)} %pad_maximum_fusion), channel_id=1, replica_groups=mesh['leaf'=16,'front'=32] {'front'}, dimensions={0} | all-to-all | bytes 1572864 | tf_op jit(solution)/shard_map/all_to_all | solution.py:24
  46.6 21.0 %all_to_all.31 = f32[32,16,256]{2,1,0:T(8,128)S(1)} all-to-all(f32[32,16,256]{2,1,0:T(8,128)S(1)} %broadcast_in_dim.18), channel_id=1, replica_groups=mesh['leaf'=16,'front'=32] {'front'}, dimensions={0} | all-to-all | bytes 1048576 | tf_op jit(solution)/shard_map/all_to_all | solution.py:24
  67.7 1.9 collective-permute-start
  69.6 1.8 collective-permute-done
  72.6 1.1 fusion.2
  73.7 3.4 %collective-permute-start.1 = (f32[32,16,128]{2,1,0:T(8,128)S(1)}, f32[32,16,128]{2,1,0:T(8,128)S(1)}, u32[]{:S(2)}, u32[]{:S(2)}) collective-permute-start(f32[32,16,128]{2,1,0:T(8,128)S(1)} %slice.35.refs_0_), channel_id=1, source_target_pairs={{0,1},{1,2},{2,3},{3,0},{4,5},{5,6},{6,7},{7,4},{8,9},{9,10},{10,1... | collective-permute-start | bytes 786440 | tf_op jit(solution)/shard_map/ppermute | solution.py:42
  77.1 3.8 %collective-permute-start.2 = (f32[32,16,128]{2,1,0:T(8,128)S(1)}, f32[32,16,128]{2,1,0:T(8,128)S(1)}, u32[]{:S(2)}, u32[]{:S(2)}) collective-permute-start(f32[32,16,128]{2,1,0:T(8,128)S(1)} %slice.35.refs_0_), channel_id=1, source_target_pairs={{0,2},{1,3},{2,0},{3,1},{4,6},{5,7},{6,4},{7,5},{8,10},{9,11},{10,... | collective-permute-start | bytes 786440 | tf_op jit(solution)/shard_map/ppermute | solution.py:42
  80.9 3.3 %collective-permute-start.3 = (f32[32,16,128]{2,1,0:T(8,128)S(1)}, f32[32,16,128]{2,1,0:T(8,128)}, u32[]{:S(2)}, u32[]{:S(2)}) collective-permute-start(f32[32,16,128]{2,1,0:T(8,128)S(1)} %slice.35.refs_0_), channel_id=1, source_target_pairs={{0,3},{1,0},{2,1},{3,2},{4,7},{5,4},{6,5},{7,6},{8,11},{9,8},{10,9... | collective-permute-start | bytes 786440 | tf_op jit(solution)/shard_map/ppermute | solution.py:42
  84.2 1.0 pad_maximum_fusion.1.stacked_ref
  85.2 4.5 %collective-permute-done.2.refs_2_ = f32[32,16,128]{2,1,0:T(8,128)S(1)} collective-permute-done((f32[32,16,128]{2,1,0:T(8,128)S(1)}, f32[32,16,128]{2,1,0:T(8,128)S(1)}, u32[]{:S(2)}, u32[]{:S(2)}) %collective-permute-start.2) | collective-permute-done | bytes 262176 | tf_op jit(solution)/shard_map/ppermute | solution.py:42
  89.7 4.5 %collective-permute-done.3.refs_3_ = f32[32,16,128]{2,1,0:T(8,128)} collective-permute-done((f32[32,16,128]{2,1,0:T(8,128)S(1)}, f32[32,16,128]{2,1,0:T(8,128)}, u32[]{:S(2)}, u32[]{:S(2)}) %collective-permute-start.3) | collective-permute-done | bytes 262176 | tf_op jit(solution)/shard_map/ppermute | solution.py:42
  94.3 2.7 %forward.1 = (f32[64,128]{1,0:T(8,128)S(1)}, f32[32,2,512]{2,1,0:T(2,128)}) custom-call(s32[1]{0:T(128)} %bitcast.10.pos_ref, f32[128,4096]{1,0:T(8,128)S(1)} %copy-done, f32[512,128]{1,0:T(8,128)S(1)} %pad_maximum_fusion.1.stacked_ref, f32[32,16,128]{2,1,0:T(8,128)S(1)} %slice.35.refs_0_, f32[32,16,128]{2,1,0:T(8,128)S(1)} %collective-permute-done.1.refs_1_, ...), custom_call_target="tpu_custom_call" | custom-call | flops 268435456 | bytes 3145728 | tf_op jit(solution)/shard_map/forward/pallas_call | solution.py:110
  97.0 5.7 %all-to-all-start.2 = ((f32[32,2,512]{2,1,0:T(2,128)}), f32[32,2,512]{2,1,0:T(2,128)S(1)}, u32[]{:S(2)}, u32[]{:S(2)}) async-start(f32[32,2,512]{2,1,0:T(2,128)} %get-tuple-element.8), calls=%async_computation.2 | async-start | bytes 262144 | tf_op jit(solution)/shard_map/all_to_all | solution.py:24
  103.8 7.9 %all-to-all-done.2.arrived_ref = f32[32,2,512]{2,1,0:T(2,128)S(1)} async-done(((f32[32,2,512]{2,1,0:T(2,128)}), f32[32,2,512]{2,1,0:T(2,128)S(1)}, u32[]{:S(2)}, u32[]{:S(2)}) %all-to-all-start.2) | async-done | bytes 131104 | tf_op jit(solution)/shard_map/all_to_all | solution.py:24
  111.7 1.5 share.1
  113.2 7.2 %all-to-all-start.3 = ((f32[16,2,1024]{2,1,0:T(2,128)}), f32[16,2,1024]{2,1,0:T(2,128)S(1)}, u32[]{:S(2)}, u32[]{:S(2)}) async-start(f32[16,2,1024]{2,1,0:T(2,128)} %share.1), calls=%async_computation.3 | async-start | bytes 262144 | tf_op jit(solution)/shard_map/all_to_all | solution.py:24
  120.4 1.3 constant_dynamic-slice_fusion.1
  121.7 7.4 %all-to-all-done.3.share_ref = f32[16,2,1024]{2,1,0:T(2,128)S(1)} async-done(((f32[16,2,1024]{2,1,0:T(2,128)}), f32[16,2,1024]{2,1,0:T(2,128)S(1)}, u32[]{:S(2)}, u32[]{:S(2)}) %all-to-all-start.3) | async-done | bytes 131104 | tf_op jit(solution)/shard_map/all_to_all | solution.py:24
  129.8 6.5 %chain.1 = f32[32,2,768]{2,1,0:T(2,128)} custom-call(s32[2]{0:T(128)} %copy-done.1, f32[8,512,256]{2,1,0:T(8,128)} %bitcast.16, f32[16,2,1024]{2,1,0:T(2,128)} %copy-done.5, f32[512,256]{1,0:T(8,128)} %copy-done.2, f32[512,256]{1,0:T(8,128)} %copy-done.3, f32[2,256]{1,0:T(2,128)} %get-tuple-element.15.below_ref, f32[2,256]{1,0:T(2,128)} %get-tuple-element.14.above_ref), custom_call_target="tpu_custom_call" | custom-call | flops 100663296 | bytes 4194304 | tf_op jit(solution)/shard_map/chain/pallas_call | solution.py:279
  136.3 16.7 %all_to_all.32.result_ref = f32[32,2,768]{2,1,0:T(2,128)S(1)} all-to-all(f32[32,2,768]{2,1,0:T(2,128)} %chain.1), channel_id=1, replica_groups=mesh['leaf'=16,'front'=32] {'front'}, dimensions={0} | all-to-all | bytes 393216 | tf_op jit(solution)/shard_map/all_to_all | solution.py:24
  153.0 1.9 spread.1
  154.9 5.6 %all-to-all-start.5 = ((f32[32,64,128]{2,1,0:T(8,128)}), f32[32,64,128]{2,1,0:T(8,128)S(1)}, u32[]{:S(2)}, u32[]{:S(2)}) async-start(f32[32,64,128]{2,1,0:T(8,128)} %spread.1), calls=%async_computation.5 | async-start | bytes 2097152 | tf_op jit(solution)/shard_map/all_to_all | solution.py:24
  161.3 27.5 %all-to-all-done.5 = f32[32,64,128]{2,1,0:T(8,128)S(1)} async-done(((f32[32,64,128]{2,1,0:T(8,128)}), f32[32,64,128]{2,1,0:T(8,128)S(1)}, u32[]{:S(2)}, u32[]{:S(2)}) %all-to-all-start.5) | async-done | bytes 1048608 | tf_op jit(solution)/shard_map/all_to_all | solution.py:24
  (43 shorter events, 6.0 us)
Async XLA Ops:
  7.2 2.0 %copy-start.8 = (s32[1,256]{1,0:T(1,128)S(1)}, s32[1,256]{1,0:T(1,128)}, u32[]{:S(2)}) copy-start(s32[1,256]{1,0:T(1,128)} %param.9) | copy-start | bytes 3076
  7.2 2.9 %copy-start.6 = (f32[256,128]{1,0:T(8,128)S(1)}, f32[256,128]{1,0:T(8,128)}, u32[]{:S(2)}) copy-start(f32[256,128]{1,0:T(8,128)} %param.8) | copy-start | bytes 393220
  7.2 122.0 %all-gather.3.cloned.1.call-start = ((), (), s32[]{:S(2)}) async-start(), calls=%async_computation.6 | async-start | bytes 4456448 | tf_op jit(solution)/shard_map/all_gather | solution.py:36
  9.2 1.5 copy-start.7
  10.1 0.7 copy-start.4
  67.7 3.8 %collective-permute-start = (f32[512,256]{1,0:T(8,128)S(1)}, f32[512,256]{1,0:T(8,128)S(1)}, u32[]{:S(2)}, u32[]{:S(2)}) collective-permute-start(f32[512,256]{1,0:T(8,128)S(1)} %bitcast.17), channel_id=1, source_target_pairs={{0,32},{32,0},{64,96},{96,64},{128,160},{160,128},{192,224},{224,1... | collective-permute-start | bytes 1572872 | tf_op jit(solution)/shard_map/ppermute | solution.py:328
  71.5 1.0 copy-start.2
  71.5 1.0 copy-start.3
  71.5 22.7 %copy-start = (f32[128,4096]{1,0:T(8,128)S(1)}, f32[128,4096]{1,0:T(8,128)}, u32[]{:S(2)}) copy-start(f32[128,4096]{1,0:T(8,128)} %inverse_ref.3) | copy-start | bytes 6291460
  73.7 11.5 %collective-permute-start.1 = (f32[32,16,128]{2,1,0:T(8,128)S(1)}, f32[32,16,128]{2,1,0:T(8,128)S(1)}, u32[]{:S(2)}, u32[]{:S(2)}) collective-permute-start(f32[32,16,128]{2,1,0:T(8,128)S(1)} %slice.35.refs_0_), channel_id=1, source_target_pairs={{0,1},{1,2},{2,3},{3,0},{4,5},{5,6},{6,7},{7,4},{8,9},{9,10},{10,1... | collective-permute-start | bytes 786440 | tf_op jit(solution)/shard_map/ppermute | solution.py:42
  77.1 12.6 %collective-permute-start.2 = (f32[32,16,128]{2,1,0:T(8,128)S(1)}, f32[32,16,128]{2,1,0:T(8,128)S(1)}, u32[]{:S(2)}, u32[]{:S(2)}) collective-permute-start(f32[32,16,128]{2,1,0:T(8,128)S(1)} %slice.35.refs_0_), channel_id=1, source_target_pairs={{0,2},{1,3},{2,0},{3,1},{4,6},{5,7},{6,4},{7,5},{8,10},{9,11},{10,... | collective-permute-start | bytes 786440 | tf_op jit(solution)/shard_map/ppermute | solution.py:42
  80.9 13.4 %collective-permute-start.3 = (f32[32,16,128]{2,1,0:T(8,128)S(1)}, f32[32,16,128]{2,1,0:T(8,128)}, u32[]{:S(2)}, u32[]{:S(2)}) collective-permute-start(f32[32,16,128]{2,1,0:T(8,128)S(1)} %slice.35.refs_0_), channel_id=1, source_target_pairs={{0,3},{1,0},{2,1},{3,2},{4,7},{5,4},{6,5},{7,6},{8,11},{9,8},{10,9... | collective-permute-start | bytes 786440 | tf_op jit(solution)/shard_map/ppermute | solution.py:42
  97.0 14.7 %all-to-all-start.2 = ((f32[32,2,512]{2,1,0:T(2,128)}), f32[32,2,512]{2,1,0:T(2,128)S(1)}, u32[]{:S(2)}, u32[]{:S(2)}) async-start(f32[32,2,512]{2,1,0:T(2,128)} %get-tuple-element.8), calls=%async_computation.2 | async-start | bytes 262144 | tf_op jit(solution)/shard_map/all_to_all | solution.py:24
  102.8 26.3 %copy-start.1 = (s32[2]{0:T(128)}, s32[2]{0:T(128)S(1)}, u32[]{:S(2)}) copy-start(s32[2]{0:T(128)S(1)} %pad_add_fusion.pos_ref) | copy-start | bytes 28
  113.2 15.9 %all-to-all-start.3 = ((f32[16,2,1024]{2,1,0:T(2,128)}), f32[16,2,1024]{2,1,0:T(2,128)S(1)}, u32[]{:S(2)}, u32[]{:S(2)}) async-start(f32[16,2,1024]{2,1,0:T(2,128)} %share.1), calls=%async_computation.3 | async-start | bytes 262144 | tf_op jit(solution)/shard_map/all_to_all | solution.py:24
  129.2 0.7 copy-start.5
  154.9 33.8 %all-to-all-start.5 = ((f32[32,64,128]{2,1,0:T(8,128)}), f32[32,64,128]{2,1,0:T(8,128)S(1)}, u32[]{:S(2)}, u32[]{:S(2)}) async-start(f32[32,64,128]{2,1,0:T(8,128)} %spread.1), calls=%async_computation.5 | async-start | bytes 2097152 | tf_op jit(solution)/shard_map/all_to_all | solution.py:24
Sparse Core Ops, SparseCore 0:
  73.8 41.5 all-gather.2

commit v15 on v14

--- a/solution.py
+++ b/solution.py
@@ -323,6 +323,8 @@
     coupling = jnp.sum(arrived[:, :, :rows], axis=0)
     side_chunk = arrived[:, :, rows:]
     coupling = gather_front(coupling).reshape(2 * rows, rows)
+    turned = [turn_along_x(side_chunk, steps) for steps in (1, x_chips - 1)]
+    coupling, *turned = lax.optimization_barrier((coupling, *turned))
 
     swap = [(s, s ^ 1) for s in range(leaf_count)]
     mate = lax.ppermute(coupling, "leaf", swap)
@@ -334,7 +336,7 @@
     g_pair = low[rows:] + product(c_low.T, lifted)
     pair_half = jnp.where(is_upper, g_pair, c_pair)
     pair_half, side_chunk = lax.optimization_barrier((pair_half, side_chunk))
-    turned = [turn_along_x(side_chunk, steps) for steps in range(1, x_chips)]
+    turned.insert(1, turn_along_x(side_chunk, 2))
     coupling_all = gather_leaf(pair_half).reshape(leaf_count // 2, 2 * rows, rows)
 
     local_forward, vectors = run_forward(

time: 197 us -> 191 us (0.970)
  blocking collectives: 73.4 us -> 52.7 us
  starting transfers between devices: 30.8 us -> 37.8 us
  waiting for transfers between devices: 53.7 us -> 60.2 us
    all_to_all x3 -> x2, blocking collectives: 73.4 us -> 52.7 us  [exchange(): lax.all_to_all(blocks, axis, 0, 0, tiled=True, axis_index_groups=groups)]
    all_to_all x3 -> x4, starting transfers between devices: 18.5 us -> 26.1 us  [exchange(): lax.all_to_all(blocks, axis, 0, 0, tiled=True, axis_index_groups=groups)]
    ppermute x3, waiting for transfers between devices: 9.07 us -> 16.1 us  [turn_along_x(): return lax.ppermute(block, 'front', pairs)]
    all_to_all x3 -> x4, waiting for transfers between devices: 42.8 us -> 42.2 us  [exchange(): lax.all_to_all(blocks, axis, 0, 0, tiled=True, axis_index_groups=groups)]
  transfers between devices with their start and end apart: 8 -> 9, of which waited for: 6 -> 8; matrix products, arithmetic and copies ran while one was open for 2% -> 2% of each run, Pallas kernels for 2% -> 2%
where the time goes in v15:
time: 191 us; the launch traced here: 190 us
  waiting for transfers between devices  60.2 us (32%)
  blocking collectives  52.7 us (28%)
  starting transfers between devices  37.8 us (20%)
  between operations  14.4 us (8%)
  Pallas kernels  12.6 us (7%)
  local copies, waits for them, and re-layouts  7.36 us (4%)
  matrix products  2.66 us (1%)
  other arithmetic  1.97 us (1%)
    all_to_all x2, blocking collectives, exchange(): lax.all_to_all(blocks, axis, 0, 0, tiled=True, axis_index_groups=groups)  52.7 us
    all_to_all x4, waiting for transfers between devices, exchange(): lax.all_to_all(blocks, axis, 0, 0, tiled=True, axis_index_groups=groups)  42.2 us
    all_to_all x4, starting transfers between devices, exchange(): lax.all_to_all(blocks, axis, 0, 0, tiled=True, axis_index_groups=groups)  26.1 us
    ppermute x3, waiting for transfers between devices, turn_along_x(): return lax.ppermute(block, 'front', pairs)  16.1 us
    ppermute x3, starting transfers between devices, turn_along_x(): return lax.ppermute(block, 'front', pairs)  9.82 us
    pallas_call x1, Pallas kernels, run_chain(): pl.pallas_call(chain_kernel, out_shape=jax.ShapeDtypeStruct((targets, sha...  6.48 us
  transfers between devices with their start and end apart: 9, of which 8 were waited for; matrix products, arithmetic and copies ran while one was open for 2% of the time, Pallas kernels for 2%

profile of v15, /device:TPU:2, one launch (start us, length us, event | category | flops | bytes accessed | tf_op | source)
XLA Modules:
  0.0 189.7 jit_solution(2628408541829947681)
XLA Ops:
  7.2 1.9 %copy.10 = f32[128,4096]{0,1:T(8,128)S(1)} copy(f32[128,4096]{1,0:T(8,128)} %inverse_ref.3) | data formatting | bytes 4194304 | tf_op args[1]
  10.7 35.7 %all_to_all.30 = f32[32,16,384]{2,1,0:T(8,128)S(1)} all-to-all(f32[32,16,384]{2,1,0:T(8,128)S(1)} %pad_maximum_fusion), channel_id=1, replica_groups=mesh['leaf'=16,'front'=32] {'front'}, dimensions={0} | all-to-all | bytes 1572864 | tf_op jit(solution)/shard_map/all_to_all | solution.py:24
  47.4 5.6 %all-to-all-start.1 = ((f32[32,16,256]{2,1,0:T(8,128)}), f32[32,16,256]{2,1,0:T(8,128)S(1)}, u32[]{:S(2)}, u32[]{:S(2)}) async-start(f32[32,16,256]{2,1,0:T(8,128)} %broadcast_in_dim.18), calls=%async_computation.1 | async-start | bytes 1048576 | tf_op jit(solution)/shard_map/all_to_all | solution.py:24
  53.0 3.4 %collective-permute-start = (f32[32,16,128]{2,1,0:T(8,128)S(1)}, f32[32,16,128]{2,1,0:T(8,128)S(1)}, u32[]{:S(2)}, u32[]{:S(2)}) collective-permute-start(f32[32,16,128]{2,1,0:T(8,128)S(1)} %slice.31.refs_0_), channel_id=1, source_target_pairs={{0,1},{1,2},{2,3},{3,0},{4,5},{5,6},{6,7},{7,4},{8,9},{9,10},{10,1... | collective-permute-start | bytes 786440 | tf_op jit(solution)/shard_map/ppermute | solution.py:42
  56.4 2.5 %collective-permute-start.1 = (f32[32,16,128]{2,1,0:T(8,128)S(1)}, f32[32,16,128]{2,1,0:T(8,128)S(1)}, u32[]{:S(2)}, u32[]{:S(2)}) collective-permute-start(f32[32,16,128]{2,1,0:T(8,128)S(1)} %slice.31.refs_0_), channel_id=1, source_target_pairs={{0,3},{1,0},{2,1},{3,2},{4,7},{5,4},{6,5},{7,6},{8,11},{9,8},{10,9... | collective-permute-start | bytes 786440 | tf_op jit(solution)/shard_map/ppermute | solution.py:42
  58.9 6.2 %collective-permute-done.refs_1_ = f32[32,16,128]{2,1,0:T(8,128)S(1)} collective-permute-done((f32[32,16,128]{2,1,0:T(8,128)S(1)}, f32[32,16,128]{2,1,0:T(8,128)S(1)}, u32[]{:S(2)}, u32[]{:S(2)}) %collective-permute-start) | collective-permute-done | bytes 262176 | tf_op jit(solution)/shard_map/ppermute | solution.py:42
  65.1 3.0 %collective-permute-done.1.refs_3_ = f32[32,16,128]{2,1,0:T(8,128)S(1)} collective-permute-done((f32[32,16,128]{2,1,0:T(8,128)S(1)}, f32[32,16,128]{2,1,0:T(8,128)S(1)}, u32[]{:S(2)}, u32[]{:S(2)}) %collective-permute-start.1) | collective-permute-done | bytes 262176 | tf_op jit(solution)/shard_map/ppermute | solution.py:42
  68.6 1.9 %collective-permute-start.2 = (f32[512,256]{1,0:T(8,128)S(1)}, f32[512,256]{1,0:T(8,128)S(1)}, u32[]{:S(2)}, u32[]{:S(2)}) collective-permute-start(f32[512,256]{1,0:T(8,128)S(1)} %bitcast.15), channel_id=1, source_target_pairs={{0,32},{32,0},{64,96},{96,64},{128,160},{160,128},{192,224},{224,1... | collective-permute-start | bytes 1572872 | tf_op jit(solution)/shard_map/ppermute | solution.py:330
  70.5 1.9 collective-permute-done.2
  73.5 1.1 fusion.2
  74.6 4.0 %collective-permute-start.3 = (f32[32,16,128]{2,1,0:T(8,128)S(1)}, f32[32,16,128]{2,1,0:T(8,128)}, u32[]{:S(2)}, u32[]{:S(2)}) collective-permute-start(f32[32,16,128]{2,1,0:T(8,128)S(1)} %slice.31.refs_0_), channel_id=1, source_target_pairs={{0,2},{1,3},{2,0},{3,1},{4,6},{5,7},{6,4},{7,5},{8,10},{9,11},{10,... | collective-permute-start | bytes 786440 | tf_op jit(solution)/shard_map/ppermute | solution.py:42
  79.6 6.9 %collective-permute-done.3.refs_2_ = f32[32,16,128]{2,1,0:T(8,128)} collective-permute-done((f32[32,16,128]{2,1,0:T(8,128)S(1)}, f32[32,16,128]{2,1,0:T(8,128)}, u32[]{:S(2)}, u32[]{:S(2)}) %collective-permute-start.3) | collective-permute-done | bytes 262176 | tf_op jit(solution)/shard_map/ppermute | solution.py:42
  86.5 2.7 %forward.1 = (f32[64,128]{1,0:T(8,128)S(1)}, f32[32,2,512]{2,1,0:T(2,128)}) custom-call(s32[1]{0:T(128)} %bitcast.10.pos_ref, f32[128,4096]{1,0:T(8,128)S(1)} %copy-done, f32[512,128]{1,0:T(8,128)S(1)} %pad_maximum_fusion.1.stacked_ref, f32[32,16,128]{2,1,0:T(8,128)S(1)} %slice.31.refs_0_, f32[32,16,128]{2,1,0:T(8,128)S(1)} %collective-permute-done.refs_1_, ...), custom_call_target="tpu_custom_call" | custom-call | flops 268435456 | bytes 3145728 | tf_op jit(solution)/shard_map/forward/pallas_call | solution.py:110
  89.2 7.6 %all-to-all-start.2 = ((f32[32,2,512]{2,1,0:T(2,128)}), f32[32,2,512]{2,1,0:T(2,128)S(1)}, u32[]{:S(2)}, u32[]{:S(2)}) async-start(f32[32,2,512]{2,1,0:T(2,128)} %get-tuple-element.14), calls=%async_computation.2 | async-start | bytes 262144 | tf_op jit(solution)/shard_map/all_to_all | solution.py:24
  97.9 7.8 %all-to-all-done.2.arrived_ref = f32[32,2,512]{2,1,0:T(2,128)S(1)} async-done(((f32[32,2,512]{2,1,0:T(2,128)}), f32[32,2,512]{2,1,0:T(2,128)S(1)}, u32[]{:S(2)}, u32[]{:S(2)}) %all-to-all-start.2) | async-done | bytes 131104 | tf_op jit(solution)/shard_map/all_to_all | solution.py:24
  105.7 1.5 share.1
  107.2 7.2 %all-to-all-start.3 = ((f32[16,2,1024]{2,1,0:T(2,128)}), f32[16,2,1024]{2,1,0:T(2,128)S(1)}, u32[]{:S(2)}, u32[]{:S(2)}) async-start(f32[16,2,1024]{2,1,0:T(2,128)} %share.1), calls=%async_computation.3 | async-start | bytes 262144 | tf_op jit(solution)/shard_map/all_to_all | solution.py:24
  114.4 1.3 constant_dynamic-slice_fusion.1
  115.7 7.4 %all-to-all-done.3.share_ref = f32[16,2,1024]{2,1,0:T(2,128)S(1)} async-done(((f32[16,2,1024]{2,1,0:T(2,128)}), f32[16,2,1024]{2,1,0:T(2,128)S(1)}, u32[]{:S(2)}, u32[]{:S(2)}) %all-to-all-start.3) | async-done | bytes 131104 | tf_op jit(solution)/shard_map/all_to_all | solution.py:24
  123.8 6.5 %chain.1 = f32[32,2,768]{2,1,0:T(2,128)} custom-call(s32[2]{0:T(128)} %copy-done.1, f32[8,512,256]{2,1,0:T(8,128)} %bitcast.14, f32[16,2,1024]{2,1,0:T(2,128)} %copy-done.4, f32[512,256]{1,0:T(8,128)} %copy-done.2, f32[512,256]{1,0:T(8,128)} %copy-done.3, f32[2,256]{1,0:T(2,128)} %get-tuple-element.21.below_ref, f32[2,256]{1,0:T(2,128)} %get-tuple-element.20.above_ref), custom_call_target="tpu_custom_call" | custom-call | flops 100663296 | bytes 4194304 | tf_op jit(solution)/shard_map/chain/pallas_call | solution.py:279
  130.3 16.9 %all_to_all.31.result_ref = f32[32,2,768]{2,1,0:T(2,128)S(1)} all-to-all(f32[32,2,768]{2,1,0:T(2,128)} %chain.1), channel_id=1, replica_groups=mesh['leaf'=16,'front'=32] {'front'}, dimensions={0} | all-to-all | bytes 393216 | tf_op jit(solution)/shard_map/all_to_all | solution.py:24
  147.2 2.0 %spread.1 = f32[32,64,128]{2,1,0:T(8,128)} custom-call(f32[32,2,768]{2,1,0:T(2,128)S(1)} %all_to_all.31.result_ref, f32[64,128]{1,0:T(8,128)S(1)} %get-tuple-element.15.forward_ref, f32[512,128]{1,0:T(8,128)S(1)} %pad_maximum_fusion.1.stacked_ref, f32[128,4096]{1,0:T(8,128)S(1)} %copy-done), custom_call_target="tpu_custom_call" | custom-call | flops 268435456 | bytes 3145728 | tf_op jit(solution)/shard_map/spread/pallas_call | solution.py:150
  149.2 5.7 %all-to-all-start.5 = ((f32[32,64,128]{2,1,0:T(8,128)}), f32[32,64,128]{2,1,0:T(8,128)S(1)}, u32[]{:S(2)}, u32[]{:S(2)}) async-start(f32[32,64,128]{2,1,0:T(8,128)} %spread.1), calls=%async_computation.5 | async-start | bytes 2097152 | tf_op jit(solution)/shard_map/all_to_all | solution.py:24
  155.7 26.5 %all-to-all-done.5 = f32[32,64,128]{2,1,0:T(8,128)S(1)} async-done(((f32[32,64,128]{2,1,0:T(8,128)}), f32[32,64,128]{2,1,0:T(8,128)S(1)}, u32[]{:S(2)}, u32[]{:S(2)}) %all-to-all-start.5) | async-done | bytes 1048608 | tf_op jit(solution)/shard_map/all_to_all | solution.py:24
  (42 shorter events, 8.2 us)
Async XLA Ops:
  7.2 2.0 %copy-start.7 = (s32[1,256]{1,0:T(1,128)S(1)}, s32[1,256]{1,0:T(1,128)}, u32[]{:S(2)}) copy-start(s32[1,256]{1,0:T(1,128)} %param.9) | copy-start | bytes 3076
  7.2 2.9 %copy-start.5 = (f32[256,128]{1,0:T(8,128)S(1)}, f32[256,128]{1,0:T(8,128)}, u32[]{:S(2)}) copy-start(f32[256,128]{1,0:T(8,128)} %param.8) | copy-start | bytes 393220
  9.2 1.5 copy-start.6
  47.4 21.2 %all-to-all-start.1 = ((f32[32,16,256]{2,1,0:T(8,128)}), f32[32,16,256]{2,1,0:T(8,128)S(1)}, u32[]{:S(2)}, u32[]{:S(2)}) async-start(f32[32,16,256]{2,1,0:T(8,128)} %broadcast_in_dim.18), calls=%async_computation.1 | async-start | bytes 1048576 | tf_op jit(solution)/shard_map/all_to_all | solution.py:24
  52.9 70.2 %all-gather.3.cloned.1.call-start = ((), (), s32[]{:S(2)}) async-start(), calls=%async_computation.6 | async-start | bytes 4456448 | tf_op jit(solution)/shard_map/all_gather | solution.py:36
  53.0 12.1 %collective-permute-start = (f32[32,16,128]{2,1,0:T(8,128)S(1)}, f32[32,16,128]{2,1,0:T(8,128)S(1)}, u32[]{:S(2)}, u32[]{:S(2)}) collective-permute-start(f32[32,16,128]{2,1,0:T(8,128)S(1)} %slice.31.refs_0_), channel_id=1, source_target_pairs={{0,1},{1,2},{2,3},{3,0},{4,5},{5,6},{6,7},{7,4},{8,9},{9,10},{10,1... | collective-permute-start | bytes 786440 | tf_op jit(solution)/shard_map/ppermute | solution.py:42
  56.4 11.7 %collective-permute-start.1 = (f32[32,16,128]{2,1,0:T(8,128)S(1)}, f32[32,16,128]{2,1,0:T(8,128)S(1)}, u32[]{:S(2)}, u32[]{:S(2)}) collective-permute-start(f32[32,16,128]{2,1,0:T(8,128)S(1)} %slice.31.refs_0_), channel_id=1, source_target_pairs={{0,3},{1,0},{2,1},{3,2},{4,7},{5,4},{6,5},{7,6},{8,11},{9,8},{10,9... | collective-permute-start | bytes 786440 | tf_op jit(solution)/shard_map/ppermute | solution.py:42
  68.6 3.8 %collective-permute-start.2 = (f32[512,256]{1,0:T(8,128)S(1)}, f32[512,256]{1,0:T(8,128)S(1)}, u32[]{:S(2)}, u32[]{:S(2)}) collective-permute-start(f32[512,256]{1,0:T(8,128)S(1)} %bitcast.15), channel_id=1, source_target_pairs={{0,32},{32,0},{64,96},{96,64},{128,160},{160,128},{192,224},{224,1... | collective-permute-start | bytes 1572872 | tf_op jit(solution)/shard_map/ppermute | solution.py:330
  72.5 1.0 copy-start.2
  72.5 1.0 copy-start.3
  72.5 14.0 %copy-start = (f32[128,4096]{1,0:T(8,128)S(1)}, f32[128,4096]{1,0:T(8,128)}, u32[]{:S(2)}) copy-start(f32[128,4096]{1,0:T(8,128)} %inverse_ref.3) | copy-start | bytes 6291460
  74.6 11.9 %collective-permute-start.3 = (f32[32,16,128]{2,1,0:T(8,128)S(1)}, f32[32,16,128]{2,1,0:T(8,128)}, u32[]{:S(2)}, u32[]{:S(2)}) collective-permute-start(f32[32,16,128]{2,1,0:T(8,128)S(1)} %slice.31.refs_0_), channel_id=1, source_target_pairs={{0,2},{1,3},{2,0},{3,1},{4,6},{5,7},{6,4},{7,5},{8,10},{9,11},{10,... | collective-permute-start | bytes 786440 | tf_op jit(solution)/shard_map/ppermute | solution.py:42
  89.2 16.5 %all-to-all-start.2 = ((f32[32,2,512]{2,1,0:T(2,128)}), f32[32,2,512]{2,1,0:T(2,128)S(1)}, u32[]{:S(2)}, u32[]{:S(2)}) async-start(f32[32,2,512]{2,1,0:T(2,128)} %get-tuple-element.14), calls=%async_computation.2 | async-start | bytes 262144 | tf_op jit(solution)/shard_map/all_to_all | solution.py:24
  96.9 26.2 %copy-start.1 = (s32[2]{0:T(128)}, s32[2]{0:T(128)S(1)}, u32[]{:S(2)}) copy-start(s32[2]{0:T(128)S(1)} %pad_add_fusion.pos_ref) | copy-start | bytes 28
  107.2 16.0 %all-to-all-start.3 = ((f32[16,2,1024]{2,1,0:T(2,128)}), f32[16,2,1024]{2,1,0:T(2,128)S(1)}, u32[]{:S(2)}, u32[]{:S(2)}) async-start(f32[16,2,1024]{2,1,0:T(2,128)} %share.1), calls=%async_computation.3 | async-start | bytes 262144 | tf_op jit(solution)/shard_map/all_to_all | solution.py:24
  123.2 0.7 copy-start.4
  149.2 33.0 %all-to-all-start.5 = ((f32[32,64,128]{2,1,0:T(8,128)}), f32[32,64,128]{2,1,0:T(8,128)S(1)}, u32[]{:S(2)}, u32[]{:S(2)}) async-start(f32[32,64,128]{2,1,0:T(8,128)} %spread.1), calls=%async_computation.5 | async-start | bytes 2097152 | tf_op jit(solution)/shard_map/all_to_all | solution.py:24
Sparse Core Ops, SparseCore 0:
  74.7 43.3 all-gather.2

commit v16 on v15

--- a/solution.py
+++ b/solution.py
@@ -210,13 +210,17 @@
     pairs = held.shape[0]
     share, rows = below_ref.shape
 
-    def fetch(y):
-        return pltpu.make_async_copy(coupling_ref.at[y], held.at[y], sems.at[y])
-
-    for y in range(pairs):
-        fetch(y).start()
-    own_low = pltpu.make_async_copy(low_ref, own.at[0], sems.at[pairs])
-    own_high = pltpu.make_async_copy(high_ref, own.at[1], sems.at[pairs + 1])
+    def fetch(y, half):
+        part = pl.ds(half * rows, rows)
+        return pltpu.make_async_copy(
+            coupling_ref.at[y, part], held.at[y, part], sems.at[half * pairs + y]
+        )
+
+    for half in range(2):
+        for y in range(pairs):
+            fetch(y, half).start()
+    own_low = pltpu.make_async_copy(low_ref, own.at[0], sems.at[2 * pairs])
+    own_high = pltpu.make_async_copy(high_ref, own.at[1], sems.at[2 * pairs + 1])
     own_low.start()
     own_high.start()
     vectors[...] = jnp.zeros_like(vectors)
@@ -232,16 +236,18 @@
     above[pairs - 1, :share, :] = above_ref[...]
 
     incoming = into[0]
+    for y in range(pairs - 1):
+        fetch(y, 0).wait()
+        head[y], tail[y] = split(held[y, :rows])
+        taken = dot_parts(two_parts(incoming), head[y], tail[y], 1)
+        incoming = vectors[y, :, :rows] - taken
+        into[y + 1] = incoming
+    fetch(pairs - 1, 0).wait()
+    head[pairs - 1], tail[pairs - 1] = split(held[pairs - 1, :rows])
     for y in range(pairs):
-        fetch(y).wait()
-        block_head, block_tail = split(held[y])
-        head[y] = block_head[:rows]
-        tail[y] = block_tail[:rows]
-        result = vectors[y] - dot_parts(two_parts(incoming), block_head, block_tail, 1)
-        incoming = result[:, :rows]
-        if y + 1 < pairs:
-            into[y + 1] = incoming
-        vectors[y] = result
+        fetch(y, 1).wait()
+        taken = dot_parts(two_parts(into[y]), *split(held[y, rows:]), 0)
+        vectors[y, :, rows:] = vectors[y, :, rows:] - taken
     from_above = above[pairs - 1]
     for y in range(pairs - 1, 0, -1):
         taken = dot_parts(two_parts(from_above), head[y], tail[y], 0)
@@ -289,7 +295,7 @@
             pltpu.VMEM((pairs + 2, padded, 2 * rows), jnp.float32),
             pltpu.VMEM((pairs, padded, rows), jnp.float32),
             pltpu.VMEM((pairs, padded, rows), jnp.float32),
-            pltpu.SemaphoreType.DMA((pairs + 2,)),
+            pltpu.SemaphoreType.DMA((2 * pairs + 2,)),
         ],
         compiler_params=pltpu.CompilerParams(vmem_limit_bytes=(56 * 1024 + 640) * 1024),
         cost_estimate=pl.CostEstimate(

time: 191 us -> 192 us (level)
  no operation moved by 1% of the time
where the time goes in v16:
time: 192 us; the launch traced here: 191 us
  waiting for transfers between devices  60.2 us (31%)
  blocking collectives  52.7 us (27%)
  starting transfers between devices  37.8 us (20%)
  between operations  14.4 us (8%)
  Pallas kernels  13.7 us (7%)
  local copies, waits for them, and re-layouts  7.36 us (4%)
  matrix products  2.66 us (1%)
  other arithmetic  1.97 us (1%)
    all_to_all x2, blocking collectives, exchange(): lax.all_to_all(blocks, axis, 0, 0, tiled=True, axis_index_groups=groups)  52.7 us
    all_to_all x4, waiting for transfers between devices, exchange(): lax.all_to_all(blocks, axis, 0, 0, tiled=True, axis_index_groups=groups)  42.3 us
    all_to_all x4, starting transfers between devices, exchange(): lax.all_to_all(blocks, axis, 0, 0, tiled=True, axis_index_groups=groups)  26.1 us
    ppermute x3, waiting for transfers between devices, turn_along_x(): return lax.ppermute(block, 'front', pairs)  16.1 us
    ppermute x3, starting transfers between devices, turn_along_x(): return lax.ppermute(block, 'front', pairs)  9.82 us
    pallas_call x1, Pallas kernels, run_chain(): pl.pallas_call(chain_kernel, out_shape=jax.ShapeDtypeStruct((targets, sha...  7.56 us
  transfers between devices with their start and end apart: 9, of which 8 were waited for; matrix products, arithmetic and copies ran while one was open for 2% of the time, Pallas kernels for 2%

profile of v16, /device:TPU:2, one launch (start us, length us, event | category | flops | bytes accessed | tf_op | source)
XLA Modules:
  0.0 190.8 jit_solution(555494940782247863)
XLA Ops:
  7.2 1.9 %copy.10 = f32[128,4096]{0,1:T(8,128)S(1)} copy(f32[128,4096]{1,0:T(8,128)} %inverse_ref.3) | data formatting | bytes 4194304 | tf_op args[1]
  10.7 35.7 %all_to_all.30 = f32[32,16,384]{2,1,0:T(8,128)S(1)} all-to-all(f32[32,16,384]{2,1,0:T(8,128)S(1)} %pad_maximum_fusion), channel_id=1, replica_groups=mesh['leaf'=16,'front'=32] {'front'}, dimensions={0} | all-to-all | bytes 1572864 | tf_op jit(solution)/shard_map/all_to_all | solution.py:24
  47.4 5.6 %all-to-all-start.1 = ((f32[32,16,256]{2,1,0:T(8,128)}), f32[32,16,256]{2,1,0:T(8,128)S(1)}, u32[]{:S(2)}, u32[]{:S(2)}) async-start(f32[32,16,256]{2,1,0:T(8,128)} %broadcast_in_dim.18), calls=%async_computation.1 | async-start | bytes 1048576 | tf_op jit(solution)/shard_map/all_to_all | solution.py:24
  53.0 3.4 %collective-permute-start = (f32[32,16,128]{2,1,0:T(8,128)S(1)}, f32[32,16,128]{2,1,0:T(8,128)S(1)}, u32[]{:S(2)}, u32[]{:S(2)}) collective-permute-start(f32[32,16,128]{2,1,0:T(8,128)S(1)} %slice.31.refs_0_), channel_id=1, source_target_pairs={{0,1},{1,2},{2,3},{3,0},{4,5},{5,6},{6,7},{7,4},{8,9},{9,10},{10,1... | collective-permute-start | bytes 786440 | tf_op jit(solution)/shard_map/ppermute | solution.py:42
  56.4 2.5 %collective-permute-start.1 = (f32[32,16,128]{2,1,0:T(8,128)S(1)}, f32[32,16,128]{2,1,0:T(8,128)S(1)}, u32[]{:S(2)}, u32[]{:S(2)}) collective-permute-start(f32[32,16,128]{2,1,0:T(8,128)S(1)} %slice.31.refs_0_), channel_id=1, source_target_pairs={{0,3},{1,0},{2,1},{3,2},{4,7},{5,4},{6,5},{7,6},{8,11},{9,8},{10,9... | collective-permute-start | bytes 786440 | tf_op jit(solution)/shard_map/ppermute | solution.py:42
  58.9 6.2 %collective-permute-done.refs_1_ = f32[32,16,128]{2,1,0:T(8,128)S(1)} collective-permute-done((f32[32,16,128]{2,1,0:T(8,128)S(1)}, f32[32,16,128]{2,1,0:T(8,128)S(1)}, u32[]{:S(2)}, u32[]{:S(2)}) %collective-permute-start) | collective-permute-done | bytes 262176 | tf_op jit(solution)/shard_map/ppermute | solution.py:42
  65.1 3.0 %collective-permute-done.1.refs_3_ = f32[32,16,128]{2,1,0:T(8,128)S(1)} collective-permute-done((f32[32,16,128]{2,1,0:T(8,128)S(1)}, f32[32,16,128]{2,1,0:T(8,128)S(1)}, u32[]{:S(2)}, u32[]{:S(2)}) %collective-permute-start.1) | collective-permute-done | bytes 262176 | tf_op jit(solution)/shard_map/ppermute | solution.py:42
  68.6 1.9 %collective-permute-start.2 = (f32[512,256]{1,0:T(8,128)S(1)}, f32[512,256]{1,0:T(8,128)S(1)}, u32[]{:S(2)}, u32[]{:S(2)}) collective-permute-start(f32[512,256]{1,0:T(8,128)S(1)} %bitcast.15), channel_id=1, source_target_pairs={{0,32},{32,0},{64,96},{96,64},{128,160},{160,128},{192,224},{224,1... | collective-permute-start | bytes 1572872 | tf_op jit(solution)/shard_map/ppermute | solution.py:336
  70.5 1.9 collective-permute-done.2
  73.5 1.1 fusion.2
  74.6 4.0 %collective-permute-start.3 = (f32[32,16,128]{2,1,0:T(8,128)S(1)}, f32[32,16,128]{2,1,0:T(8,128)}, u32[]{:S(2)}, u32[]{:S(2)}) collective-permute-start(f32[32,16,128]{2,1,0:T(8,128)S(1)} %slice.31.refs_0_), channel_id=1, source_target_pairs={{0,2},{1,3},{2,0},{3,1},{4,6},{5,7},{6,4},{7,5},{8,10},{9,11},{10,... | collective-permute-start | bytes 786440 | tf_op jit(solution)/shard_map/ppermute | solution.py:42
  79.6 6.9 %collective-permute-done.3.refs_2_ = f32[32,16,128]{2,1,0:T(8,128)} collective-permute-done((f32[32,16,128]{2,1,0:T(8,128)S(1)}, f32[32,16,128]{2,1,0:T(8,128)}, u32[]{:S(2)}, u32[]{:S(2)}) %collective-permute-start.3) | collective-permute-done | bytes 262176 | tf_op jit(solution)/shard_map/ppermute | solution.py:42
  86.5 2.7 %forward.1 = (f32[64,128]{1,0:T(8,128)S(1)}, f32[32,2,512]{2,1,0:T(2,128)}) custom-call(s32[1]{0:T(128)} %bitcast.10.pos_ref, f32[128,4096]{1,0:T(8,128)S(1)} %copy-done, f32[512,128]{1,0:T(8,128)S(1)} %pad_maximum_fusion.1.stacked_ref, f32[32,16,128]{2,1,0:T(8,128)S(1)} %slice.31.refs_0_, f32[32,16,128]{2,1,0:T(8,128)S(1)} %collective-permute-done.refs_1_, ...), custom_call_target="tpu_custom_call" | custom-call | flops 268435456 | bytes 3145728 | tf_op jit(solution)/shard_map/forward/pallas_call | solution.py:110
  89.2 7.6 %all-to-all-start.2 = ((f32[32,2,512]{2,1,0:T(2,128)}), f32[32,2,512]{2,1,0:T(2,128)S(1)}, u32[]{:S(2)}, u32[]{:S(2)}) async-start(f32[32,2,512]{2,1,0:T(2,128)} %get-tuple-element.14), calls=%async_computation.2 | async-start | bytes 262144 | tf_op jit(solution)/shard_map/all_to_all | solution.py:24
  97.9 7.8 %all-to-all-done.2.arrived_ref = f32[32,2,512]{2,1,0:T(2,128)S(1)} async-done(((f32[32,2,512]{2,1,0:T(2,128)}), f32[32,2,512]{2,1,0:T(2,128)S(1)}, u32[]{:S(2)}, u32[]{:S(2)}) %all-to-all-start.2) | async-done | bytes 131104 | tf_op jit(solution)/shard_map/all_to_all | solution.py:24
  105.7 1.5 share.1
  107.2 7.2 %all-to-all-start.3 = ((f32[16,2,1024]{2,1,0:T(2,128)}), f32[16,2,1024]{2,1,0:T(2,128)S(1)}, u32[]{:S(2)}, u32[]{:S(2)}) async-start(f32[16,2,1024]{2,1,0:T(2,128)} %share.1), calls=%async_computation.3 | async-start | bytes 262144 | tf_op jit(solution)/shard_map/all_to_all | solution.py:24
  114.4 1.3 constant_dynamic-slice_fusion.1
  115.7 7.4 %all-to-all-done.3.share_ref = f32[16,2,1024]{2,1,0:T(2,128)S(1)} async-done(((f32[16,2,1024]{2,1,0:T(2,128)}), f32[16,2,1024]{2,1,0:T(2,128)S(1)}, u32[]{:S(2)}, u32[]{:S(2)}) %all-to-all-start.3) | async-done | bytes 131104 | tf_op jit(solution)/shard_map/all_to_all | solution.py:24
  123.8 7.6 %chain.1 = f32[32,2,768]{2,1,0:T(2,128)} custom-call(s32[2]{0:T(128)} %copy-done.1, f32[8,512,256]{2,1,0:T(8,128)} %bitcast.14, f32[16,2,1024]{2,1,0:T(2,128)} %copy-done.4, f32[512,256]{1,0:T(8,128)} %copy-done.2, f32[512,256]{1,0:T(8,128)} %copy-done.3, f32[2,256]{1,0:T(2,128)} %get-tuple-element.21.below_ref, f32[2,256]{1,0:T(2,128)} %get-tuple-element.20.above_ref), custom_call_target="tpu_custom_call" | custom-call | flops 100663296 | bytes 4194304 | tf_op jit(solution)/shard_map/chain/pallas_call | solution.py:285
  131.4 16.9 %all_to_all.31.result_ref = f32[32,2,768]{2,1,0:T(2,128)S(1)} all-to-all(f32[32,2,768]{2,1,0:T(2,128)} %chain.1), channel_id=1, replica_groups=mesh['leaf'=16,'front'=32] {'front'}, dimensions={0} | all-to-all | bytes 393216 | tf_op jit(solution)/shard_map/all_to_all | solution.py:24
  148.3 1.9 %spread.1 = f32[32,64,128]{2,1,0:T(8,128)} custom-call(f32[32,2,768]{2,1,0:T(2,128)S(1)} %all_to_all.31.result_ref, f32[64,128]{1,0:T(8,128)S(1)} %get-tuple-element.15.forward_ref, f32[512,128]{1,0:T(8,128)S(1)} %pad_maximum_fusion.1.stacked_ref, f32[128,4096]{1,0:T(8,128)S(1)} %copy-done), custom_call_target="tpu_custom_call" | custom-call | flops 268435456 | bytes 3145728 | tf_op jit(solution)/shard_map/spread/pallas_call | solution.py:150
  150.2 5.6 %all-to-all-start.5 = ((f32[32,64,128]{2,1,0:T(8,128)}), f32[32,64,128]{2,1,0:T(8,128)S(1)}, u32[]{:S(2)}, u32[]{:S(2)}) async-start(f32[32,64,128]{2,1,0:T(8,128)} %spread.1), calls=%async_computation.5 | async-start | bytes 2097152 | tf_op jit(solution)/shard_map/all_to_all | solution.py:24
  156.7 26.5 %all-to-all-done.5 = f32[32,64,128]{2,1,0:T(8,128)S(1)} async-done(((f32[32,64,128]{2,1,0:T(8,128)}), f32[32,64,128]{2,1,0:T(8,128)S(1)}, u32[]{:S(2)}, u32[]{:S(2)}) %all-to-all-start.5) | async-done | bytes 1048608 | tf_op jit(solution)/shard_map/all_to_all | solution.py:24
  (42 shorter events, 8.2 us)
Async XLA Ops:
  7.2 2.0 %copy-start.7 = (s32[1,256]{1,0:T(1,128)S(1)}, s32[1,256]{1,0:T(1,128)}, u32[]{:S(2)}) copy-start(s32[1,256]{1,0:T(1,128)} %param.9) | copy-start | bytes 3076
  7.2 2.9 %copy-start.5 = (f32[256,128]{1,0:T(8,128)S(1)}, f32[256,128]{1,0:T(8,128)}, u32[]{:S(2)}) copy-start(f32[256,128]{1,0:T(8,128)} %param.8) | copy-start | bytes 393220
  9.2 1.5 copy-start.6
  47.4 21.2 %all-to-all-start.1 = ((f32[32,16,256]{2,1,0:T(8,128)}), f32[32,16,256]{2,1,0:T(8,128)S(1)}, u32[]{:S(2)}, u32[]{:S(2)}) async-start(f32[32,16,256]{2,1,0:T(8,128)} %broadcast_in_dim.18), calls=%async_computation.1 | async-start | bytes 1048576 | tf_op jit(solution)/shard_map/all_to_all | solution.py:24
  52.9 70.2 %all-gather.3.cloned.1.call-start = ((), (), s32[]{:S(2)}) async-start(), calls=%async_computation.6 | async-start | bytes 4456448 | tf_op jit(solution)/shard_map/all_gather | solution.py:36
  53.0 12.1 %collective-permute-start = (f32[32,16,128]{2,1,0:T(8,128)S(1)}, f32[32,16,128]{2,1,0:T(8,128)S(1)}, u32[]{:S(2)}, u32[]{:S(2)}) collective-permute-start(f32[32,16,128]{2,1,0:T(8,128)S(1)} %slice.31.refs_0_), channel_id=1, source_target_pairs={{0,1},{1,2},{2,3},{3,0},{4,5},{5,6},{6,7},{7,4},{8,9},{9,10},{10,1... | collective-permute-start | bytes 786440 | tf_op jit(solution)/shard_map/ppermute | solution.py:42
  56.4 11.7 %collective-permute-start.1 = (f32[32,16,128]{2,1,0:T(8,128)S(1)}, f32[32,16,128]{2,1,0:T(8,128)S(1)}, u32[]{:S(2)}, u32[]{:S(2)}) collective-permute-start(f32[32,16,128]{2,1,0:T(8,128)S(1)} %slice.31.refs_0_), channel_id=1, source_target_pairs={{0,3},{1,0},{2,1},{3,2},{4,7},{5,4},{6,5},{7,6},{8,11},{9,8},{10,9... | collective-permute-start | bytes 786440 | tf_op jit(solution)/shard_map/ppermute | solution.py:42
  68.6 3.8 %collective-permute-start.2 = (f32[512,256]{1,0:T(8,128)S(1)}, f32[512,256]{1,0:T(8,128)S(1)}, u32[]{:S(2)}, u32[]{:S(2)}) collective-permute-start(f32[512,256]{1,0:T(8,128)S(1)} %bitcast.15), channel_id=1, source_target_pairs={{0,32},{32,0},{64,96},{96,64},{128,160},{160,128},{192,224},{224,1... | collective-permute-start | bytes 1572872 | tf_op jit(solution)/shard_map/ppermute | solution.py:336
  72.5 1.0 copy-start.2
  72.5 1.0 copy-start.3
  72.5 14.0 %copy-start = (f32[128,4096]{1,0:T(8,128)S(1)}, f32[128,4096]{1,0:T(8,128)}, u32[]{:S(2)}) copy-start(f32[128,4096]{1,0:T(8,128)} %inverse_ref.3) | copy-start | bytes 6291460
  74.6 11.9 %collective-permute-start.3 = (f32[32,16,128]{2,1,0:T(8,128)S(1)}, f32[32,16,128]{2,1,0:T(8,128)}, u32[]{:S(2)}, u32[]{:S(2)}) collective-permute-start(f32[32,16,128]{2,1,0:T(8,128)S(1)} %slice.31.refs_0_), channel_id=1, source_target_pairs={{0,2},{1,3},{2,0},{3,1},{4,6},{5,7},{6,4},{7,5},{8,10},{9,11},{10,... | collective-permute-start | bytes 786440 | tf_op jit(solution)/shard_map/ppermute | solution.py:42
  89.2 16.5 %all-to-all-start.2 = ((f32[32,2,512]{2,1,0:T(2,128)}), f32[32,2,512]{2,1,0:T(2,128)S(1)}, u32[]{:S(2)}, u32[]{:S(2)}) async-start(f32[32,2,512]{2,1,0:T(2,128)} %get-tuple-element.14), calls=%async_computation.2 | async-start | bytes 262144 | tf_op jit(solution)/shard_map/all_to_all | solution.py:24
  96.9 26.2 %copy-start.1 = (s32[2]{0:T(128)}, s32[2]{0:T(128)S(1)}, u32[]{:S(2)}) copy-start(s32[2]{0:T(128)S(1)} %pad_add_fusion.pos_ref) | copy-start | bytes 28
  107.2 16.0 %all-to-all-start.3 = ((f32[16,2,1024]{2,1,0:T(2,128)}), f32[16,2,1024]{2,1,0:T(2,128)S(1)}, u32[]{:S(2)}, u32[]{:S(2)}) async-start(f32[16,2,1024]{2,1,0:T(2,128)} %share.1), calls=%async_computation.3 | async-start | bytes 262144 | tf_op jit(solution)/shard_map/all_to_all | solution.py:24
  123.2 0.7 copy-start.4
  150.2 33.0 %all-to-all-start.5 = ((f32[32,64,128]{2,1,0:T(8,128)}), f32[32,64,128]{2,1,0:T(8,128)S(1)}, u32[]{:S(2)}, u32[]{:S(2)}) async-start(f32[32,64,128]{2,1,0:T(8,128)} %spread.1), calls=%async_computation.5 | async-start | bytes 2097152 | tf_op jit(solution)/shard_map/all_to_all | solution.py:24
Sparse Core Ops, SparseCore 0:
  74.7 43.3 all-gather.2

commit v17 on v13

--- a/solution.py
+++ b/solution.py
@@ -324,8 +324,9 @@
     coupling = jnp.sum(arrived[:, :, :rows], axis=0)
     side_chunk = arrived[:, :, rows:]
     coupling = gather_front(coupling).reshape(2 * rows, rows)
-    turned = [turn_along_x(side_chunk, steps) for steps in range(1, x_chips)]
-    coupling, *turned = lax.optimization_barrier((coupling, *turned))
+    turned = [turn_along_x(side_chunk, steps) for steps in (1, x_chips - 1)]
+    coupling, side_chunk, *turned = lax.optimization_barrier((coupling, side_chunk, *turned))
+    far = turn_along_x(side_chunk, 2)
 
     swap = [(s, s ^ 1) for s in range(leaf_count)]
     mate = lax.ppermute(coupling, "leaf", swap)
@@ -336,6 +337,7 @@
     c_pair = -product(c_high, c_low)
     g_pair = low[rows:] + product(c_low.T, lifted)
     pair_half = jnp.where(is_upper, g_pair, c_pair)
+    turned.insert(1, far)
     coupling_all = gather_leaf(pair_half).reshape(leaf_count // 2, 2 * rows, rows)
 
     local_forward, vectors = run_forward(

time: 198 us -> 193 us (0.975)
  waiting for transfers between devices: 63.2 us -> 58.3 us
    all_gather x1, waiting for transfers between devices: 6.97 us -> 0.01 us  [gather_leaf(): return lax.all_gather(block, 'leaf', axis=0)]
    ppermute x3, waiting for transfers between devices: 11.2 us -> 15.1 us  [turn_along_x(): return lax.ppermute(block, 'front', pairs)]
    unnamed x26 -> x22, local copies, waits for them, and re-layouts: 5.25 us -> 4.25 us
  transfers between devices with their start and end apart: 9 -> 9, of which waited for: 8 -> 7; matrix products, arithmetic and copies ran while one was open for 2% -> 3% of each run, Pallas kernels for 2% -> 2%
where the time goes in v17:
time: 193 us; the launch traced here: 192 us
  waiting for transfers between devices  58.3 us (30%)
  blocking collectives  56.5 us (29%)
  starting transfers between devices  37.8 us (20%)
  between operations  14.4 us (7%)
  Pallas kernels  12.6 us (7%)
  local copies, waits for them, and re-layouts  8.31 us (4%)
  matrix products  2.65 us (1%)
    all_to_all x2, blocking collectives, exchange(): lax.all_to_all(blocks, axis, 0, 0, tiled=True, axis_index_groups=groups)  56.5 us
    all_to_all x4, waiting for transfers between devices, exchange(): lax.all_to_all(blocks, axis, 0, 0, tiled=True, axis_index_groups=groups)  43.2 us
    all_to_all x4, starting transfers between devices, exchange(): lax.all_to_all(blocks, axis, 0, 0, tiled=True, axis_index_groups=groups)  26.1 us
    ppermute x3, waiting for transfers between devices, turn_along_x(): return lax.ppermute(block, 'front', pairs)  15.1 us
    ppermute x3, starting transfers between devices, turn_along_x(): return lax.ppermute(block, 'front', pairs)  9.82 us
    pallas_call x1, Pallas kernels, run_chain(): pl.pallas_call(chain_kernel, out_shape=jax.ShapeDtypeStruct((targets, sha...  6.48 us
    unnamed x22, local copies, waits for them, and re-layouts  4.25 us
  transfers between devices with their start and end apart: 9, of which 7 were waited for; matrix products, arithmetic and copies ran while one was open for 3% of the time, Pallas kernels for 2%

profile of v17, /device:TPU:2, one launch (start us, length us, event | category | flops | bytes accessed | tf_op | source)
XLA Modules:
  0.0 191.7 jit_solution(12274152098823362680)
XLA Ops:
  7.2 1.9 %copy.10 = f32[128,4096]{0,1:T(8,128)S(1)} copy(f32[128,4096]{1,0:T(8,128)} %inverse_ref.3) | data formatting | bytes 4194304 | tf_op args[1]
  10.7 35.7 %all_to_all.30 = f32[32,16,384]{2,1,0:T(8,128)S(1)} all-to-all(f32[32,16,384]{2,1,0:T(8,128)S(1)} %pad_maximum_fusion), channel_id=1, replica_groups=mesh['leaf'=16,'front'=32] {'front'}, dimensions={0} | all-to-all | bytes 1572864 | tf_op jit(solution)/shard_map/all_to_all | solution.py:25
  47.4 5.6 %all-to-all-start.1 = ((f32[32,16,256]{2,1,0:T(8,128)}), f32[32,16,256]{2,1,0:T(8,128)S(1)}, u32[]{:S(2)}, u32[]{:S(2)}) async-start(f32[32,16,256]{2,1,0:T(8,128)} %broadcast_in_dim.18), calls=%async_computation.1 | async-start | bytes 1048576 | tf_op jit(solution)/shard_map/all_to_all | solution.py:25
  53.0 3.4 %collective-permute-start = (f32[32,16,128]{2,1,0:T(8,128)S(1)}, f32[32,16,128]{2,1,0:T(8,128)S(1)}, u32[]{:S(2)}, u32[]{:S(2)}) collective-permute-start(f32[32,16,128]{2,1,0:T(8,128)S(1)} %slice.31.refs_0_), channel_id=1, source_target_pairs={{0,1},{1,2},{2,3},{3,0},{4,5},{5,6},{6,7},{7,4},{8,9},{9,10},{10,1... | collective-permute-start | bytes 786440 | tf_op jit(solution)/shard_map/ppermute | solution.py:43
  56.4 2.5 %collective-permute-start.1 = (f32[32,16,128]{2,1,0:T(8,128)S(1)}, f32[32,16,128]{2,1,0:T(8,128)S(1)}, u32[]{:S(2)}, u32[]{:S(2)}) collective-permute-start(f32[32,16,128]{2,1,0:T(8,128)S(1)} %slice.31.refs_0_), channel_id=1, source_target_pairs={{0,3},{1,0},{2,1},{3,2},{4,7},{5,4},{6,5},{7,6},{8,11},{9,8},{10,9... | collective-permute-start | bytes 786440 | tf_op jit(solution)/shard_map/ppermute | solution.py:43
  58.9 6.2 %collective-permute-done.refs_1_ = f32[32,16,128]{2,1,0:T(8,128)S(1)} collective-permute-done((f32[32,16,128]{2,1,0:T(8,128)S(1)}, f32[32,16,128]{2,1,0:T(8,128)S(1)}, u32[]{:S(2)}, u32[]{:S(2)}) %collective-permute-start) | collective-permute-done | bytes 262176 | tf_op jit(solution)/shard_map/ppermute | solution.py:43
  65.1 3.0 %collective-permute-done.1.refs_3_ = f32[32,16,128]{2,1,0:T(8,128)S(1)} collective-permute-done((f32[32,16,128]{2,1,0:T(8,128)S(1)}, f32[32,16,128]{2,1,0:T(8,128)S(1)}, u32[]{:S(2)}, u32[]{:S(2)}) %collective-permute-start.1) | collective-permute-done | bytes 262176 | tf_op jit(solution)/shard_map/ppermute | solution.py:43
  68.6 1.9 collective-permute-start.2
  70.6 4.0 %collective-permute-start.3 = (f32[32,16,128]{2,1,0:T(8,128)S(1)}, f32[32,16,128]{2,1,0:T(8,128)}, u32[]{:S(2)}, u32[]{:S(2)}) collective-permute-start(f32[32,16,128]{2,1,0:T(8,128)S(1)} %slice.31.refs_0_), channel_id=1, source_target_pairs={{0,2},{1,3},{2,0},{3,1},{4,6},{5,7},{6,4},{7,5},{8,10},{9,11},{10,... | collective-permute-start | bytes 786440 | tf_op jit(solution)/shard_map/ppermute | solution.py:43
  75.7 1.1 fusion.2
  76.8 6.0 %collective-permute-done.3.refs_2_ = f32[32,16,128]{2,1,0:T(8,128)} collective-permute-done((f32[32,16,128]{2,1,0:T(8,128)S(1)}, f32[32,16,128]{2,1,0:T(8,128)}, u32[]{:S(2)}, u32[]{:S(2)}) %collective-permute-start.3) | collective-permute-done | bytes 262176 | tf_op jit(solution)/shard_map/ppermute | solution.py:43
  83.7 2.7 %forward.1 = (f32[64,128]{1,0:T(8,128)S(1)}, f32[32,2,512]{2,1,0:T(2,128)}) custom-call(s32[1]{0:T(128)} %bitcast.10.pos_ref, f32[128,4096]{1,0:T(8,128)S(1)} %copy-done, f32[512,128]{1,0:T(8,128)S(1)} %pad_maximum_fusion.1.stacked_ref, f32[32,16,128]{2,1,0:T(8,128)S(1)} %slice.31.refs_0_, f32[32,16,128]{2,1,0:T(8,128)S(1)} %collective-permute-done.refs_1_, ...), custom_call_target="tpu_custom_call" | custom-call | flops 268435456000 | bytes 3145728 | tf_op jit(solution)/shard_map/forward/pallas_call | solution.py:111
  86.4 7.6 %all-to-all-start.2 = ((f32[32,2,512]{2,1,0:T(2,128)}), f32[32,2,512]{2,1,0:T(2,128)S(1)}, u32[]{:S(2)}, u32[]{:S(2)}) async-start(f32[32,2,512]{2,1,0:T(2,128)} %get-tuple-element.12), calls=%async_computation.2 | async-start | bytes 262144 | tf_op jit(solution)/shard_map/all_to_all | solution.py:25
  94.2 1.0 slice.35.high_ref
  95.1 7.8 %all-to-all-done.2.arrived_ref = f32[32,2,512]{2,1,0:T(2,128)S(1)} async-done(((f32[32,2,512]{2,1,0:T(2,128)}), f32[32,2,512]{2,1,0:T(2,128)S(1)}, u32[]{:S(2)}, u32[]{:S(2)}) %all-to-all-start.2) | async-done | bytes 131104 | tf_op jit(solution)/shard_map/all_to_all | solution.py:25
  102.9 1.5 share.1
  104.4 7.2 %all-to-all-start.3 = ((f32[16,2,1024]{2,1,0:T(2,128)}), f32[16,2,1024]{2,1,0:T(2,128)S(1)}, u32[]{:S(2)}, u32[]{:S(2)}) async-start(f32[16,2,1024]{2,1,0:T(2,128)} %share.1), calls=%async_computation.3 | async-start | bytes 262144 | tf_op jit(solution)/shard_map/all_to_all | solution.py:25
  111.7 1.3 constant_dynamic-slice_fusion.1
  113.0 8.4 %all-to-all-done.3.share_ref = f32[16,2,1024]{2,1,0:T(2,128)S(1)} async-done(((f32[16,2,1024]{2,1,0:T(2,128)}), f32[16,2,1024]{2,1,0:T(2,128)S(1)}, u32[]{:S(2)}, u32[]{:S(2)}) %all-to-all-start.3) | async-done | bytes 131104 | tf_op jit(solution)/shard_map/all_to_all | solution.py:25
  122.0 6.5 %chain.1 = f32[32,2,768]{2,1,0:T(2,128)} custom-call(s32[2]{0:T(128)} %copy-done.1, f32[8,512,256]{2,1,0:T(8,128)} %bitcast.14, f32[16,2,1024]{2,1,0:T(2,128)} %copy-done.6, f32[512,256]{1,0:T(8,128)} %copy-done.4, f32[512,256]{1,0:T(8,128)} %copy-done.5, f32[2,256]{1,0:T(2,128)} %get-tuple-element.19.below_ref, f32[2,256]{1,0:T(2,128)} %get-tuple-element.18.above_ref), custom_call_target="tpu_custom_call" | custom-call | flops 100663296 | bytes 4194304 | tf_op jit(solution)/shard_map/chain/pallas_call | solution.py:280
  128.5 20.8 %all_to_all.31.result_ref = f32[32,2,768]{2,1,0:T(2,128)S(1)} all-to-all(f32[32,2,768]{2,1,0:T(2,128)} %chain.1), channel_id=1, replica_groups=mesh['leaf'=16,'front'=32] {'front'}, dimensions={0} | all-to-all | bytes 393216 | tf_op jit(solution)/shard_map/all_to_all | solution.py:25
  149.3 1.9 %spread.1 = f32[32,64,128]{2,1,0:T(8,128)} custom-call(f32[32,2,768]{2,1,0:T(2,128)S(1)} %all_to_all.31.result_ref, f32[64,128]{1,0:T(8,128)S(1)} %get-tuple-element.13.forward_ref, f32[512,128]{1,0:T(8,128)S(1)} %pad_maximum_fusion.1.stacked_ref, f32[128,4096]{1,0:T(8,128)S(1)} %copy-done), custom_call_target="tpu_custom_call" | custom-call | flops 268435456 | bytes 3145728 | tf_op jit(solution)/shard_map/spread/pallas_call | solution.py:151
  151.2 5.6 %all-to-all-start.5 = ((f32[32,64,128]{2,1,0:T(8,128)}), f32[32,64,128]{2,1,0:T(8,128)S(1)}, u32[]{:S(2)}, u32[]{:S(2)}) async-start(f32[32,64,128]{2,1,0:T(8,128)} %spread.1), calls=%async_computation.5 | async-start | bytes 2097152 | tf_op jit(solution)/shard_map/all_to_all | solution.py:25
  157.7 26.5 %all-to-all-done.5 = f32[32,64,128]{2,1,0:T(8,128)S(1)} async-done(((f32[32,64,128]{2,1,0:T(8,128)}), f32[32,64,128]{2,1,0:T(8,128)S(1)}, u32[]{:S(2)}, u32[]{:S(2)}) %all-to-all-start.5) | async-done | bytes 1048608 | tf_op jit(solution)/shard_map/all_to_all | solution.py:25
  (46 shorter events, 7.3 us)
Async XLA Ops:
  7.2 2.0 %copy-start.9 = (s32[1,256]{1,0:T(1,128)S(1)}, s32[1,256]{1,0:T(1,128)}, u32[]{:S(2)}) copy-start(s32[1,256]{1,0:T(1,128)} %param.9) | copy-start | bytes 3076
  7.2 2.9 %copy-start.7 = (f32[256,128]{1,0:T(8,128)S(1)}, f32[256,128]{1,0:T(8,128)}, u32[]{:S(2)}) copy-start(f32[256,128]{1,0:T(8,128)} %param.8) | copy-start | bytes 393220
  9.1 1.5 copy-start.8
  47.4 21.2 %all-to-all-start.1 = ((f32[32,16,256]{2,1,0:T(8,128)}), f32[32,16,256]{2,1,0:T(8,128)S(1)}, u32[]{:S(2)}, u32[]{:S(2)}) async-start(f32[32,16,256]{2,1,0:T(8,128)} %broadcast_in_dim.18), calls=%async_computation.1 | async-start | bytes 1048576 | tf_op jit(solution)/shard_map/all_to_all | solution.py:25
  52.9 68.4 %all-gather.3.cloned.1.call-start = ((), (), s32[]{:S(2)}) async-start(), calls=%async_computation.6 | async-start | bytes 4456448 | tf_op jit(solution)/shard_map/all_gather | solution.py:37
  53.0 12.1 %collective-permute-start = (f32[32,16,128]{2,1,0:T(8,128)S(1)}, f32[32,16,128]{2,1,0:T(8,128)S(1)}, u32[]{:S(2)}, u32[]{:S(2)}) collective-permute-start(f32[32,16,128]{2,1,0:T(8,128)S(1)} %slice.31.refs_0_), channel_id=1, source_target_pairs={{0,1},{1,2},{2,3},{3,0},{4,5},{5,6},{6,7},{7,4},{8,9},{9,10},{10,1... | collective-permute-start | bytes 786440 | tf_op jit(solution)/shard_map/ppermute | solution.py:43
  56.4 11.7 %collective-permute-start.1 = (f32[32,16,128]{2,1,0:T(8,128)S(1)}, f32[32,16,128]{2,1,0:T(8,128)S(1)}, u32[]{:S(2)}, u32[]{:S(2)}) collective-permute-start(f32[32,16,128]{2,1,0:T(8,128)S(1)} %slice.31.refs_0_), channel_id=1, source_target_pairs={{0,3},{1,0},{2,1},{3,2},{4,7},{5,4},{6,5},{7,6},{8,11},{9,8},{10,9... | collective-permute-start | bytes 786440 | tf_op jit(solution)/shard_map/ppermute | solution.py:43
  68.0 6.6 %copy-start.2 = (f32[32,16,128]{2,1,0:T(8,128)}, f32[32,16,128]{2,1,0:T(8,128)S(1)}, u32[]{:S(2)}) copy-start(f32[32,16,128]{2,1,0:T(8,128)S(1)} %collective-permute-done.1.refs_3_) | copy-start | bytes 786436
  68.6 6.0 %collective-permute-start.2 = (f32[512,256]{1,0:T(8,128)S(1)}, f32[512,256]{1,0:T(8,128)S(1)}, u32[]{:S(2)}, u32[]{:S(2)}) collective-permute-start(f32[512,256]{1,0:T(8,128)S(1)} %bitcast.15), channel_id=1, source_target_pairs={{0,32},{32,0},{64,96},{96,64},{128,160},{160,128},{192,224},{224,1... | collective-permute-start | bytes 1572872 | tf_op jit(solution)/shard_map/ppermute | solution.py:332
  70.6 12.2 %collective-permute-start.3 = (f32[32,16,128]{2,1,0:T(8,128)S(1)}, f32[32,16,128]{2,1,0:T(8,128)}, u32[]{:S(2)}, u32[]{:S(2)}) collective-permute-start(f32[32,16,128]{2,1,0:T(8,128)S(1)} %slice.31.refs_0_), channel_id=1, source_target_pairs={{0,2},{1,3},{2,0},{3,1},{4,6},{5,7},{6,4},{7,5},{8,10},{9,11},{10,... | collective-permute-start | bytes 786440 | tf_op jit(solution)/shard_map/ppermute | solution.py:43
  74.6 1.0 copy-start.4
  74.6 1.0 copy-start.5
  74.6 8.1 %copy-start = (f32[128,4096]{1,0:T(8,128)S(1)}, f32[128,4096]{1,0:T(8,128)}, u32[]{:S(2)}) copy-start(f32[128,4096]{1,0:T(8,128)} %inverse_ref.3) | copy-start | bytes 6291460
  82.8 1.0 copy-start.3
  86.4 16.5 %all-to-all-start.2 = ((f32[32,2,512]{2,1,0:T(2,128)}), f32[32,2,512]{2,1,0:T(2,128)S(1)}, u32[]{:S(2)}, u32[]{:S(2)}) async-start(f32[32,2,512]{2,1,0:T(2,128)} %get-tuple-element.12), calls=%async_computation.2 | async-start | bytes 262144 | tf_op jit(solution)/shard_map/all_to_all | solution.py:25
  94.2 27.2 %copy-start.1 = (s32[2]{0:T(128)}, s32[2]{0:T(128)S(1)}, u32[]{:S(2)}) copy-start(s32[2]{0:T(128)S(1)} %pad_add_fusion.pos_ref) | copy-start | bytes 28
  104.4 16.9 %all-to-all-start.3 = ((f32[16,2,1024]{2,1,0:T(2,128)}), f32[16,2,1024]{2,1,0:T(2,128)S(1)}, u32[]{:S(2)}, u32[]{:S(2)}) async-start(f32[16,2,1024]{2,1,0:T(2,128)} %share.1), calls=%async_computation.3 | async-start | bytes 262144 | tf_op jit(solution)/shard_map/all_to_all | solution.py:25
  121.3 0.7 copy-start.6
  151.2 33.0 %all-to-all-start.5 = ((f32[32,64,128]{2,1,0:T(8,128)}), f32[32,64,128]{2,1,0:T(8,128)S(1)}, u32[]{:S(2)}, u32[]{:S(2)}) async-start(f32[32,64,128]{2,1,0:T(8,128)} %spread.1), calls=%async_computation.5 | async-start | bytes 2097152 | tf_op jit(solution)/shard_map/all_to_all | solution.py:25
Sparse Core Ops, SparseCore 0:
  76.9 44.0 all-gather.2
